TPU v7x, 128 devices: a whole 4x4x4 slice. The times are simulated.
128 devices in a mesh: sess: 16 (over y_hi, x, core), exp: 8 (over y_lo, z).
Axes of the slice: x: 4, y: 4 (y_hi: 2, y_lo: 2; y = y_hi * 2 + y_lo), z: 4, core: 2. Of those that a mesh axis runs over, the one named last changes fastest.
Arguments:
- residual: bfloat16 [8192, 4096], P(('sess', 'exp')), may hold values from -6 to 6
- mamba_input: bfloat16 [8192, 8192], P('sess', 'exp'), may hold values from -6 to 6
- mamba_gate: bfloat16 [8192, 8192], P('sess', 'exp'), may hold values from -6 to 6
- filter_taps: float32 [4, 8192], P(None, 'exp'), may hold values from -3 to 3
- filter_bias: float32 [8192], P('exp'), may hold values from -3 to 3
- input_select: bfloat16 [8192, 288], P('exp'), may hold values from -0.0625 to 0.0625
- step_weight: bfloat16 [256, 8192], P(None, 'exp'), may hold values from -0.375 to 0.375
- step_bias: float32 [8192], P('exp'), may hold values from -6.9 to -2.25
- decay_log: float32 [16, 8192], P(None, 'exp'), may hold values from 0 to 2.77
- skip_scale: float32 [8192], P('exp'), may hold values from 0.5 to 1.5
- output_weight: bfloat16 [8192, 4096], P('exp'), may hold values from -0.0625 to 0.0625
- query_weight: bfloat16 [4096, 4096], P(None, 'exp'), may hold values from -1 to 1
- key_matrix: bfloat16 [4096, 1024], P(None, 'exp'), may hold values from -0.09375 to 0.09375
- value_matrix: bfloat16 [4096, 1024], P(None, 'exp'), may hold values from -0.09375 to 0.09375
- head_weight: bfloat16 [4096, 4096], P('exp'), may hold values from -0.09375 to 0.09375
- cache_keys: bfloat16 [32, 256, 1024], P('sess', None, 'exp'), may hold values from -6 to 6
- stored_cache_values: bfloat16 [32, 256, 1024], P('sess', None, 'exp'), may hold values from -6 to 6
- cache_state: float32 [32, 16, 8192], P('sess', None, 'exp'), may hold values from -6 to 6
- cache_filter: bfloat16 [32, 3, 8192], P('sess', None, 'exp'), may hold values from -6 to 6
- prompt_slot: int32 [32], replicated, may hold values from 0 to 31, each once
- session_prompt: int32 [64], replicated, may hold values from 0 to 31
Outputs:
- layer_out: bfloat16 [8192, 4096], P(('sess', 'exp'))
Inputs may be any that keep to these rules, and one draw needn't show every extreme that they name: `prompt_slot`: each prompt has its own row of the cache arrays. `session_prompt`: several sessions may resume from one prompt.
All inputs are finite; a program needn't handle non-finite values.
Results may differ from a plain program's by a relative error of at most 0.035.
Values may be sent and summed in bfloat16 or wider, within the bound.
No kernel may reach another device: no remote copies, remote signals or barrier semaphores. Data moves between devices by JAX's collectives and lax.ppermute only.
A program may use at most 128 MiB of HBM per device.

v0:
```python
import math

import jax
import jax.numpy as jnp
from jax import lax
from jax.sharding import PartitionSpec as P

HEAD_SIZE = 128
NEW = 128


EPSILON = 1e-06


def selective_scan(step_size, signal, input_mix, readout, start_state, decay_rate, unroll_by):
    sessions = start_state.shape[0]
    frames = step_size.shape[0] // sessions

    def frame_major(tensor):
        return jnp.swapaxes(tensor.reshape(sessions, frames, tensor.shape[-1]), 0, 1)

    def advance(carried, inputs):
        frame_size, frame_signal, frame_input, frame_readout = inputs
        carried = (
            jnp.exp(frame_size[:, None, :] * decay_rate[None]) * carried
            + (frame_size * frame_signal)[:, None, :] * frame_input[:, :, None]
        )
        return (carried, jnp.sum(frame_readout[:, :, None] * carried, axis=1))

    last_state, emitted = lax.scan(
        advance,
        start_state,
        (frame_major(step_size), frame_major(signal), frame_major(input_mix), frame_major(readout)),
        unroll=unroll_by,
    )
    return jnp.swapaxes(emitted, 0, 1).reshape(sessions * frames, -1)


def normalize(hidden):
    return (hidden * lax.rsqrt(jnp.mean(hidden * hidden, axis=-1, keepdims=True) + EPSILON)).astype(
        jnp.bfloat16
    )


def attend_group(queries, new_keys, new_values, old_keys, old_values, group_sessions):
    key_heads = new_keys.shape[1] // HEAD_SIZE
    sharing = queries.shape[1] // new_keys.shape[1]
    cached = old_keys.shape[1]
    keys_all = jnp.concatenate(
        [old_keys, new_keys.reshape(group_sessions, NEW, -1)], axis=1
    ).reshape(group_sessions, cached + NEW, key_heads, HEAD_SIZE)
    values_all = jnp.concatenate(
        [old_values, new_values.reshape(group_sessions, NEW, -1)], axis=1
    ).reshape(group_sessions, cached + NEW, key_heads, HEAD_SIZE)
    query_grid = queries.reshape(group_sessions, NEW, key_heads, sharing, HEAD_SIZE)
    scores = jnp.einsum(
        "sqhgd,skhd->shgqk", query_grid, keys_all, preferred_element_type=jnp.float32
    ) / math.sqrt(HEAD_SIZE)
    visible = jnp.arange(cached + NEW)[None, :] <= cached + jnp.arange(NEW)[:, None]
    scores = jnp.where(visible, scores, -1e30)
    top_score = jnp.max(scores, axis=-1, keepdims=True)
    lifted = jnp.exp(scores - top_score)
    weights = (lifted / jnp.sum(lifted, axis=-1, keepdims=True)).astype(jnp.bfloat16)
    attended = jnp.einsum(
        "shgqk,skhd->sqhgd", weights, values_all, preferred_element_type=jnp.float32
    )
    return attended.astype(jnp.bfloat16).reshape(group_sessions * NEW, -1)


def shards(
    residual,
    mamba_input,
    mamba_gate,
    filter_taps,
    filter_bias,
    input_select,
    step_weight,
    step_bias,
    decay_log,
    skip_scale,
    output_weight,
    query_weight,
    key_matrix,
    value_matrix,
    head_weight,
    cache_keys,
    stored_cache_values,
    cache_state,
    cache_filter,
    prompt_slot,
    session_prompt,
):
    group_sessions = mamba_input.shape[0] // NEW
    held_rows = cache_state.shape[0]
    channels = mamba_input.shape[1]
    first_session = lax.axis_index("sess") * group_sessions
    own_prompts = lax.dynamic_slice_in_dim(session_prompt, first_session, group_sessions)
    wanted = prompt_slot[own_prompts]
    state_start = (
        jnp.zeros((group_sessions,) + cache_state.shape[1:], jnp.float32),
        jnp.zeros((group_sessions,) + cache_filter.shape[1:], jnp.float32),
    )
    state_piece = lax.all_gather(
        cache_state.astype(jnp.bfloat16), "sess", axis=0, tiled=True
    ).astype(jnp.float32)
    filter_piece = lax.all_gather(
        cache_filter.astype(jnp.float32).astype(jnp.bfloat16), "sess", axis=0, tiled=True
    ).astype(jnp.float32)
    chooser = (
        wanted[:, None] == jnp.arange(state_piece.shape[0], dtype=jnp.int32)[None, :]
    ).astype(jnp.float32)
    start_state = state_start[0] + jnp.einsum(
        "jr,rnc->jnc", chooser, state_piece, precision=lax.Precision.HIGHEST
    )
    filter_prefix = state_start[1] + jnp.einsum(
        "jr,rkc->jkc", chooser, filter_piece, precision=lax.Precision.HIGHEST
    )
    every_slot = prompt_slot[session_prompt]
    holder = every_slot // held_rows
    local_row = every_slot % held_rows
    chooser = (
        (holder == lax.axis_index("sess"))[:, None]
        & (local_row[:, None] == jnp.arange(held_rows, dtype=jnp.int32)[None, :])
    ).astype(jnp.bfloat16)
    send_keys = jnp.einsum(
        "jr,rcw->jcw", chooser, cache_keys, preferred_element_type=jnp.float32
    ).astype(jnp.bfloat16)
    send_values = jnp.einsum(
        "jr,rcw->jcw", chooser, stored_cache_values, preferred_element_type=jnp.float32
    ).astype(jnp.bfloat16)
    got_keys, got_values = (
        lax.all_to_all(send_keys, "sess", split_axis=0, concat_axis=0, tiled=True),
        lax.all_to_all(send_values, "sess", split_axis=0, concat_axis=0, tiled=True),
    )
    source_row = wanted // held_rows * group_sessions + jnp.arange(group_sessions, dtype=jnp.int32)
    old_keys = got_keys[source_row]
    old_values = got_values[source_row]
    tap_count = filter_taps.shape[0]
    series = jnp.concatenate(
        [filter_prefix, mamba_input.astype(jnp.float32).reshape(group_sessions, NEW, channels)],
        axis=1,
    )
    filtered = filter_bias + sum(
        (filter_taps[offset] * series[:, offset : offset + NEW] for offset in range(tap_count))
    )
    filter_out = jax.nn.silu(filtered).astype(jnp.bfloat16).reshape(group_sessions * NEW, channels)
    projected = lax.psum(
        jnp.dot(filter_out, input_select, preferred_element_type=jnp.float32).astype(jnp.bfloat16),
        "exp",
    ).astype(jnp.float32)
    step_rank = step_weight.shape[0]
    states = decay_log.shape[0]
    step_in = projected[:, :step_rank].astype(jnp.bfloat16)
    step_size = jax.nn.softplus(
        jnp.dot(step_in, step_weight, preferred_element_type=jnp.float32) + step_bias
    )
    input_mix = projected[:, step_rank : step_rank + states]
    readout = projected[:, step_rank + states :]
    signal = filter_out.astype(jnp.float32)
    emitted = selective_scan(
        step_size, signal, input_mix, readout, start_state, -jnp.exp(decay_log), 8
    )
    gated = ((emitted + skip_scale * signal) * jax.nn.silu(mamba_gate.astype(jnp.float32))).astype(
        jnp.bfloat16
    )
    after_mamba = residual.astype(jnp.float32) + lax.psum_scatter(
        jnp.dot(gated, output_weight, preferred_element_type=jnp.float32).astype(jnp.bfloat16),
        "exp",
        scatter_dimension=0,
        tiled=True,
    ).astype(jnp.float32)
    pieces = lax.all_gather(normalize(after_mamba), "exp", axis=0, tiled=True)
    projected_rows = jnp.concatenate(
        [
            jnp.dot(pieces, query_weight, preferred_element_type=jnp.float32),
            jnp.dot(pieces, key_matrix, preferred_element_type=jnp.float32),
            jnp.dot(pieces, value_matrix, preferred_element_type=jnp.float32),
        ],
        axis=1,
    ).astype(jnp.bfloat16)
    query_width = query_weight.shape[1]
    key_width = key_matrix.shape[1]
    queries = projected_rows[:, :query_width]
    new_keys = projected_rows[:, query_width : query_width + key_width]
    new_values = projected_rows[:, query_width + key_width :]
    heads_out = attend_group(queries, new_keys, new_values, old_keys, old_values, group_sessions)
    head_total = lax.psum_scatter(
        jnp.dot(heads_out, head_weight, preferred_element_type=jnp.float32).astype(jnp.bfloat16),
        "exp",
        scatter_dimension=0,
        tiled=True,
    ).astype(jnp.float32)
    return (after_mamba + head_total).astype(jnp.bfloat16)


def solution(mesh):
    return jax.shard_map(
        shards,
        mesh=mesh,
        in_specs=(
            P(("sess", "exp"), None),
            P("sess", "exp"),
            P("sess", "exp"),
            P(None, "exp"),
            P("exp"),
            P("exp", None),
            P(None, "exp"),
            P("exp"),
            P(None, "exp"),
            P("exp"),
            P("exp", None),
            P(None, "exp"),
            P(None, "exp"),
            P(None, "exp"),
            P("exp", None),
            P("sess", None, "exp"),
            P("sess", None, "exp"),
            P("sess", None, "exp"),
            P("sess", None, "exp"),
            P(),
            P(),
        ),
        out_specs=P(("sess", "exp"), None),
        check_vma=False,
    )
```

profile of v0, /device:TPU:0, one launch (start us, length us, event | category | flops | bytes accessed | tf_op | source)
XLA Modules:
  0.0 494.1 jit_solution(1669462651447133371)
XLA Ops:
  9.8 25.1 %all_gather.10 = bf16[32,3,1024]{2,1,0:T(4,128)(2,1)S(1)} all-gather(bf16[2,3,1024]{2,1,0:T(4,128)(2,1)S(1)} %copy.109), channel_id=1, replica_groups=mesh['sess'=16,'exp'=8] {'sess'}, dimensions={0}, use_global_device_ids=true | all-gather | bytes 208896 | tf_op jit(solution)/shard_map/all_gather | solution.py:106
  34.9 1.3 gather_fusion
  36.5 1.5 convert.7
  38.0 2.4 convert_bitcast_fusion
  40.4 1.2 convolution_convert_fusion.5
  42.5 71.8 %all-reduce.2.cloned.1.call-done = bf16[512,288]{0,1:T(8,128)(2,1)} async-done(((bf16[512,288]{0,1:T(8,128)(2,1)}), bf16[512,288]{0,1:T(8,128)(2,1)}) %all-reduce.2.cloned.1.call-update) | async-done | bytes 294928 | tf_op jit(solution)/shard_map/psum | solution.py:147
  115.4 2.3 compare_select_fusion
  117.8 2.7 copy.112
  120.4 2.4 fusion.49
  123.0 80.3 %while.12 = (s32[]{:T(128)}, f32[4,16,1024]{2,1,0:T(8,128)S(1)}, f32[16,8,4,1024]{3,2,1,0:T(4,128)}, f32[16,8,4,1024]{3,2,1,0:T(4,128)}, f32[16,1024]{1,0:T(8,12...) while((s32[]{:T(128)}, f32[4,16,1024]{2,1,0:T(8,128)S(1)}, ...), condition=%wide.region_10.11_spmd, body=%wide.region_1.10_spmd.sunk | while | flops 4718601 | bytes 3422045 | solution.py:30
  123.2 1.6 constant_dynamic-slice_fusion.25
  124.9 0.9 fusion.98
  128.1 2.1 constant_dynamic-slice_fusion.25
  130.2 0.9 fusion.98
  133.3 1.6 constant_dynamic-slice_fusion.25
  135.0 0.9 fusion.98
  138.1 1.6 constant_dynamic-slice_fusion.25
  139.8 0.9 fusion.98
  143.0 1.6 constant_dynamic-slice_fusion.25
  144.6 0.9 fusion.98
  147.8 1.9 constant_dynamic-slice_fusion.25
  149.7 0.9 fusion.98
  152.9 1.7 constant_dynamic-slice_fusion.25
  154.5 0.9 fusion.98
  157.7 2.5 constant_dynamic-slice_fusion.25
  160.2 0.9 fusion.98
  163.4 1.7 constant_dynamic-slice_fusion.25
  165.0 0.9 fusion.98
  168.2 1.6 constant_dynamic-slice_fusion.25
  169.9 0.9 fusion.98
  173.0 1.6 constant_dynamic-slice_fusion.25
  174.7 0.9 fusion.98
  177.8 1.9 constant_dynamic-slice_fusion.25
  179.8 0.9 fusion.98
  182.9 1.9 constant_dynamic-slice_fusion.25
  184.8 0.9 fusion.98
  188.0 1.7 constant_dynamic-slice_fusion.25
  189.7 0.9 fusion.98
  192.9 2.2 constant_dynamic-slice_fusion.25
  195.1 0.9 fusion.98
  198.3 1.8 constant_dynamic-slice_fusion.25
  200.2 0.9 fusion.98
  203.3 3.0 copy.117
  207.7 6.2 %convolution_convert_fusion = bf16[512,4096]{1,0:T(8,128)(2,1)} fusion(bf16[512,1024]{1,0:T(8,128)(2,1)S(1)} %fusion.39, bf16[1024,4096]{1,0:T(8,128)(2,1)S(1)} %copy-done.11), kind=kOutput, calls=%fused_computation.94 | convolution fusion | flops 4297064448 | bytes 13631488 | tf_op jit(solution)/shard_map/dot_general | solution.py:167
  215.4 1.3 convolution_convert_fusion.3
  216.7 4.6 copy.119
  221.3 6.6 %all-to-all-start = ((bf16[64,256,128]{2,1,0:T(8,128)(2,1)}), bf16[64,256,128]{2,1,0:T(8,128)(2,1)}, u32[]{:S(2)}, u32[]{:S(2)}) async-start(bf16[64,256,128]{2,1,0:T(8,128)(2,1)} %copy.119), calls=%async_computation.1 | async-start | bytes 8388608 | tf_op jit(solution)/shard_map/all_to_all | solution.py:133
  228.2 82.7 %reduce-scatter.3.cloned.1.call-done = bf16[64,4096]{1,0:T(8,128)(2,1)} async-done(((bf16[512,4096]{1,0:T(8,128)(2,1)}), bf16[64,4096]{1,0:T(8,128)(2,1)}) %reduce-scatter.3.cloned.1.call-update) | async-done | bytes 524304 | tf_op jit(solution)/shard_map/reduce_scatter | solution.py:166
  310.9 1.3 multiply_reduce_fusion.8
  312.3 2.0 multiply_convert_fusion.1
  314.3 1.3 convolution_convert_fusion.2
  315.6 4.6 copy.123
  320.3 6.6 %all-to-all-start.1 = ((bf16[64,256,128]{2,1,0:T(8,128)(2,1)}), bf16[64,256,128]{2,1,0:T(8,128)(2,1)}, u32[]{:S(2)}, u32[]{:S(2)}) async-start(bf16[64,256,128]{2,1,0:T(8,128)(2,1)} %copy.123), calls=%async_computation.2 | async-start | bytes 8388608 | tf_op jit(solution)/shard_map/all_to_all | solution.py:132
  327.0 2.8 gather_fusion.2
  329.9 57.3 %all-to-all-done.1 = bf16[64,256,128]{2,1,0:T(8,128)(2,1)} async-done(((bf16[64,256,128]{2,1,0:T(8,128)(2,1)}), bf16[64,256,128]{2,1,0:T(8,128)(2,1)}, u32[]{:S(2)}, u32[]{:S(2)}) %all-to-all-start.1) | async-done | bytes 4194336 | tf_op jit(solution)/shard_map/all_to_all | solution.py:132
  387.2 2.8 gather_fusion.3
  390.0 20.6 %all-gather.5.cloned.1.call-done = bf16[512,4096]{1,0:T(8,128)(2,1)} async-done(((bf16[64,4096]{1,0:T(8,128)(2,1)}), bf16[512,4096]{1,0:T(8,128)(2,1)}) %all-gather.5.cloned.1.call-update) | async-done | bytes 4194320 | tf_op jit(solution)/shard_map/all_gather | solution.py:172
  410.6 5.8 %convolution_convert_fusion.4 = bf16[512,512]{1,0:T(8,128)(2,1)S(1)} fusion(bf16[512,4096]{1,0:T(8,128)(2,1)} %all-gather.5.cloned.1.call-done, bf16[4096,512]{1,0:T(8,128)(2,1)} %param.34), kind=kOutput, calls=%fused_computation.131 | convolution fusion | flops 2147745792 | bytes 8912896 | tf_op jit(solution)/shard_map/dot_general | solution.py:175
  416.5 3.4 convolution_convert_fusion.7
  420.1 3.7 convolution_convert_fusion.6
  425.1 1.0 fusion.46
  426.5 6.5 %convolution_convert_fusion.1 = bf16[512,4096]{1,0:T(8,128)(2,1)} fusion(bf16[512,4096]{1,0:T(8,128)(2,1)} %param.37, bf16[64,8,4,128]{3,2,1,0:T(4,128)(2,1)S(1)} %bitcast.247), kind=kOutput, calls=%fused_computation.95 | convolution fusion | flops 2149580800 | bytes 8912896 | tf_op jit(solution)/shard_map/dot_general | solution.py:188
  433.0 52.0 %reduce-scatter.5.cloned.1.call-done = bf16[64,4096]{1,0:T(8,128)(2,1)} async-done(((bf16[512,4096]{1,0:T(8,128)(2,1)}), bf16[64,4096]{1,0:T(8,128)(2,1)}) %reduce-scatter.5.cloned.1.call-update) | async-done | bytes 524304 | tf_op jit(solution)/shard_map/reduce_scatter | solution.py:187
  485.0 2.0 add_convert_fusion
  (284 shorter events, 44.8 us)
Async XLA Ops:
  7.4 409.2 %copy-start = (bf16[4096,128]{1,0:T(8,128)(2,1)S(1)}, bf16[4096,128]{1,0:T(8,128)(2,1)}, u32[]{:S(2)}) copy-start(bf16[4096,128]{1,0:T(8,128)(2,1)} %param.36) | copy-start | bytes 3145732
  7.4 106.9 %all-reduce.2.cloned.1.call-start = ((), (), s32[]{:S(2)}) async-start(), calls=%async_computation.5 | async-start | bytes 589824 | tf_op jit(solution)/shard_map/psum | solution.py:147
  9.8 28.1 %copy-start.9 = (f32[1024]{0:T(1024)S(1)}, f32[1024]{0:T(1024)}, u32[]{:S(2)}) copy-start(f32[1024]{0:T(1024)} %param.27) | copy-start | bytes 12292
  37.9 2.5 copy-start.12
  40.4 1.3 copy-start.7
  40.4 2.1 copy-start.8
  40.4 75.0 %copy-start.13 = (bf16[256,1024]{1,0:T(8,128)(2,1)S(1)}, bf16[256,1024]{1,0:T(8,128)(2,1)}, u32[]{:S(2)}) copy-start(bf16[256,1024]{1,0:T(8,128)(2,1)} %param.29) | copy-start | bytes 1572868
  40.4 75.0 %copy-start.14 = (f32[1024]{0:T(1024)S(1)}, f32[1024]{0:T(1024)}, u32[]{:S(2)}) copy-start(f32[1024]{0:T(1024)} %param.30) | copy-start | bytes 12292
  41.7 78.8 %all-gather.3.cloned.1.call-start = ((), (), s32[]{:S(2)}) async-start(), calls=%async_computation.4 | async-start | bytes 1114112 | tf_op jit(solution)/shard_map/all_gather | solution.py:103
  42.4 268.5 %reduce-scatter.3.cloned.1.call-start = ((), (), s32[]{:S(2)}) async-start(), calls=%async_computation.6 | async-start | bytes 4718592 | tf_op jit(solution)/shard_map/reduce_scatter | solution.py:166
  203.3 3.0 copy-start.4
  203.3 3.0 copy-start.10
  203.3 4.4 copy-start.11
  213.9 0.7 copy-start.15
  213.9 0.7 copy-start.1
  213.9 1.5 copy-start.5
  221.3 89.6 %copy-start.2 = (bf16[64,4096]{1,0:T(8,128)(2,1)S(1)}, bf16[64,4096]{1,0:T(8,128)(2,1)}, u32[]{:S(2)}) copy-start(bf16[64,4096]{1,0:T(8,128)(2,1)} %param.23) | copy-start | bytes 1572868
  221.3 98.9 %all-to-all-start = ((bf16[64,256,128]{2,1,0:T(8,128)(2,1)}), bf16[64,256,128]{2,1,0:T(8,128)(2,1)}, u32[]{:S(2)}, u32[]{:S(2)}) async-start(bf16[64,256,128]{2,1,0:T(8,128)(2,1)} %copy.119), calls=%async_computation.1 | async-start | bytes 8388608 | tf_op jit(solution)/shard_map/all_to_all | solution.py:133
  227.9 86.4 %copy-start.6 = (bf16[2,256,128]{2,1,0:T(8,128)(2,1)S(1)}, bf16[2,256,128]{2,1,0:T(8,128)(2,1)}, u32[]{:S(2)}) copy-start(bf16[2,256,128]{2,1,0:T(8,128)(2,1)} %param.38) | copy-start | bytes 393220
  227.9 182.7 %all-gather.5.cloned.1.call-start = ((), (), s32[]{:S(2)}) async-start(), calls=%async_computation.7 | async-start | bytes 4718592 | tf_op jit(solution)/shard_map/all_gather | solution.py:172
  320.3 66.9 %all-to-all-start.1 = ((bf16[64,256,128]{2,1,0:T(8,128)(2,1)}), bf16[64,256,128]{2,1,0:T(8,128)(2,1)}, u32[]{:S(2)}, u32[]{:S(2)}) async-start(bf16[64,256,128]{2,1,0:T(8,128)(2,1)} %copy.123), calls=%async_computation.2 | async-start | bytes 8388608 | tf_op jit(solution)/shard_map/all_to_all | solution.py:132
  326.8 158.1 %reduce-scatter.5.cloned.1.call-start = ((), (), s32[]{:S(2)}) async-start(), calls=%async_computation.8 | async-start | bytes 4718592 | tf_op jit(solution)/shard_map/reduce_scatter | solution.py:187
  433.0 52.0 %copy-start.3 = (bf16[64,4096]{1,0:T(8,128)(2,1)S(1)}, bf16[64,4096]{1,0:T(8,128)(2,1)}, u32[]{:S(2)}) copy-start(bf16[64,4096]{1,0:T(8,128)(2,1)} %reduce-scatter.3.cloned.1.call-done) | copy-start | bytes 1572868
Sparse Core Ops, SparseCore 0:
  41.8 72.4 all-reduce.1
  214.0 96.8 reduce-scatter.2
  314.4 96.1 all-gather.4
  433.1 51.7 reduce-scatter.4
Sparse Core Ops, SparseCore 1:
  44.9 42.7 all-gather.2
where the time goes:
time: 498 us; the launch traced here: 494 us
  waiting for transfers between devices  284 us (57%)
  local copies, waits for them, and re-layouts  68.6 us (14%)
  other arithmetic  50.3 us (10%)
  matrix products  36.1 us (7%)
  blocking collectives  25.1 us (5%)
  between operations  14.9 us (3%)
  starting transfers between devices  13.5 us (3%)
    reduce_scatter x1, waiting for transfers between devices, shards(): lax.psum_scatter(jnp.dot(gated, output_weight, preferred_element_type=jnp...  82.7 us
    psum x1, waiting for transfers between devices, shards(): lax.psum(jnp.dot(filter_out, input_select, preferred_element_type=jnp.flo...  71.8 us
    all_to_all x1, waiting for transfers between devices, shards(): lax.all_to_all(send_keys, 'sess', split_axis=0, concat_axis=0, tiled=True)  57.3 us
    reduce_scatter x1, waiting for transfers between devices, shards(): lax.psum_scatter(jnp.dot(heads_out, head_weight, preferred_element_type=j...  52 us
    slice x16, local copies, waits for them, and re-layouts, selective_scan(): lax.scan(advance, start_state, (frame_major(step_size), frame_major(signa...  29.2 us
    all_gather x1, blocking collectives, shards(): lax.all_gather(cache_filter.astype(jnp.float32).astype(jnp.bfloat16), 'se...  25.1 us
    reduce_sum x48, other arithmetic, advance(): return (carried, jnp.sum(frame_readout[:, :, None] * carried, axis=1))  22.7 us
    all_gather x1, waiting for transfers between devices, shards(): pieces = lax.all_gather(normalize(after_mamba), 'exp', axis=0, tiled=True)  20.6 us
  transfers between devices with their start and end apart: 7, of which 5 were waited for; matrix products, arithmetic and copies ran while one was open for 6% of the time, Pallas kernels for 0%

commit v1 on v0

v1 whole, which is shorter than its diff:
```python
import functools
import math

import jax
import jax.numpy as jnp
from jax import lax
from jax.experimental import pallas as pl
from jax.experimental.pallas import tpu as pltpu
from jax.sharding import PartitionSpec as P

HEAD_SIZE = 128
NEW = 128
OWN = 64
EPSILON = 1e-06
LOG2E = math.log2(math.e)
MIB = 1 << 20


def y_swap():
    return [(y * 4 + z, (1 - y) * 4 + z) for y in range(2) for z in range(4)]


def z_shift(d):
    return [(y * 4 + z, y * 4 + (z + d) % 4) for y in range(2) for z in range(4)]


def sess_shift(far, x, core):
    return [
        (f * 8 + a * 2 + c, (f ^ far) * 8 + ((a + x) % 4) * 2 + (c ^ core))
        for f in range(2)
        for a in range(4)
        for c in range(2)
    ]


def sess_gather(value):
    pair = jnp.concatenate([value, lax.ppermute(value, "sess", sess_shift(1, 0, 0))], axis=0)
    mine = jnp.concatenate(
        [pair] + [lax.ppermute(pair, "sess", sess_shift(0, -d, 0)) for d in (1, 2, 3)], axis=0
    )
    return mine, lax.ppermute(mine, "sess", sess_shift(0, 0, 1))


def exp_gather(value):
    pair = jnp.stack([value, lax.ppermute(value, "exp", y_swap())])
    return jnp.stack([pair] + [lax.ppermute(pair, "exp", z_shift(-d)) for d in (1, 2, 3)])


def session_of(g, meta):
    return ((meta[1] >> 2) ^ (1 - (g >> 1))) * 2 + (g & 1)


def place_of(g, meta, prompts, slots):
    slot = slots[prompts[meta[0] * 4 + session_of(g, meta)]]
    holder = slot >> 1
    far = (holder >> 3) ^ (meta[0] >> 3)
    x = ((holder >> 1) - (meta[0] >> 1)) & 3
    return (x * 2 + far) * 2 + (slot & 1), (holder ^ meta[0]) & 1


def z_step(g, half, meta):
    return ((g & 1) * 2 + half - meta[1]) & 3


def row_of(g, meta, prompts, slots):
    return place_of(g, meta, prompts, slots)[0]


def side_of(g, meta, prompts, slots):
    return place_of(g, meta, prompts, slots)[1]


def conv_kernel(
    meta, prompts, slots, x_ref, here_ref, there_ref, taps_ref, bias_ref, select_ref, out_ref, part_ref, series
):
    g = pl.program_id(0)
    new, channels = x_ref.shape
    rows = here_ref.shape[1]
    here = here_ref[0].astype(jnp.float32)
    there = there_ref[0].astype(jnp.float32)
    series[8 - rows : 8] = jnp.where(side_of(g, meta, prompts, slots) == 1, there, here)
    series[8:] = x_ref[...].astype(jnp.float32)
    total = jnp.broadcast_to(bias_ref[...], (new, channels))
    for k in range(taps_ref.shape[0]):
        total += taps_ref[k : k + 1] * series[8 - rows + k : 8 - rows + k + new]
    out = (total / (1.0 + jnp.exp(-total))).astype(jnp.bfloat16)
    out_ref[...] = out
    part_ref[...] = jnp.dot(
        out, select_ref[...], preferred_element_type=jnp.float32
    ).astype(jnp.bfloat16)


def whole(a):
    return pl.BlockSpec(a.shape, lambda *_: (0,) * a.ndim)


def conv_project(scalars, x, here, there, taps, bias, select):
    tokens, channels = x.shape
    rows = here.shape[1]
    bias = bias.reshape(1, channels)

    def by_session(g, meta, prompts, slots):
        return session_of(g, meta), 0

    def by_row(g, *refs):
        return row_of(g, *refs), 0, 0

    return pl.pallas_call(
        conv_kernel,
        grid_spec=pltpu.PrefetchScalarGridSpec(
            num_scalar_prefetch=3,
            grid=(tokens // NEW,),
            in_specs=[
                pl.BlockSpec((NEW, channels), by_session),
                pl.BlockSpec((1, rows, channels), by_row),
                pl.BlockSpec((1, rows, channels), by_row),
                whole(taps),
                whole(bias),
                whole(select),
            ],
            out_specs=[
                pl.BlockSpec((NEW, channels), by_session),
                pl.BlockSpec((NEW, select.shape[1]), by_session),
            ],
            scratch_shapes=[pltpu.VMEM((NEW + 8, channels), jnp.float32)],
        ),
        out_shape=[
            jax.ShapeDtypeStruct((tokens, channels), jnp.bfloat16),
            jax.ShapeDtypeStruct((tokens, select.shape[1]), jnp.bfloat16),
        ],
        compiler_params=pltpu.CompilerParams(vmem_limit_bytes=32 * MIB),
        name="conv_project",
    )(*scalars, x, here, there, taps, bias, select)


def scan_kernel(
    meta,
    prompts,
    slots,
    first_ref,
    second_ref,
    signal_ref,
    gate_ref,
    weight_ref,
    bias_ref,
    decay_ref,
    here_ref,
    there_ref,
    skip_ref,
    gated_ref,
    rate_s,
    state_s,
    step_s,
    drive_s,
    emit_s,
    mix_s,
):
    g = pl.program_id(0)
    new, channels = signal_ref.shape
    states = decay_ref.shape[0]
    blocks = channels // 128
    rank = weight_ref.shape[0]
    half = new // 2

    @pl.when(g == 0)
    def _():
        rate = jnp.exp(decay_ref[...]) * (-LOG2E)
        for b in range(blocks):
            rate_s[:, b, :] = rate[:, b * 128 : (b + 1) * 128]

    start = jnp.where(
        side_of(g, meta, prompts, slots) == 1,
        there_ref[0].astype(jnp.float32),
        here_ref[0].astype(jnp.float32),
    )
    for b in range(blocks):
        state_s[:, b, :] = start[:, b * 128 : (b + 1) * 128]
    projected = jnp.concatenate([first_ref[0, 0], second_ref[0, 0]], axis=0)
    before = (
        jnp.dot(projected[:, :rank], weight_ref[...], preferred_element_type=jnp.float32)
        + bias_ref[...]
    )
    size = jnp.maximum(before, 0.0) + jnp.log1p(jnp.exp(-jnp.abs(before)))
    drive = size * signal_ref[...].astype(jnp.float32)
    for b in range(blocks):
        cols = slice(b * 128, (b + 1) * 128)
        step_s[:, b] = size[:, cols].reshape(new // 8, 8, 128)
        drive_s[:, b] = drive[:, cols].reshape(new // 8, 8, 128)
    mix = jnp.transpose(projected[:, rank:].astype(jnp.float32))
    for t in range(new):
        mix_s[t] = jnp.broadcast_to(mix[:, t : t + 1], (2 * states, 128))

    def advance(i, state):
        state = list(state)
        for s in range(8):
            d = step_s[i, :, s, :]
            u = drive_s[i, :, s, :]
            t = i * 8 + s
            total = None
            for n in range(states):
                state[n] = jnp.exp2(d * rate_s[n]) * state[n] + u * mix_s[t, n : n + 1, :]
                term = state[n] * mix_s[t, states + n : states + n + 1, :]
                total = term if total is None else total + term
            emit_s[i, :, s, :] = total
        return tuple(state)

    lax.fori_loop(0, new // 8, advance, tuple(state_s[n] for n in range(states)))
    for b in range(blocks):
        cols = slice(b * 128, (b + 1) * 128)
        emitted = emit_s[:, b].reshape(new, 128)
        gate = gate_ref[:, cols].astype(jnp.float32)
        signal = signal_ref[:, cols].astype(jnp.float32)
        gated = (
            (emitted + skip_ref[:, cols] * signal) * (gate / (1.0 + jnp.exp(-gate)))
        ).astype(jnp.bfloat16)
        for k in range(2):
            gated_ref[0, z_step(g, k, meta), :, cols] = gated[k * half : (k + 1) * half]


def scan_gate(scalars, projected, signal, gate, weight, bias, decay, here, there, skip):
    tokens, channels = signal.shape
    states = decay.shape[0]
    blocks = channels // 128
    width = projected.shape[-1]
    bias = bias.reshape(1, channels)
    skip = skip.reshape(1, channels)

    def by_session(g, meta, prompts, slots):
        return session_of(g, meta), 0

    def by_row(g, *refs):
        return row_of(g, *refs), 0, 0

    def piece(half):
        return lambda g, meta, prompts, slots: (z_step(g, half, meta), 1 - (g >> 1), 0, 0)

    return pl.pallas_call(
        scan_kernel,
        grid_spec=pltpu.PrefetchScalarGridSpec(
            num_scalar_prefetch=3,
            grid=(tokens // NEW,),
            in_specs=[
                pl.BlockSpec((1, 1, OWN, width), piece(0)),
                pl.BlockSpec((1, 1, OWN, width), piece(1)),
                pl.BlockSpec((NEW, channels), by_session),
                pl.BlockSpec((NEW, channels), by_session),
                whole(weight),
                whole(bias),
                whole(decay),
                pl.BlockSpec((1, states, channels), by_row),
                pl.BlockSpec((1, states, channels), by_row),
                whole(skip),
            ],
            out_specs=pl.BlockSpec(
                (1, 4, OWN, channels), lambda g, *_: (1 - (g >> 1), 0, 0, 0)
            ),
            scratch_shapes=[
                pltpu.VMEM((states, blocks, 128), jnp.float32),
                pltpu.VMEM((states, blocks, 128), jnp.float32),
                pltpu.VMEM((NEW // 8, blocks, 8, 128), jnp.float32),
                pltpu.VMEM((NEW // 8, blocks, 8, 128), jnp.float32),
                pltpu.VMEM((NEW // 8, blocks, 8, 128), jnp.float32),
                pltpu.VMEM((NEW, 2 * states, 128), jnp.float32),
            ],
        ),
        out_shape=jax.ShapeDtypeStruct((2, 4, OWN, channels), jnp.bfloat16),
        compiler_params=pltpu.CompilerParams(vmem_limit_bytes=32 * MIB),
        name="scan_gate",
    )(*scalars, projected, projected, signal, gate, weight, bias, decay, here, there, skip)


def attend_kernel(
    meta, prompts, slots, *refs
):
    (*rows_refs, here_k, here_v, there_k, there_v, out_ref) = refs
    g = pl.program_id(0)
    rows = jnp.concatenate([r[0, 0, 0] for r in rows_refs], axis=0)
    there = side_of(g, meta, prompts, slots) == 1
    old_keys = jnp.where(there, there_k[0], here_k[0])
    old_values = jnp.where(there, there_v[0], here_v[0])
    new = rows.shape[0]
    heads = rows.shape[1] // HEAD_SIZE - 2
    new_keys = rows[:, heads * HEAD_SIZE : (heads + 1) * HEAD_SIZE]
    new_values = rows[:, (heads + 1) * HEAD_SIZE :]
    queries = jnp.concatenate(
        [rows[:, k * HEAD_SIZE : (k + 1) * HEAD_SIZE] for k in range(heads)], axis=0
    )
    contract = (((1,), (1,)), ((), ()))
    scale = 1.0 / math.sqrt(HEAD_SIZE)
    old = lax.dot_general(queries, old_keys, contract, preferred_element_type=jnp.float32) * scale
    fresh = lax.dot_general(queries, new_keys, contract, preferred_element_type=jnp.float32) * scale
    at = lax.broadcasted_iota(jnp.int32, fresh.shape, 0) & (new - 1)
    fresh = jnp.where(lax.broadcasted_iota(jnp.int32, fresh.shape, 1) <= at, fresh, -1e30)
    top = jnp.maximum(
        jnp.max(old, axis=-1, keepdims=True), jnp.max(fresh, axis=-1, keepdims=True)
    )
    old = jnp.exp(old - top)
    fresh = jnp.exp(fresh - top)
    total = jnp.sum(old, axis=-1, keepdims=True) + jnp.sum(fresh, axis=-1, keepdims=True)
    inverse = 1.0 / total
    attended = jnp.dot(
        (old * inverse).astype(jnp.bfloat16), old_values, preferred_element_type=jnp.float32
    ) + jnp.dot(
        (fresh * inverse).astype(jnp.bfloat16), new_values, preferred_element_type=jnp.float32
    )
    attended = attended.astype(jnp.bfloat16)
    half = new // 2
    for k in range(2):
        for n in range(heads):
            out_ref[0, z_step(g, k, meta), :, n * HEAD_SIZE : (n + 1) * HEAD_SIZE] = attended[
                n * new + k * half : n * new + (k + 1) * half
            ]


def attend(scalars, rows, here_k, here_v, there_k, there_v):
    width = rows.shape[-1]
    quarter = rows.shape[3]
    cached = here_k.shape[1]
    query_width = width - 2 * HEAD_SIZE

    def piece(half, part):
        return lambda g, meta, prompts, slots: (part, 1 - (g >> 1), z_step(g, half, meta), 0, 0)

    def by_row(g, *refs):
        return row_of(g, *refs), 0, 0

    old = pl.BlockSpec((1, cached, HEAD_SIZE), by_row)
    return pl.pallas_call(
        attend_kernel,
        grid_spec=pltpu.PrefetchScalarGridSpec(
            num_scalar_prefetch=3,
            grid=(4,),
            in_specs=[
                pl.BlockSpec((1, 1, 1, quarter, width), piece(half, part))
                for half in range(2)
                for part in range(2)
            ]
            + [old] * 4,
            out_specs=pl.BlockSpec(
                (1, 4, OWN, query_width), lambda g, *_: (1 - (g >> 1), 0, 0, 0)
            ),
        ),
        out_shape=jax.ShapeDtypeStruct((2, 4, OWN, query_width), jnp.bfloat16),
        compiler_params=pltpu.CompilerParams(vmem_limit_bytes=32 * MIB),
        name="attend",
    )(*scalars, rows, rows, rows, rows, here_k, here_v, there_k, there_v)


def scatter_sum(left, weight):
    n = weight.shape[1]
    split = n // 2
    first, second = weight[:, :split], weight[:, split:]
    depth = left.shape[-1]

    def times(rows, w):
        lead = rows.shape[:-1]
        return (
            jnp.dot(rows.reshape(-1, depth), w, preferred_element_type=jnp.float32)
            .astype(jnp.bfloat16)
            .reshape(lead + (w.shape[1],))
        )

    got_a = lax.ppermute(times(left[1], first), "exp", y_swap())
    got_b = [
        lax.ppermute(times(left[:, d], second), "exp", z_shift(d)) for d in (1, 3, 2)
    ]
    own_a = times(left[0], first)
    own_b = times(left[:, 0], second)
    sum_b = own_b.astype(jnp.float32) + sum(v.astype(jnp.float32) for v in got_b)
    later_b = lax.ppermute(sum_b[1].astype(jnp.bfloat16), "exp", y_swap())
    sum_a = own_a.astype(jnp.float32) + got_a.astype(jnp.float32)
    later_a = [
        lax.ppermute(sum_a[d].astype(jnp.bfloat16), "exp", z_shift(d)) for d in (1, 3, 2)
    ]
    return jnp.concatenate(
        [
            sum_a[0] + sum(v.astype(jnp.float32) for v in later_a),
            sum_b[0] + later_b.astype(jnp.float32),
        ],
        axis=1,
    )


def token_gather(own):
    half = own.shape[0] // 2
    a, b = own[:half], own[half:]
    a_near = [a] + [None] * 3
    for d in (1, 3, 2):
        a_near[d] = lax.ppermute(a, "exp", z_shift(-d))
    b_pair = jnp.stack([b, lax.ppermute(b, "exp", y_swap())])
    a_near = jnp.stack(a_near)
    a_far = lax.ppermute(a_near, "exp", y_swap())
    b_all = [b_pair] + [None] * 3
    for d in (1, 3, 2):
        b_all[d] = lax.ppermute(b_pair, "exp", z_shift(-d))
    return jnp.stack([jnp.stack([a_near, a_far]), jnp.stack(b_all, axis=1)])


def normalize(hidden):
    return (
        hidden * lax.rsqrt(jnp.mean(hidden * hidden, axis=-1, keepdims=True) + EPSILON)
    ).astype(jnp.bfloat16)


def shards(
    residual,
    mamba_input,
    mamba_gate,
    filter_taps,
    filter_bias,
    input_select,
    step_weight,
    step_bias,
    decay_log,
    skip_scale,
    output_weight,
    query_weight,
    key_matrix,
    value_matrix,
    head_weight,
    cache_keys,
    stored_cache_values,
    cache_state,
    cache_filter,
    prompt_slot,
    session_prompt,
):
    meta = jnp.stack([lax.axis_index("sess"), lax.axis_index("exp")]).astype(jnp.int32)
    scalars = (meta, session_prompt, prompt_slot)
    filter_here, filter_there = sess_gather(cache_filter)
    state_here, state_there = sess_gather(cache_state.astype(jnp.bfloat16))
    keys_here, keys_there = sess_gather(cache_keys)
    values_here, values_there = sess_gather(stored_cache_values)
    signal, part = conv_project(
        scalars, mamba_input, filter_here, filter_there, filter_taps, filter_bias, input_select
    )
    pieces = lax.all_to_all(part.reshape(8, OWN, -1), "exp", 0, 0, tiled=True)
    own = jnp.sum(pieces.astype(jnp.float32), axis=0).astype(jnp.bfloat16)
    projected = exp_gather(own)
    gated = scan_gate(
        scalars,
        projected,
        signal,
        mamba_gate,
        step_weight,
        step_bias,
        decay_log,
        state_here,
        state_there,
        skip_scale,
    )
    after_mamba = residual.astype(jnp.float32) + scatter_sum(gated, output_weight)
    tokens = token_gather(normalize(after_mamba))
    weight = jnp.concatenate([query_weight, key_matrix, value_matrix], axis=1)
    rows = (
        jnp.dot(
            tokens.reshape(-1, tokens.shape[-1]), weight, preferred_element_type=jnp.float32
        )
        .astype(jnp.bfloat16)
        .reshape(tokens.shape[:-1] + (weight.shape[1],))
    )
    heads_out = attend(scalars, rows, keys_here, values_here, keys_there, values_there)
    return (after_mamba + scatter_sum(heads_out, head_weight)).astype(jnp.bfloat16)


def solution(mesh):
    return jax.shard_map(
        shards,
        mesh=mesh,
        in_specs=(
            P(("sess", "exp"), None),
            P("sess", "exp"),
            P("sess", "exp"),
            P(None, "exp"),
            P("exp"),
            P("exp", None),
            P(None, "exp"),
            P("exp"),
            P(None, "exp"),
            P("exp"),
            P("exp", None),
            P(None, "exp"),
            P(None, "exp"),
            P(None, "exp"),
            P("exp", None),
            P("sess", None, "exp"),
            P("sess", None, "exp"),
            P("sess", None, "exp"),
            P("sess", None, "exp"),
            P(),
            P(),
        ),
        out_specs=P(("sess", "exp"), None),
        check_vma=False,
    )
```

time: 498 us -> 221 us (0.44)
  waiting for transfers between devices: 284 us -> 92.9 us
  starting transfers between devices: 13.5 us -> 66.3 us
  local copies, waits for them, and re-layouts: 68.6 us -> 16.4 us
  other arithmetic: 50.3 us -> 7.22 us
  blocking collectives: 25.1 us -> 0 us
  Pallas kernels: 0 us -> 24.6 us
  matrix products: 36.1 us -> 12.3 us
  between operations: 14.9 us -> 0.66 us
    reduce_scatter x2 -> x0, waiting for transfers between devices: 135 us -> none  [the longest x1 82.7 us: shards(): lax.psum_scatter(jnp.dot(gated, output_weight, preferred_element_type=jnp...]
    ppermute x0 -> x48, waiting for transfers between devices: none -> 90.7 us  [the longest x6 34.9 us: scatter_sum(): lax.ppermute(times(left[:, d], second), 'exp', z_shift(d))]
    psum x1 -> x0, waiting for transfers between devices: 71.8 us -> none  [shards(): lax.psum(jnp.dot(filter_out, input_select, preferred_element_type=jnp.flo...]
    ppermute x0 -> x48, starting transfers between devices: none -> 60 us  [the longest x12 15.5 us: sess_gather(): lax.ppermute(pair, 'sess', sess_shift(0, -d, 0))]
    all_to_all x2 -> x1, waiting for transfers between devices: 57.3 us -> 2.22 us  [shards(): pieces = lax.all_to_all(part.reshape(8, OWN, -1), 'exp', 0, 0, tiled=True)]
    slice x18 -> x4, local copies, waits for them, and re-layouts: 30.8 us -> 0.22 us  [the longest x2 0.11 us: scatter_sum(): got_a = lax.ppermute(times(left[1], first), 'exp', y_swap())]
    all_gather x1 -> x0, blocking collectives: 25.1 us -> none  [shards(): lax.all_gather(cache_filter.astype(jnp.float32).astype(jnp.bfloat16), 'se...]
    pallas_call x0 -> x3, Pallas kernels: none -> 24.6 us  [the longest x1 17.7 us: scan_gate(): pl.pallas_call(scan_kernel, grid_spec=pltpu.PrefetchScalarGridSpec(num_sc...]
  transfers between devices with their start and end apart: 7 -> 49, of which waited for: 5 -> 24; matrix products, arithmetic and copies ran while one was open for 6% -> 11% of each run, Pallas kernels for 0% -> 10%
where the time goes in v1:
time: 221 us; the launch traced here: 220 us
  waiting for transfers between devices  92.9 us (42%)
  starting transfers between devices  66.3 us (30%)
  Pallas kernels  24.6 us (11%)
  local copies, waits for them, and re-layouts  16.4 us (7%)
  matrix products  12.3 us (6%)
  other arithmetic  7.22 us (3%)
    ppermute x6, waiting for transfers between devices, scatter_sum(): lax.ppermute(times(left[:, d], second), 'exp', z_shift(d))  34.9 us
    pallas_call x1, Pallas kernels, scan_gate(): pl.pallas_call(scan_kernel, grid_spec=pltpu.PrefetchScalarGridSpec(num_sc...  17.7 us
    ppermute x12, starting transfers between devices, sess_gather(): lax.ppermute(pair, 'sess', sess_shift(0, -d, 0))  15.5 us
    ppermute x6, waiting for transfers between devices, scatter_sum(): lax.ppermute(sum_a[d].astype(jnp.bfloat16), 'exp', z_shift(d))  14.9 us
    ppermute x12, waiting for transfers between devices, sess_gather(): lax.ppermute(pair, 'sess', sess_shift(0, -d, 0))  14 us
    unnamed x53, local copies, waits for them, and re-layouts  13.8 us
    ppermute x6, starting transfers between devices, scatter_sum(): lax.ppermute(times(left[:, d], second), 'exp', z_shift(d))  9.15 us
    dot_general x12, matrix products, times(): jnp.dot(rows.reshape(-1, depth), w, preferred_element_type=jnp.float32)  8.82 us
  transfers between devices with their start and end apart: 49, of which 24 were waited for; matrix products, arithmetic and copies ran while one was open for 11% of the time, Pallas kernels for 10%

profile of v1, /device:TPU:0, one launch (start us, length us, event | category | flops | bytes accessed | tf_op | source)
XLA Modules:
  0.0 220.3 jit_solution(17268951571263845003)
XLA Ops:
  0.8 3.4 %collective-permute-start = (bf16[2,3,1024]{2,1,0:T(4,128)(2,1)S(1)}, bf16[2,3,1024]{2,1,0:T(4,128)(2,1)S(1)}, u32[]{:S(2)}, u32[]{:S(2)}) collective-permute-start(bf16[2,3,1024]{2,1,0:T(4,128)(2,1)S(1)} %get-tuple-element.55), channel_id=1, source_target_pairs={{0,64},{8,72},{16,80},{24,88},{32,96},{40,104},{48,112},{56,120},{... | collective-permute-start | bytes 36872 | tf_op jit(solution)/shard_map/ppermute | solution.py:37
  4.2 0.9 constant_dynamic-update-slice_fusion.11
  6.2 2.9 %collective-permute-start.1 = (bf16[4,3,1024]{2,1,0:T(4,128)(2,1)S(1)}, bf16[4,3,1024]{2,1,0:T(4,128)(2,1)S(1)}, u32[]{:S(2)}, u32[]{:S(2)}) collective-permute-start(bf16[4,3,1024]{2,1,0:T(4,128)(2,1)S(1)} %get-tuple-element.51), channel_id=1, source_target_pairs={{0,48},{8,56},{16,0},{24,8},{32,16},{40,24},{48,32},{56,40},{64,11... | collective-permute-start | bytes 73736 | tf_op jit(solution)/shard_map/ppermute | solution.py:39
  9.2 1.4 copy.30.select_ref
  11.5 0.9 collective-permute-start.3
  12.4 3.7 %collective-permute-done.2 = bf16[4,3,1024]{2,1,0:T(4,128)(2,1)S(1)} collective-permute-done((bf16[4,3,1024]{2,1,0:T(4,128)(2,1)S(1)}, bf16[4,3,1024]{2,1,0:T(4,128)(2,1)S(1)}, u32[]{:S(2)}, u32[]{:S(2)}) %collective-permute-start.2) | collective-permute-done | bytes 24608 | tf_op jit(solution)/shard_map/ppermute | solution.py:39
  18.3 0.9 collective-permute-start.12
  19.2 1.2 copy-done.1
  23.2 3.4 %conv_project.1 = (bf16[512,1024]{1,0:T(8,128)(2,1)S(1)}, bf16[512,288]{1,0:T(8,128)(2,1)S(1)}) custom-call(s32[2]{0:T(128)S(1)} %pad_add_fusion.meta, s32[64]{0:T(128)S(1)} %copy-done.6, s32[32]{0:T(128)S(1)} %copy-done.8, bf16[512,1024]{1,0:T(8,128)(2,1)S(1)} %copy-done.1, bf16[16,3,1024]{2,1,0:T(4,128)(2,1)S(1)} %constant_dynamic-update-slice_fusion.2.here_ref, ...), custom_call_target="tpu_custom_call" | custom-call | tf_op jit(solution)/shard_map/conv_project/pallas_call | solution.py:108
  27.4 6.3 %all-to-all-start = ((bf16[8,64,288]{2,1,0:T(8,128)(2,1)}), bf16[8,64,288]{2,1,0:T(8,128)(2,1)}, u32[]{:S(2)}, u32[]{:S(2)}) async-start(bf16[8,64,288]{2,1,0:T(8,128)(2,1)} %bitcast.118), calls=%async_computation | async-start | bytes 786432 | tf_op jit(solution)/shard_map/all_to_all | solution.py:437
  33.7 0.9 constant_dynamic-update-slice_fusion.9
  34.6 0.9 constant_dynamic-update-slice_fusion.8
  35.6 0.9 constant_dynamic-update-slice_fusion.7.here_ref
  36.6 3.0 %collective-permute-start.30 = (bf16[2,256,128]{2,1,0:T(8,128)(2,1)}, bf16[2,256,128]{2,1,0:T(8,128)(2,1)}, u32[]{:S(2)}, u32[]{:S(2)}) collective-permute-start(bf16[2,256,128]{2,1,0:T(8,128)(2,1)} %param.36), channel_id=1, source_target_pairs={{0,64},{8,72},{16,80},{24,88},{32,96},{40,104},{48,112},{56,120},{... | collective-permute-start | bytes 393224 | tf_op jit(solution)/shard_map/ppermute | solution.py:37
  40.2 2.2 %all-to-all-done = bf16[8,64,288]{2,1,0:T(8,128)(2,1)} async-done(((bf16[8,64,288]{2,1,0:T(8,128)(2,1)}), bf16[8,64,288]{2,1,0:T(8,128)(2,1)}, u32[]{:S(2)}, u32[]{:S(2)}) %all-to-all-start) | async-done | bytes 294944 | tf_op jit(solution)/shard_map/all_to_all | solution.py:437
  42.4 1.1 reduce_sum.21
  44.3 0.9 constant_dynamic-update-slice_fusion.13
  45.3 3.6 %collective-permute-done.5 = bf16[64,288]{1,0:T(8,128)(2,1)S(1)} collective-permute-done((bf16[64,288]{1,0:T(8,128)(2,1)S(1)}, bf16[64,288]{1,0:T(8,128)(2,1)S(1)}, u32[]{:S(2)}, u32[]{:S(2)}) %collective-permute-start.5) | collective-permute-done | bytes 36896 | tf_op jit(solution)/shard_map/ppermute | solution.py:45
  48.9 2.7 %collective-permute-start.6 = (bf16[2,64,288]{2,1,0:T(8,128)(2,1)S(1)}, bf16[2,64,288]{2,1,0:T(8,128)(2,1)S(1)}, u32[]{:S(2)}, u32[]{:S(2)}) collective-permute-start(bf16[2,64,288]{2,1,0:T(8,128)(2,1)S(1)} %get-tuple-element.50), channel_id=1, source_target_pairs={{0,3},{1,0},{2,1},{3,2},{4,7},{5,4},{6,5},{7,6},{8,11},{9,8},{10,9... | collective-permute-start | bytes 221192 | tf_op jit(solution)/shard_map/ppermute | solution.py:46
  53.3 1.0 constant_dynamic-update-slice_fusion.12
  54.3 1.4 collective-permute-done.6
  55.6 2.6 %collective-permute-done.7 = bf16[2,64,288]{2,1,0:T(8,128)(2,1)S(1)} collective-permute-done((bf16[2,64,288]{2,1,0:T(8,128)(2,1)S(1)}, bf16[2,64,288]{2,1,0:T(8,128)(2,1)S(1)}, u32[]{:S(2)}, u32[]{:S(2)}) %collective-permute-start.7) | collective-permute-done | bytes 73760 | tf_op jit(solution)/shard_map/ppermute | solution.py:46
  58.3 1.0 collective-permute-done.8
  61.0 17.7 %scan_gate.1 = bf16[2,4,64,1024]{3,2,1,0:T(8,128)(2,1)S(1)} custom-call(s32[2]{0:T(128)S(1)} %pad_add_fusion.meta, s32[64]{0:T(128)S(1)} %copy-done.7, s32[32]{0:T(128)S(1)} %copy-done.9, bf16[4,2,64,288]{3,2,1,0:T(8,128)(2,1)S(1)} %pad_maximum_fusion.3.first_ref.second_ref, bf16[4,2,64,288]{3,2,1,0:T(8,128)(2,1)S(1)} %pad_maximum_fusion.3.first_ref.second_ref, ...), custom_call_target="tpu_custom_call" | custom-call | tf_op jit(solution)/shard_map/scan_gate/pallas_call | solution.py:237
  78.8 1.3 fusion.21
  80.1 1.2 collective-permute-start.14
  82.9 3.5 %collective-permute-start.19 = (bf16[2,64,2048]{2,1,0:T(8,128)(2,1)S(1)}, bf16[2,64,2048]{2,1,0:T(8,128)(2,1)S(1)}, u32[]{:S(2)}, u32[]{:S(2)}) collective-permute-start(bf16[2,64,2048]{2,1,0:T(8,128)(2,1)S(1)} %bitcast.154), channel_id=1, source_target_pairs={{0,3},{1,0},{2,1},{3,2},{4,7},{5,4},{6,5},{7,6},{8,11},{9,8},{10,9... | collective-permute-start | bytes 1572872 | tf_op jit(solution)/shard_map/ppermute | solution.py:365
  87.2 1.3 fusion.18
  89.2 18.1 %collective-permute-done.18 = bf16[2,64,2048]{2,1,0:T(8,128)(2,1)S(1)} collective-permute-done((bf16[2,64,2048]{2,1,0:T(8,128)(2,1)S(1)}, bf16[2,64,2048]{2,1,0:T(8,128)(2,1)S(1)}, u32[]{:S(2)}, u32[]{:S(2)}) %collective-permute-start.18) | collective-permute-done | bytes 524320 | tf_op jit(solution)/shard_map/ppermute | solution.py:365
  107.3 2.5 %collective-permute-start.31 = (bf16[4,256,128]{2,1,0:T(8,128)(2,1)S(1)}, bf16[4,256,128]{2,1,0:T(8,128)(2,1)S(1)}, u32[]{:S(2)}, u32[]{:S(2)}) collective-permute-start(bf16[4,256,128]{2,1,0:T(8,128)(2,1)S(1)} %get-tuple-element.45), channel_id=1, source_target_pairs={{0,48},{8,56},{16,0},{24,8},{32,16},{40,24},{48,32},{56,40},{64,11... | collective-permute-start | bytes 786440 | tf_op jit(solution)/shard_map/ppermute | solution.py:39
  110.2 0.9 collective-permute-start.21
  111.7 3.2 %collective-permute-start.16 = (bf16[64,2048]{1,0:T(8,128)(2,1)S(1)}, bf16[64,2048]{1,0:T(8,128)(2,1)S(1)}, u32[]{:S(2)}, u32[]{:S(2)}) collective-permute-start(bf16[64,2048]{1,0:T(8,128)(2,1)S(1)} %get-tuple-element.22), channel_id=1, source_target_pairs={{0,3},{1,0},{2,1},{3,2},{4,7},{5,4},{6,5},{7,6},{8,11},{9,8},{10,9... | collective-permute-start | bytes 786440 | tf_op jit(solution)/shard_map/ppermute | solution.py:373
  115.0 1.7 collective-permute-done.21
  116.7 3.3 %collective-permute-done.15 = bf16[64,2048]{1,0:T(8,128)(2,1)S(1)} collective-permute-done((bf16[64,2048]{1,0:T(8,128)(2,1)S(1)}, bf16[64,2048]{1,0:T(8,128)(2,1)S(1)}, u32[]{:S(2)}, u32[]{:S(2)}) %collective-permute-start.15) | collective-permute-done | bytes 262176 | tf_op jit(solution)/shard_map/ppermute | solution.py:373
  120.0 3.2 %collective-permute-done.16 = bf16[64,2048]{1,0:T(8,128)(2,1)S(1)} collective-permute-done((bf16[64,2048]{1,0:T(8,128)(2,1)S(1)}, bf16[64,2048]{1,0:T(8,128)(2,1)S(1)}, u32[]{:S(2)}, u32[]{:S(2)}) %collective-permute-start.16) | collective-permute-done | bytes 262176 | tf_op jit(solution)/shard_map/ppermute | solution.py:373
  123.2 1.3 collective-permute-done.17
  125.2 0.9 collective-permute-start.26
  126.2 2.5 %collective-permute-start.32 = (bf16[4,256,128]{2,1,0:T(8,128)(2,1)S(1)}, bf16[4,256,128]{2,1,0:T(8,128)(2,1)S(1)}, u32[]{:S(2)}, u32[]{:S(2)}) collective-permute-start(bf16[4,256,128]{2,1,0:T(8,128)(2,1)S(1)} %get-tuple-element.45), channel_id=1, source_target_pairs={{0,32},{8,40},{16,48},{24,56},{32,0},{40,8},{48,16},{56,24},{64,96... | collective-permute-start | bytes 786440 | tf_op jit(solution)/shard_map/ppermute | solution.py:39
  129.3 3.2 %collective-permute-start.22 = (bf16[32,4096]{1,0:T(8,128)(2,1)S(1)}, bf16[32,4096]{1,0:T(8,128)(2,1)S(1)}, u32[]{:S(2)}, u32[]{:S(2)}) collective-permute-start(bf16[32,4096]{1,0:T(8,128)(2,1)S(1)} %get-tuple-element.38), channel_id=1, source_target_pairs={{0,3},{1,0},{2,1},{3,2},{4,7},{5,4},{6,5},{7,6},{8,11},{9,8},{10,9... | collective-permute-start | bytes 786440 | tf_op jit(solution)/shard_map/ppermute | solution.py:389
  132.5 0.9 collective-permute-start.23
  133.5 6.2 %collective-permute-done.22 = bf16[32,4096]{1,0:T(8,128)(2,1)S(1)} collective-permute-done((bf16[32,4096]{1,0:T(8,128)(2,1)S(1)}, bf16[32,4096]{1,0:T(8,128)(2,1)S(1)}, u32[]{:S(2)}, u32[]{:S(2)}) %collective-permute-start.22) | collective-permute-done | bytes 262176 | tf_op jit(solution)/shard_map/ppermute | solution.py:389
  139.7 3.0 %collective-permute-start.35 = (bf16[4,256,128]{2,1,0:T(8,128)(2,1)S(1)}, bf16[4,256,128]{2,1,0:T(8,128)(2,1)S(1)}, u32[]{:S(2)}, u32[]{:S(2)}) collective-permute-start(bf16[4,256,128]{2,1,0:T(8,128)(2,1)S(1)} %get-tuple-element.41), channel_id=1, source_target_pairs={{0,48},{8,56},{16,0},{24,8},{32,16},{40,24},{48,32},{56,40},{64,11... | collective-permute-start | bytes 786440 | tf_op jit(solution)/shard_map/ppermute | solution.py:39
  143.4 3.0 %collective-permute-start.27 = (bf16[2,32,4096]{2,1,0:T(8,128)(2,1)S(1)}, bf16[2,32,4096]{2,1,0:T(8,128)(2,1)S(1)}, u32[]{:S(2)}, u32[]{:S(2)}) collective-permute-start(bf16[2,32,4096]{2,1,0:T(8,128)(2,1)S(1)} %get-tuple-element.40), channel_id=1, source_target_pairs={{0,3},{1,0},{2,1},{3,2},{4,7},{5,4},{6,5},{7,6},{8,11},{9,8},{10,9... | collective-permute-start | bytes 1572872 | tf_op jit(solution)/shard_map/ppermute | solution.py:395
  147.6 1.8 collective-permute-done.35
  149.3 1.0 collective-permute-start.25
  150.4 1.0 collective-permute-done.36
  151.6 7.5 %collective-permute-done.37 = bf16[4,256,128]{2,1,0:T(8,128)(2,1)S(1)} collective-permute-done((bf16[4,256,128]{2,1,0:T(8,128)(2,1)S(1)}, bf16[4,256,128]{2,1,0:T(8,128)(2,1)S(1)}, u32[]{:S(2)}, u32[]{:S(2)}) %collective-permute-start.37) | collective-permute-done | bytes 262176 | tf_op jit(solution)/shard_map/ppermute | solution.py:39
  159.1 4.5 %collective-permute-done.27 = bf16[2,32,4096]{2,1,0:T(8,128)(2,1)S(1)} collective-permute-done((bf16[2,32,4096]{2,1,0:T(8,128)(2,1)S(1)}, bf16[2,32,4096]{2,1,0:T(8,128)(2,1)S(1)}, u32[]{:S(2)}, u32[]{:S(2)}) %collective-permute-start.27) | collective-permute-done | bytes 524320 | tf_op jit(solution)/shard_map/ppermute | solution.py:395
  163.6 3.8 %collective-permute-done.29 = bf16[2,32,4096]{2,1,0:T(8,128)(2,1)S(1)} collective-permute-done((bf16[2,32,4096]{2,1,0:T(8,128)(2,1)S(1)}, bf16[2,32,4096]{2,1,0:T(8,128)(2,1)S(1)}, u32[]{:S(2)}, u32[]{:S(2)}) %collective-permute-start.29) | collective-permute-done | bytes 524320 | tf_op jit(solution)/shard_map/ppermute | solution.py:395
  169.0 1.8 copy-done.16
  171.4 3.4 %fusion.38 = bf16[512,768]{1,0:T(8,128)(2,1)S(1)} fusion(bf16[512,4096]{1,0:T(8,128)(2,1)S(1)} %bitcast.122, bf16[4096,128]{1,0:T(8,128)(2,1)S(1)} %copy-done.18, bf16[4096,128]{1,0:T(8,128)(2,1)S(1)} %copy-done.19, bf16[4096,512]{1,0:T(8,128)(2,1)S(1)} %copy-done.16), kind=kOutput, calls=%fused_computation.37 | convolution fusion | flops 3240493056 | bytes 11272192 | tf_op jit(solution)/shard_map/dot_general | solution.py:456
  174.9 3.5 %attend.1 = bf16[2,4,64,512]{3,2,1,0:T(8,128)(2,1)S(1)} custom-call(s32[2]{0:T(128)S(1)} %pad_add_fusion.meta, s32[64]{0:T(128)S(1)} %copy-done.7, s32[32]{0:T(128)S(1)} %copy-done.9, bf16[2,2,4,32,768]{4,3,2,1,0:T(8,128)(2,1)S(1)} %bitcast.114, bf16[2,2,4,32,768]{4,3,2,1,0:T(8,128)(2,1)S(1)} %bitcast.115, bf16[2,2,4,32,768]{4,3,2,1,0:T(8,128)(2,1)S(1)} %bitcast.116, ...), custom_call_target="tpu_custom_call" | custom-call | tf_op jit(solution)/shard_map/attend/pallas_call | solution.py:328
  179.2 1.0 collective-permute-start.40
  181.9 3.2 %collective-permute-start.45 = (bf16[2,64,2048]{2,1,0:T(8,128)(2,1)S(1)}, bf16[2,64,2048]{2,1,0:T(8,128)(2,1)S(1)}, u32[]{:S(2)}, u32[]{:S(2)}) collective-permute-start(bf16[2,64,2048]{2,1,0:T(8,128)(2,1)S(1)} %bitcast.158), channel_id=1, source_target_pairs={{0,3},{1,0},{2,1},{3,2},{4,7},{5,4},{6,5},{7,6},{8,11},{9,8},{10,9... | collective-permute-start | bytes 1572872 | tf_op jit(solution)/shard_map/ppermute | solution.py:365
  185.6 1.5 collective-permute-start.46
  188.4 16.8 %collective-permute-done.44 = bf16[2,64,2048]{2,1,0:T(8,128)(2,1)S(1)} collective-permute-done((bf16[2,64,2048]{2,1,0:T(8,128)(2,1)S(1)}, bf16[2,64,2048]{2,1,0:T(8,128)(2,1)S(1)}, u32[]{:S(2)}, u32[]{:S(2)}) %collective-permute-start.44) | collective-permute-done | bytes 524320 | tf_op jit(solution)/shard_map/ppermute | solution.py:365
  205.5 1.0 collective-permute-start.47
  207.1 1.5 collective-permute-start.41
  208.5 2.2 collective-permute-start.42
  210.7 1.4 collective-permute-start.43
  212.1 3.7 %collective-permute-done.41 = bf16[64,2048]{1,0:T(8,128)(2,1)S(1)} collective-permute-done((bf16[64,2048]{1,0:T(8,128)(2,1)S(1)}, bf16[64,2048]{1,0:T(8,128)(2,1)S(1)}, u32[]{:S(2)}, u32[]{:S(2)}) %collective-permute-start.41) | collective-permute-done | bytes 262176 | tf_op jit(solution)/shard_map/ppermute | solution.py:373
  215.8 1.6 collective-permute-done.42
  217.4 1.8 collective-permute-done.43
  219.4 1.0 fusion.45
  (142 shorter events, 28.8 us)
Async XLA Ops:
  0.0 59.4 %copy-start.9 = (s32[32]{0:T(128)S(1)}, s32[32]{0:T(128)}, u32[]{:S(2)}) copy-start(s32[32]{0:T(128)} %slots.5) | copy-start | bytes 388
  0.0 59.4 %copy-start.7 = (s32[64]{0:T(128)S(1)}, s32[64]{0:T(128)}, u32[]{:S(2)}) copy-start(s32[64]{0:T(128)} %prompts.5) | copy-start | bytes 772
  0.0 59.4 %copy-start.11 = (f32[1024]{0:T(1024)S(1)}, f32[1024]{0:T(1024)}, u32[]{:S(2)}) copy-start(f32[1024]{0:T(1024)} %param.28) | copy-start | bytes 12292
  0.0 59.4 %copy-start = (bf16[512,1024]{1,0:T(8,128)(2,1)S(1)}, bf16[512,1024]{1,0:T(8,128)(2,1)}, u32[]{:S(2)}) copy-start(bf16[512,1024]{1,0:T(8,128)(2,1)} %gate_ref.1) | copy-start | bytes 3145732
  0.8 5.3 %collective-permute-start = (bf16[2,3,1024]{2,1,0:T(4,128)(2,1)S(1)}, bf16[2,3,1024]{2,1,0:T(4,128)(2,1)S(1)}, u32[]{:S(2)}, u32[]{:S(2)}) collective-permute-start(bf16[2,3,1024]{2,1,0:T(4,128)(2,1)S(1)} %get-tuple-element.55), channel_id=1, source_target_pairs={{0,64},{8,72},{16,80},{24,88},{32,96},{40,104},{48,112},{56,120},{... | collective-permute-start | bytes 36872 | tf_op jit(solution)/shard_map/ppermute | solution.py:37
  5.1 11.0 %collective-permute-start.9 = (bf16[2,16,1024]{2,1,0:T(8,128)(2,1)S(1)}, bf16[2,16,1024]{2,1,0:T(8,128)(2,1)S(1)}, u32[]{:S(2)}, u32[]{:S(2)}) collective-permute-start(bf16[2,16,1024]{2,1,0:T(8,128)(2,1)S(1)} %get-tuple-element.10), channel_id=1, source_target_pairs={{0,64},{8,72},{16,80},{24,88},{32,96},{40,104},{48,112},{56,120},{... | collective-permute-start | bytes 196616 | tf_op jit(solution)/shard_map/ppermute | solution.py:37
  6.2 6.2 %collective-permute-start.1 = (bf16[4,3,1024]{2,1,0:T(4,128)(2,1)S(1)}, bf16[4,3,1024]{2,1,0:T(4,128)(2,1)S(1)}, u32[]{:S(2)}, u32[]{:S(2)}) collective-permute-start(bf16[4,3,1024]{2,1,0:T(4,128)(2,1)S(1)} %get-tuple-element.51), channel_id=1, source_target_pairs={{0,48},{8,56},{16,0},{24,8},{32,16},{40,24},{48,32},{56,40},{64,11... | collective-permute-start | bytes 73736 | tf_op jit(solution)/shard_map/ppermute | solution.py:39
  10.6 5.5 %collective-permute-start.2 = (bf16[4,3,1024]{2,1,0:T(4,128)(2,1)S(1)}, bf16[4,3,1024]{2,1,0:T(4,128)(2,1)S(1)}, u32[]{:S(2)}, u32[]{:S(2)}) collective-permute-start(bf16[4,3,1024]{2,1,0:T(4,128)(2,1)S(1)} %get-tuple-element.51), channel_id=1, source_target_pairs={{0,32},{8,40},{16,48},{24,56},{32,0},{40,8},{48,16},{56,24},{64,96... | collective-permute-start | bytes 73736 | tf_op jit(solution)/shard_map/ppermute | solution.py:39
  11.5 6.1 %collective-permute-start.3 = (bf16[4,3,1024]{2,1,0:T(4,128)(2,1)S(1)}, bf16[4,3,1024]{2,1,0:T(4,128)(2,1)S(1)}, u32[]{:S(2)}, u32[]{:S(2)}) collective-permute-start(bf16[4,3,1024]{2,1,0:T(4,128)(2,1)S(1)} %get-tuple-element.51), channel_id=1, source_target_pairs={{0,16},{8,24},{16,32},{24,40},{32,48},{40,56},{48,0},{56,8},{64,80... | collective-permute-start | bytes 73736 | tf_op jit(solution)/shard_map/ppermute | solution.py:39
  16.8 16.9 %collective-permute-start.10 = (bf16[4,16,1024]{2,1,0:T(8,128)(2,1)}, bf16[4,16,1024]{2,1,0:T(8,128)(2,1)}, u32[]{:S(2)}, u32[]{:S(2)}) collective-permute-start(bf16[4,16,1024]{2,1,0:T(8,128)(2,1)} %pad_maximum_fusion.4), channel_id=1, source_target_pairs={{0,48},{8,56},{16,0},{24,8},{32,16},{40,24},{48,32},{56,40},{64,11... | collective-permute-start | bytes 393224 | tf_op jit(solution)/shard_map/ppermute | solution.py:39
  17.6 1.6 collective-permute-start.4
  17.7 16.9 %collective-permute-start.11 = (bf16[4,16,1024]{2,1,0:T(8,128)(2,1)}, bf16[4,16,1024]{2,1,0:T(8,128)(2,1)}, u32[]{:S(2)}, u32[]{:S(2)}) collective-permute-start(bf16[4,16,1024]{2,1,0:T(8,128)(2,1)} %pad_maximum_fusion.4), channel_id=1, source_target_pairs={{0,32},{8,40},{16,48},{24,56},{32,0},{40,8},{48,16},{56,24},{64,96... | collective-permute-start | bytes 393224 | tf_op jit(solution)/shard_map/ppermute | solution.py:39
  18.3 17.2 %collective-permute-start.12 = (bf16[4,16,1024]{2,1,0:T(8,128)(2,1)}, bf16[4,16,1024]{2,1,0:T(8,128)(2,1)}, u32[]{:S(2)}, u32[]{:S(2)}) collective-permute-start(bf16[4,16,1024]{2,1,0:T(8,128)(2,1)} %pad_maximum_fusion.4), channel_id=1, source_target_pairs={{0,16},{8,24},{16,32},{24,40},{32,48},{40,56},{48,0},{56,8},{64,80... | collective-permute-start | bytes 393224 | tf_op jit(solution)/shard_map/ppermute | solution.py:39
  19.2 1.2 copy-start.1
  26.6 0.7 copy-start.3
  26.6 32.8 %copy-start.2 = (bf16[256,1024]{1,0:T(8,128)(2,1)S(1)}, bf16[256,1024]{1,0:T(8,128)(2,1)}, u32[]{:S(2)}) copy-start(bf16[256,1024]{1,0:T(8,128)(2,1)} %weight_ref.1) | copy-start | bytes 1572868
  27.4 15.0 %all-to-all-start = ((bf16[8,64,288]{2,1,0:T(8,128)(2,1)}), bf16[8,64,288]{2,1,0:T(8,128)(2,1)}, u32[]{:S(2)}, u32[]{:S(2)}) async-start(bf16[8,64,288]{2,1,0:T(8,128)(2,1)} %bitcast.118), calls=%async_computation | async-start | bytes 786432 | tf_op jit(solution)/shard_map/all_to_all | solution.py:437
  36.5 22.9 %collective-permute-start.13 = (bf16[16,16,1024]{2,1,0:T(8,128)(2,1)S(1)}, bf16[16,16,1024]{2,1,0:T(8,128)(2,1)}, u32[]{:S(2)}, u32[]{:S(2)}) collective-permute-start(bf16[16,16,1024]{2,1,0:T(8,128)(2,1)S(1)} %constant_dynamic-update-slice_fusion.7.here_ref), channel_id=1, source_target_pairs={{0,8},{8,0},{16,24},{24,16},{32,40},{40,32},{48,56},{56,48},{64,72... | collective-permute-start | bytes 1572872 | tf_op jit(solution)/shard_map/ppermute | solution.py:41
  36.6 15.9 %collective-permute-start.30 = (bf16[2,256,128]{2,1,0:T(8,128)(2,1)}, bf16[2,256,128]{2,1,0:T(8,128)(2,1)}, u32[]{:S(2)}, u32[]{:S(2)}) collective-permute-start(bf16[2,256,128]{2,1,0:T(8,128)(2,1)} %param.36), channel_id=1, source_target_pairs={{0,64},{8,72},{16,80},{24,88},{32,96},{40,104},{48,112},{56,120},{... | collective-permute-start | bytes 393224 | tf_op jit(solution)/shard_map/ppermute | solution.py:37
  39.5 89.6 %collective-permute-start.34 = (bf16[2,256,128]{2,1,0:T(8,128)(2,1)}, bf16[2,256,128]{2,1,0:T(8,128)(2,1)S(1)}, u32[]{:S(2)}, u32[]{:S(2)}) collective-permute-start(bf16[2,256,128]{2,1,0:T(8,128)(2,1)} %param.37), channel_id=1, source_target_pairs={{0,64},{8,72},{16,80},{24,88},{32,96},{40,104},{48,112},{56,120},{... | collective-permute-start | bytes 393224 | tf_op jit(solution)/shard_map/ppermute | solution.py:37
  43.5 5.4 %collective-permute-start.5 = (bf16[64,288]{1,0:T(8,128)(2,1)S(1)}, bf16[64,288]{1,0:T(8,128)(2,1)S(1)}, u32[]{:S(2)}, u32[]{:S(2)}) collective-permute-start(bf16[64,288]{1,0:T(8,128)(2,1)S(1)} %reduce_sum.21), channel_id=1, source_target_pairs={{0,4},{1,5},{2,6},{3,7},{4,0},{5,1},{6,2},{7,3},{8,12},{9,13},{10,... | collective-permute-start | bytes 110600 | tf_op jit(solution)/shard_map/ppermute | solution.py:45
  48.9 6.8 %collective-permute-start.6 = (bf16[2,64,288]{2,1,0:T(8,128)(2,1)S(1)}, bf16[2,64,288]{2,1,0:T(8,128)(2,1)S(1)}, u32[]{:S(2)}, u32[]{:S(2)}) collective-permute-start(bf16[2,64,288]{2,1,0:T(8,128)(2,1)S(1)} %get-tuple-element.50), channel_id=1, source_target_pairs={{0,3},{1,0},{2,1},{3,2},{4,7},{5,4},{6,5},{7,6},{8,11},{9,8},{10,9... | collective-permute-start | bytes 221192 | tf_op jit(solution)/shard_map/ppermute | solution.py:46
  51.6 6.7 %collective-permute-start.7 = (bf16[2,64,288]{2,1,0:T(8,128)(2,1)S(1)}, bf16[2,64,288]{2,1,0:T(8,128)(2,1)S(1)}, u32[]{:S(2)}, u32[]{:S(2)}) collective-permute-start(bf16[2,64,288]{2,1,0:T(8,128)(2,1)S(1)} %get-tuple-element.50), channel_id=1, source_target_pairs={{0,2},{1,3},{2,0},{3,1},{4,6},{5,7},{6,4},{7,5},{8,10},{9,11},{10,... | collective-permute-start | bytes 221192 | tf_op jit(solution)/shard_map/ppermute | solution.py:46
  52.5 6.8 %collective-permute-start.8 = (bf16[2,64,288]{2,1,0:T(8,128)(2,1)S(1)}, bf16[2,64,288]{2,1,0:T(8,128)(2,1)S(1)}, u32[]{:S(2)}, u32[]{:S(2)}) collective-permute-start(bf16[2,64,288]{2,1,0:T(8,128)(2,1)S(1)} %get-tuple-element.50), channel_id=1, source_target_pairs={{0,1},{1,2},{2,3},{3,0},{4,5},{5,6},{6,7},{7,4},{8,9},{9,10},{10,1... | collective-permute-start | bytes 221192 | tf_op jit(solution)/shard_map/ppermute | solution.py:46
  59.4 0.8 copy-start.4
  61.0 17.8 %copy-start.15 = (bf16[1024,4096]{1,0:T(8,128)(2,1)S(1)}, bf16[1024,4096]{1,0:T(8,128)(2,1)}, u32[]{:S(2)}) copy-start(bf16[1024,4096]{1,0:T(8,128)(2,1)} %param.31) | copy-start | bytes 25165828
  80.1 31.0 %collective-permute-start.14 = (bf16[4,64,2048]{2,1,0:T(8,128)(2,1)S(1)}, bf16[4,64,2048]{2,1,0:T(8,128)(2,1)S(1)}, u32[]{:S(2)}, u32[]{:S(2)}) collective-permute-start(bf16[4,64,2048]{2,1,0:T(8,128)(2,1)S(1)} %bitcast.152), channel_id=1, source_target_pairs={{0,4},{1,5},{2,6},{3,7},{4,0},{5,1},{6,2},{7,3},{8,12},{9,13},{10,... | collective-permute-start | bytes 3145736 | tf_op jit(solution)/shard_map/ppermute | solution.py:363
  82.1 25.2 %collective-permute-start.18 = (bf16[2,64,2048]{2,1,0:T(8,128)(2,1)S(1)}, bf16[2,64,2048]{2,1,0:T(8,128)(2,1)S(1)}, u32[]{:S(2)}, u32[]{:S(2)}) collective-permute-start(bf16[2,64,2048]{2,1,0:T(8,128)(2,1)S(1)} %bitcast.155), channel_id=1, source_target_pairs={{0,1},{1,2},{2,3},{3,0},{4,5},{5,6},{6,7},{7,4},{8,9},{9,10},{10,1... | collective-permute-start | bytes 1572872 | tf_op jit(solution)/shard_map/ppermute | solution.py:365
  82.9 26.9 %collective-permute-start.19 = (bf16[2,64,2048]{2,1,0:T(8,128)(2,1)S(1)}, bf16[2,64,2048]{2,1,0:T(8,128)(2,1)S(1)}, u32[]{:S(2)}, u32[]{:S(2)}) collective-permute-start(bf16[2,64,2048]{2,1,0:T(8,128)(2,1)S(1)} %bitcast.154), channel_id=1, source_target_pairs={{0,3},{1,0},{2,1},{3,2},{4,7},{5,4},{6,5},{7,6},{8,11},{9,8},{10,9... | collective-permute-start | bytes 1572872 | tf_op jit(solution)/shard_map/ppermute | solution.py:365
  87.1 22.7 %collective-permute-start.20 = (bf16[2,64,2048]{2,1,0:T(8,128)(2,1)S(1)}, bf16[2,64,2048]{2,1,0:T(8,128)(2,1)S(1)}, u32[]{:S(2)}, u32[]{:S(2)}) collective-permute-start(bf16[2,64,2048]{2,1,0:T(8,128)(2,1)S(1)} %bitcast.156), channel_id=1, source_target_pairs={{0,2},{1,3},{2,0},{3,1},{4,6},{5,7},{6,4},{7,5},{8,10},{9,11},{10,... | collective-permute-start | bytes 1572872 | tf_op jit(solution)/shard_map/ppermute | solution.py:365
  107.3 21.9 %collective-permute-start.31 = (bf16[4,256,128]{2,1,0:T(8,128)(2,1)S(1)}, bf16[4,256,128]{2,1,0:T(8,128)(2,1)S(1)}, u32[]{:S(2)}, u32[]{:S(2)}) collective-permute-start(bf16[4,256,128]{2,1,0:T(8,128)(2,1)S(1)} %get-tuple-element.45), channel_id=1, source_target_pairs={{0,48},{8,56},{16,0},{24,8},{32,16},{40,24},{48,32},{56,40},{64,11... | collective-permute-start | bytes 786440 | tf_op jit(solution)/shard_map/ppermute | solution.py:39
  110.2 6.5 %collective-permute-start.21 = (bf16[64,2048]{1,0:T(8,128)(2,1)S(1)}, bf16[64,2048]{1,0:T(8,128)(2,1)S(1)}, u32[]{:S(2)}, u32[]{:S(2)}) collective-permute-start(bf16[64,2048]{1,0:T(8,128)(2,1)S(1)} %fusion.50), channel_id=1, source_target_pairs={{0,4},{1,5},{2,6},{3,7},{4,0},{5,1},{6,2},{7,3},{8,12},{9,13},{10,... | collective-permute-start | bytes 786440 | tf_op jit(solution)/shard_map/ppermute | solution.py:370
  111.1 13.5 %copy-start.13 = (bf16[64,4096]{1,0:T(8,128)(2,1)S(1)}, bf16[64,4096]{1,0:T(8,128)(2,1)}, u32[]{:S(2)}) copy-start(bf16[64,4096]{1,0:T(8,128)(2,1)} %param.21) | copy-start | bytes 1572868
  111.7 8.4 %collective-permute-start.15 = (bf16[64,2048]{1,0:T(8,128)(2,1)S(1)}, bf16[64,2048]{1,0:T(8,128)(2,1)S(1)}, u32[]{:S(2)}, u32[]{:S(2)}) collective-permute-start(bf16[64,2048]{1,0:T(8,128)(2,1)S(1)} %get-tuple-element.20), channel_id=1, source_target_pairs={{0,1},{1,2},{2,3},{3,0},{4,5},{5,6},{6,7},{7,4},{8,9},{9,10},{10,1... | collective-permute-start | bytes 786440 | tf_op jit(solution)/shard_map/ppermute | solution.py:373
  111.7 11.5 %collective-permute-start.16 = (bf16[64,2048]{1,0:T(8,128)(2,1)S(1)}, bf16[64,2048]{1,0:T(8,128)(2,1)S(1)}, u32[]{:S(2)}, u32[]{:S(2)}) collective-permute-start(bf16[64,2048]{1,0:T(8,128)(2,1)S(1)} %get-tuple-element.22), channel_id=1, source_target_pairs={{0,3},{1,0},{2,1},{3,2},{4,7},{5,4},{6,5},{7,6},{8,11},{9,8},{10,9... | collective-permute-start | bytes 786440 | tf_op jit(solution)/shard_map/ppermute | solution.py:373
  116.7 9.5 %copy-start.14 = (bf16[2,256,128]{2,1,0:T(8,128)(2,1)S(1)}, bf16[2,256,128]{2,1,0:T(8,128)(2,1)}, u32[]{:S(2)}) copy-start(bf16[2,256,128]{2,1,0:T(8,128)(2,1)} %param.37) | copy-start | bytes 393220
  116.7 7.9 %collective-permute-start.17 = (bf16[64,2048]{1,0:T(8,128)(2,1)S(1)}, bf16[64,2048]{1,0:T(8,128)(2,1)S(1)}, u32[]{:S(2)}, u32[]{:S(2)}) collective-permute-start(bf16[64,2048]{1,0:T(8,128)(2,1)S(1)} %get-tuple-element.21), channel_id=1, source_target_pairs={{0,2},{1,3},{2,0},{3,1},{4,6},{5,7},{6,4},{7,5},{8,10},{9,11},{10,... | collective-permute-start | bytes 786440 | tf_op jit(solution)/shard_map/ppermute | solution.py:373
  125.2 8.1 %collective-permute-start.26 = (bf16[32,4096]{1,0:T(8,128)(2,1)S(1)}, bf16[32,4096]{1,0:T(8,128)(2,1)S(1)}, u32[]{:S(2)}, u32[]{:S(2)}) collective-permute-start(bf16[32,4096]{1,0:T(8,128)(2,1)S(1)} %get-tuple-element.37), channel_id=1, source_target_pairs={{0,4},{1,5},{2,6},{3,7},{4,0},{5,1},{6,2},{7,3},{8,12},{9,13},{10,... | collective-permute-start | bytes 786440 | tf_op jit(solution)/shard_map/ppermute | solution.py:390
  126.2 20.4 %collective-permute-start.32 = (bf16[4,256,128]{2,1,0:T(8,128)(2,1)S(1)}, bf16[4,256,128]{2,1,0:T(8,128)(2,1)S(1)}, u32[]{:S(2)}, u32[]{:S(2)}) collective-permute-start(bf16[4,256,128]{2,1,0:T(8,128)(2,1)S(1)} %get-tuple-element.45), channel_id=1, source_target_pairs={{0,32},{8,40},{16,48},{24,56},{32,0},{40,8},{48,16},{56,24},{64,96... | collective-permute-start | bytes 786440 | tf_op jit(solution)/shard_map/ppermute | solution.py:39
  128.7 18.0 %collective-permute-start.33 = (bf16[4,256,128]{2,1,0:T(8,128)(2,1)S(1)}, bf16[4,256,128]{2,1,0:T(8,128)(2,1)S(1)}, u32[]{:S(2)}, u32[]{:S(2)}) collective-permute-start(bf16[4,256,128]{2,1,0:T(8,128)(2,1)S(1)} %get-tuple-element.45), channel_id=1, source_target_pairs={{0,16},{8,24},{16,32},{24,40},{32,48},{40,56},{48,0},{56,8},{64,80... | collective-permute-start | bytes 786440 | tf_op jit(solution)/shard_map/ppermute | solution.py:39
  129.3 10.4 %collective-permute-start.22 = (bf16[32,4096]{1,0:T(8,128)(2,1)S(1)}, bf16[32,4096]{1,0:T(8,128)(2,1)S(1)}, u32[]{:S(2)}, u32[]{:S(2)}) collective-permute-start(bf16[32,4096]{1,0:T(8,128)(2,1)S(1)} %get-tuple-element.38), channel_id=1, source_target_pairs={{0,3},{1,0},{2,1},{3,2},{4,7},{5,4},{6,5},{7,6},{8,11},{9,8},{10,9... | collective-permute-start | bytes 786440 | tf_op jit(solution)/shard_map/ppermute | solution.py:389
  132.5 10.2 %collective-permute-start.23 = (bf16[32,4096]{1,0:T(8,128)(2,1)S(1)}, bf16[32,4096]{1,0:T(8,128)(2,1)S(1)}, u32[]{:S(2)}, u32[]{:S(2)}) collective-permute-start(bf16[32,4096]{1,0:T(8,128)(2,1)S(1)} %get-tuple-element.38), channel_id=1, source_target_pairs={{0,2},{1,3},{2,0},{3,1},{4,6},{5,7},{6,4},{7,5},{8,10},{9,11},{10,... | collective-permute-start | bytes 786440 | tf_op jit(solution)/shard_map/ppermute | solution.py:389
  133.4 10.1 %collective-permute-start.24 = (bf16[32,4096]{1,0:T(8,128)(2,1)S(1)}, bf16[32,4096]{1,0:T(8,128)(2,1)S(1)}, u32[]{:S(2)}, u32[]{:S(2)}) collective-permute-start(bf16[32,4096]{1,0:T(8,128)(2,1)S(1)} %get-tuple-element.38), channel_id=1, source_target_pairs={{0,1},{1,2},{2,3},{3,0},{4,5},{5,6},{6,7},{7,4},{8,9},{9,10},{10,1... | collective-permute-start | bytes 786440 | tf_op jit(solution)/shard_map/ppermute | solution.py:389
  139.7 9.7 %collective-permute-start.35 = (bf16[4,256,128]{2,1,0:T(8,128)(2,1)S(1)}, bf16[4,256,128]{2,1,0:T(8,128)(2,1)S(1)}, u32[]{:S(2)}, u32[]{:S(2)}) collective-permute-start(bf16[4,256,128]{2,1,0:T(8,128)(2,1)S(1)} %get-tuple-element.41), channel_id=1, source_target_pairs={{0,48},{8,56},{16,0},{24,8},{32,16},{40,24},{48,32},{56,40},{64,11... | collective-permute-start | bytes 786440 | tf_op jit(solution)/shard_map/ppermute | solution.py:39
  142.6 8.8 %collective-permute-start.36 = (bf16[4,256,128]{2,1,0:T(8,128)(2,1)S(1)}, bf16[4,256,128]{2,1,0:T(8,128)(2,1)S(1)}, u32[]{:S(2)}, u32[]{:S(2)}) collective-permute-start(bf16[4,256,128]{2,1,0:T(8,128)(2,1)S(1)} %get-tuple-element.41), channel_id=1, source_target_pairs={{0,32},{8,40},{16,48},{24,56},{32,0},{40,8},{48,16},{56,24},{64,96... | collective-permute-start | bytes 786440 | tf_op jit(solution)/shard_map/ppermute | solution.py:39
  143.4 20.1 %collective-permute-start.27 = (bf16[2,32,4096]{2,1,0:T(8,128)(2,1)S(1)}, bf16[2,32,4096]{2,1,0:T(8,128)(2,1)S(1)}, u32[]{:S(2)}, u32[]{:S(2)}) collective-permute-start(bf16[2,32,4096]{2,1,0:T(8,128)(2,1)S(1)} %get-tuple-element.40), channel_id=1, source_target_pairs={{0,3},{1,0},{2,1},{3,2},{4,7},{5,4},{6,5},{7,6},{8,11},{9,8},{10,9... | collective-permute-start | bytes 1572872 | tf_op jit(solution)/shard_map/ppermute | solution.py:395
  146.6 17.0 %collective-permute-start.28 = (bf16[2,32,4096]{2,1,0:T(8,128)(2,1)S(1)}, bf16[2,32,4096]{2,1,0:T(8,128)(2,1)S(1)}, u32[]{:S(2)}, u32[]{:S(2)}) collective-permute-start(bf16[2,32,4096]{2,1,0:T(8,128)(2,1)S(1)} %get-tuple-element.40), channel_id=1, source_target_pairs={{0,2},{1,3},{2,0},{3,1},{4,6},{5,7},{6,4},{7,5},{8,10},{9,11},{10,... | collective-permute-start | bytes 1572872 | tf_op jit(solution)/shard_map/ppermute | solution.py:395
  146.7 20.6 %collective-permute-start.29 = (bf16[2,32,4096]{2,1,0:T(8,128)(2,1)S(1)}, bf16[2,32,4096]{2,1,0:T(8,128)(2,1)S(1)}, u32[]{:S(2)}, u32[]{:S(2)}) collective-permute-start(bf16[2,32,4096]{2,1,0:T(8,128)(2,1)S(1)} %get-tuple-element.40), channel_id=1, source_target_pairs={{0,1},{1,2},{2,3},{3,0},{4,5},{5,6},{6,7},{7,4},{8,9},{9,10},{10,1... | collective-permute-start | bytes 1572872 | tf_op jit(solution)/shard_map/ppermute | solution.py:395
  149.3 19.1 %collective-permute-start.25 = (bf16[4,32,4096]{2,1,0:T(8,128)(2,1)S(1)}, bf16[4,32,4096]{2,1,0:T(8,128)(2,1)S(1)}, u32[]{:S(2)}, u32[]{:S(2)}) collective-permute-start(bf16[4,32,4096]{2,1,0:T(8,128)(2,1)S(1)} %get-tuple-element.19), channel_id=1, source_target_pairs={{0,4},{1,5},{2,6},{3,7},{4,0},{5,1},{6,2},{7,3},{8,12},{9,13},{10,... | collective-permute-start | bytes 3145736 | tf_op jit(solution)/shard_map/ppermute | solution.py:392
  151.4 7.6 %collective-permute-start.37 = (bf16[4,256,128]{2,1,0:T(8,128)(2,1)S(1)}, bf16[4,256,128]{2,1,0:T(8,128)(2,1)S(1)}, u32[]{:S(2)}, u32[]{:S(2)}) collective-permute-start(bf16[4,256,128]{2,1,0:T(8,128)(2,1)S(1)} %get-tuple-element.41), channel_id=1, source_target_pairs={{0,16},{8,24},{16,32},{24,40},{32,48},{40,56},{48,0},{56,8},{64,80... | collective-permute-start | bytes 786440 | tf_op jit(solution)/shard_map/ppermute | solution.py:39
  159.0 15.8 %collective-permute-start.38 = (bf16[16,256,128]{2,1,0:T(8,128)(2,1)S(1)}, bf16[16,256,128]{2,1,0:T(8,128)(2,1)S(1)}, u32[]{:S(2)}, u32[]{:S(2)}) collective-permute-start(bf16[16,256,128]{2,1,0:T(8,128)(2,1)S(1)} %constant_dynamic-update-slice_fusion.14.refs_4_), channel_id=1, source_target_pairs={{0,8},{8,0},{16,24},{24,16},{32,40},{40,32},{48,56},{56,48},{64,72... | collective-permute-start | bytes 3145736 | tf_op jit(solution)/shard_map/ppermute | solution.py:41
  163.6 11.3 %collective-permute-start.39 = (bf16[16,256,128]{2,1,0:T(8,128)(2,1)S(1)}, bf16[16,256,128]{2,1,0:T(8,128)(2,1)S(1)}, u32[]{:S(2)}, u32[]{:S(2)}) collective-permute-start(bf16[16,256,128]{2,1,0:T(8,128)(2,1)S(1)} %constant_dynamic-update-slice_fusion.21.refs_5_), channel_id=1, source_target_pairs={{0,8},{8,0},{16,24},{24,16},{32,40},{40,32},{48,56},{56,48},{64,72... | collective-permute-start | bytes 3145736 | tf_op jit(solution)/shard_map/ppermute | solution.py:41
  168.6 2.2 copy-start.16
  168.6 2.5 %copy-start.18 = (bf16[4096,128]{1,0:T(8,128)(2,1)S(1)}, bf16[4096,128]{1,0:T(8,128)(2,1)}, u32[]{:S(2)}) copy-start(bf16[4096,128]{1,0:T(8,128)(2,1)} %param.34) | copy-start | bytes 3145732
  168.6 2.8 %copy-start.19 = (bf16[4096,128]{1,0:T(8,128)(2,1)S(1)}, bf16[4096,128]{1,0:T(8,128)(2,1)}, u32[]{:S(2)}) copy-start(bf16[4096,128]{1,0:T(8,128)(2,1)} %param.33) | copy-start | bytes 3145732
  174.9 3.6 %copy-start.17 = (bf16[512,4096]{1,0:T(8,128)(2,1)S(1)}, bf16[512,4096]{1,0:T(8,128)(2,1)}, u32[]{:S(2)}) copy-start(bf16[512,4096]{1,0:T(8,128)(2,1)} %param.35) | copy-start | bytes 12582916
  179.2 27.3 %collective-permute-start.40 = (bf16[4,64,2048]{2,1,0:T(8,128)(2,1)S(1)}, bf16[4,64,2048]{2,1,0:T(8,128)(2,1)S(1)}, u32[]{:S(2)}, u32[]{:S(2)}) collective-permute-start(bf16[4,64,2048]{2,1,0:T(8,128)(2,1)S(1)} %bitcast.153), channel_id=1, source_target_pairs={{0,4},{1,5},{2,6},{3,7},{4,0},{5,1},{6,2},{7,3},{8,12},{9,13},{10,... | collective-permute-start | bytes 3145736 | tf_op jit(solution)/shard_map/ppermute | solution.py:363
  180.7 24.4 %collective-permute-start.44 = (bf16[2,64,2048]{2,1,0:T(8,128)(2,1)S(1)}, bf16[2,64,2048]{2,1,0:T(8,128)(2,1)S(1)}, u32[]{:S(2)}, u32[]{:S(2)}) collective-permute-start(bf16[2,64,2048]{2,1,0:T(8,128)(2,1)S(1)} %bitcast.157), channel_id=1, source_target_pairs={{0,1},{1,2},{2,3},{3,0},{4,5},{5,6},{6,7},{7,4},{8,9},{9,10},{10,1... | collective-permute-start | bytes 1572872 | tf_op jit(solution)/shard_map/ppermute | solution.py:365
  181.9 23.2 %collective-permute-start.45 = (bf16[2,64,2048]{2,1,0:T(8,128)(2,1)S(1)}, bf16[2,64,2048]{2,1,0:T(8,128)(2,1)S(1)}, u32[]{:S(2)}, u32[]{:S(2)}) collective-permute-start(bf16[2,64,2048]{2,1,0:T(8,128)(2,1)S(1)} %bitcast.158), channel_id=1, source_target_pairs={{0,3},{1,0},{2,1},{3,2},{4,7},{5,4},{6,5},{7,6},{8,11},{9,8},{10,9... | collective-permute-start | bytes 1572872 | tf_op jit(solution)/shard_map/ppermute | solution.py:365
  185.6 19.5 %collective-permute-start.46 = (bf16[2,64,2048]{2,1,0:T(8,128)(2,1)S(1)}, bf16[2,64,2048]{2,1,0:T(8,128)(2,1)S(1)}, u32[]{:S(2)}, u32[]{:S(2)}) collective-permute-start(bf16[2,64,2048]{2,1,0:T(8,128)(2,1)S(1)} %bitcast.159), channel_id=1, source_target_pairs={{0,2},{1,3},{2,0},{3,1},{4,6},{5,7},{6,4},{7,5},{8,10},{9,11},{10,... | collective-permute-start | bytes 1572872 | tf_op jit(solution)/shard_map/ppermute | solution.py:365
  205.5 6.6 %collective-permute-start.47 = (bf16[64,2048]{1,0:T(8,128)(2,1)S(1)}, bf16[64,2048]{1,0:T(8,128)(2,1)S(1)}, u32[]{:S(2)}, u32[]{:S(2)}) collective-permute-start(bf16[64,2048]{1,0:T(8,128)(2,1)S(1)} %fusion.51), channel_id=1, source_target_pairs={{0,4},{1,5},{2,6},{3,7},{4,0},{5,1},{6,2},{7,3},{8,12},{9,13},{10,... | collective-permute-start | bytes 786440 | tf_op jit(solution)/shard_map/ppermute | solution.py:370
  207.1 8.8 %collective-permute-start.41 = (bf16[64,2048]{1,0:T(8,128)(2,1)S(1)}, bf16[64,2048]{1,0:T(8,128)(2,1)S(1)}, u32[]{:S(2)}, u32[]{:S(2)}) collective-permute-start(bf16[64,2048]{1,0:T(8,128)(2,1)S(1)} %get-tuple-element.15), channel_id=1, source_target_pairs={{0,1},{1,2},{2,3},{3,0},{4,5},{5,6},{6,7},{7,4},{8,9},{9,10},{10,1... | collective-permute-start | bytes 786440 | tf_op jit(solution)/shard_map/ppermute | solution.py:373
  208.5 8.9 %collective-permute-start.42 = (bf16[64,2048]{1,0:T(8,128)(2,1)S(1)}, bf16[64,2048]{1,0:T(8,128)(2,1)S(1)}, u32[]{:S(2)}, u32[]{:S(2)}) collective-permute-start(bf16[64,2048]{1,0:T(8,128)(2,1)S(1)} %get-tuple-element.17), channel_id=1, source_target_pairs={{0,3},{1,0},{2,1},{3,2},{4,7},{5,4},{6,5},{7,6},{8,11},{9,8},{10,9... | collective-permute-start | bytes 786440 | tf_op jit(solution)/shard_map/ppermute | solution.py:373
  210.7 8.5 %collective-permute-start.43 = (bf16[64,2048]{1,0:T(8,128)(2,1)S(1)}, bf16[64,2048]{1,0:T(8,128)(2,1)S(1)}, u32[]{:S(2)}, u32[]{:S(2)}) collective-permute-start(bf16[64,2048]{1,0:T(8,128)(2,1)S(1)} %get-tuple-element.16), channel_id=1, source_target_pairs={{0,2},{1,3},{2,0},{3,1},{4,6},{5,7},{6,4},{7,5},{8,10},{9,11},{10,... | collective-permute-start | bytes 786440 | tf_op jit(solution)/shard_map/ppermute | solution.py:373
  (5 other events, 3.4 us)

commit v2 on v1

v2 whole, which is shorter than its diff:
```python
import functools
import math

import jax
import jax.numpy as jnp
from jax import lax
from jax.experimental import pallas as pl
from jax.experimental.pallas import tpu as pltpu
from jax.sharding import PartitionSpec as P

HEAD_SIZE = 128
NEW = 128
OWN = 64
EPSILON = 1e-06
LOG2E = math.log2(math.e)
MIB = 1 << 20


def y_swap():
    return [(y * 4 + z, (1 - y) * 4 + z) for y in range(2) for z in range(4)]


def z_shift(d):
    return [(y * 4 + z, y * 4 + (z + d) % 4) for y in range(2) for z in range(4)]


def sess_shift(far, x, core):
    return [
        (f * 8 + a * 2 + c, (f ^ far) * 8 + ((a + x) % 4) * 2 + (c ^ core))
        for f in range(2)
        for a in range(4)
        for c in range(2)
    ]


def from_y(value):
    half = value.shape[0] // 2
    direct, around = [], []
    for f in range(2):
        for low in range(8):
            for y in range(2):
                for z in range(4):
                    here = (f * 8 + low) * 8 + y * 4 + z
                    direct.append((here, (f * 8 + low) * 8 + (1 - y) * 4 + z))
                    around.append((here, ((1 - f) * 8 + low) * 8 + (1 - y) * 4 + z))
    return jnp.concatenate(
        [
            lax.ppermute(value[:half], ("sess", "exp"), direct),
            lax.ppermute(value[half:], ("sess", "exp"), around),
        ],
        axis=0,
    )


def copies_to_all(value, axis, count):
    return lax.all_to_all(
        jnp.broadcast_to(value[None], (count,) + value.shape), axis, 0, 0, tiled=True
    )


def session_of(g, meta):
    return ((meta[1] >> 2) ^ (g >> 1)) * 2 + (g & 1)


def slot_of(g, meta, prompts, slots):
    return slots[prompts[meta[0] * 4 + session_of(g, meta)]]


def place_of(g, meta, prompts, slots):
    slot = slot_of(g, meta, prompts, slots)
    holder = slot >> 1
    far = (holder >> 3) ^ (meta[0] >> 3)
    x = ((holder >> 1) - (meta[0] >> 1)) & 3
    return (x * 2 + far) * 2 + (slot & 1), (holder ^ meta[0]) & 1


def z_step(g, half, meta):
    return ((g & 1) * 2 + half - meta[1]) & 3


def cache_row_of(g, meta, prompts, slots):
    slot = slot_of(g, meta, prompts, slots)
    holder = slot >> 1
    far = (holder >> 3) ^ (meta[0] >> 3)
    return ((holder & 7) * 2 + far) * 2 + (slot & 1)


def row_of(g, meta, prompts, slots):
    return place_of(g, meta, prompts, slots)[0]


def side_of(g, meta, prompts, slots):
    return place_of(g, meta, prompts, slots)[1]


def conv_kernel(
    meta,
    prompts,
    slots,
    x_ref,
    prefix_ref,
    taps_ref,
    bias_ref,
    select_ref,
    out_ref,
    part_ref,
    series,
):
    new, channels = x_ref.shape
    rows = prefix_ref.shape[1]
    odd = (slot_of(pl.program_id(0), meta, prompts, slots) & 1) == 1
    for k in range(rows):
        pair = prefix_ref[0, k].astype(jnp.float32)
        series[8 - rows + k : 9 - rows + k] = jnp.where(odd, pair[1:2], pair[0:1])
    series[8:] = x_ref[...].astype(jnp.float32)
    total = jnp.broadcast_to(bias_ref[...], (new, channels))
    for k in range(taps_ref.shape[0]):
        total += taps_ref[k : k + 1] * series[8 - rows + k : 8 - rows + k + new]
    out = (total / (1.0 + jnp.exp(-total))).astype(jnp.bfloat16)
    out_ref[...] = out
    part_ref[...] = lax.dot_general(
        out, select_ref[...], (((1,), (1,)), ((), ())), preferred_element_type=jnp.float32
    ).astype(jnp.bfloat16)


def whole(a):
    return pl.BlockSpec(a.shape, lambda *_: (0,) * a.ndim)


def conv_project(scalars, x, prefixes, taps, bias, select):
    tokens, channels = x.shape
    width = select.shape[0]
    bias = bias.reshape(1, channels)

    def by_session(g, meta, prompts, slots):
        return session_of(g, meta), 0

    def by_holder(g, *refs):
        return slot_of(g, *refs) >> 1, 0, 0, 0

    return pl.pallas_call(
        conv_kernel,
        grid_spec=pltpu.PrefetchScalarGridSpec(
            num_scalar_prefetch=3,
            grid=(tokens // NEW,),
            in_specs=[
                pl.BlockSpec((NEW, channels), by_session),
                pl.BlockSpec((1,) + prefixes.shape[1:], by_holder),
                whole(taps),
                whole(bias),
                whole(select),
            ],
            out_specs=[
                pl.BlockSpec((NEW, channels), by_session),
                pl.BlockSpec((NEW, width), by_session),
            ],
            scratch_shapes=[pltpu.VMEM((NEW + 8, channels), jnp.float32)],
        ),
        out_shape=[
            jax.ShapeDtypeStruct((tokens, channels), jnp.bfloat16),
            jax.ShapeDtypeStruct((tokens, width), jnp.bfloat16),
        ],
        compiler_params=pltpu.CompilerParams(vmem_limit_bytes=60 * MIB),
        name="conv_project",
    )(*scalars, x, prefixes, taps, bias, select)


def scan_kernel(
    meta,
    prompts,
    slots,
    projected_ref,
    signal_ref,
    gate_ref,
    weight_ref,
    bias_ref,
    decay_ref,
    here_ref,
    there_ref,
    skip_ref,
    out_weight,
    part_a,
    part_b0,
    part_b1,
    part_b2,
    part_b3,
    rate_s,
    state_s,
    step_s,
    drive_s,
    emit_s,
    mix_s,
    gated_s,
    weight_s,
    sems,
    *,
    far,
):
    chunks = sems.shape[0]
    tile = out_weight.shape[1] // chunks

    def fetch(n):
        cols = pl.ds(n * tile, tile)
        return pltpu.make_async_copy(out_weight.at[:, cols], weight_s.at[:, cols], sems.at[n])

    g = pl.program_id(0) + 2 * far
    new, channels = signal_ref.shape
    states = decay_ref.shape[0]
    blocks = channels // 128
    rank = weight_ref.shape[0]
    half = new // 2

    @pl.when(pl.program_id(0) == 0)
    def _():
        for n in range(chunks):
            fetch(n).start()
        rate = jnp.exp(decay_ref[...]) * (-LOG2E)
        for b in range(blocks):
            rate_s[:, b, :] = rate[:, b * 128 : (b + 1) * 128]

    start = jnp.where(
        side_of(g, meta, prompts, slots) == 1,
        there_ref[0, :states].astype(jnp.float32),
        here_ref[0, :states].astype(jnp.float32),
    )
    for b in range(blocks):
        state_s[:, b, :] = start[:, b * 128 : (b + 1) * 128]
    projected = projected_ref[...]
    before = (
        jnp.dot(projected[:, :rank], weight_ref[...], preferred_element_type=jnp.float32)
        + bias_ref[...]
    )
    size = jnp.maximum(before, 0.0) + jnp.log1p(jnp.exp(-jnp.abs(before)))
    drive = size * signal_ref[...].astype(jnp.float32)
    for b in range(blocks):
        cols = slice(b * 128, (b + 1) * 128)
        step_s[:, b] = size[:, cols].reshape(new // 8, 8, 128)
        drive_s[:, b] = drive[:, cols].reshape(new // 8, 8, 128)
    mix = jnp.transpose(projected[:, rank:].astype(jnp.float32))
    for t in range(new):
        mix_s[t] = jnp.broadcast_to(mix[:, t : t + 1], (2 * states, 128))

    def advance(i, state):
        state = list(state)
        rates = [rate_s[n] for n in range(states)]
        for s in range(8):
            d = step_s[i, :, s, :]
            u = drive_s[i, :, s, :]
            t = i * 8 + s
            total = None
            for n in range(states):
                state[n] = jnp.exp2(d * rates[n]) * state[n] + u * mix_s[t, n : n + 1, :]
                term = state[n] * mix_s[t, states + n : states + n + 1, :]
                total = term if total is None else total + term
            emit_s[i, :, s, :] = total
        return tuple(state)

    lax.fori_loop(0, new // 8, advance, tuple(state_s[n] for n in range(states)))
    for b in range(blocks):
        cols = slice(b * 128, (b + 1) * 128)
        emitted = emit_s[:, b].reshape(new, 128)
        gate = gate_ref[:, cols].astype(jnp.float32)
        signal = signal_ref[:, cols].astype(jnp.float32)
        gated = (
            (emitted + skip_ref[:, cols] * signal) * (gate / (1.0 + jnp.exp(-gate)))
        ).astype(jnp.bfloat16)
        for k in range(2):
            gated_s[z_step(g, k, meta), :, cols] = gated[k * half : (k + 1) * half]

    @pl.when(pl.program_id(0) == pl.num_programs(0) - 1)
    def _():
        rows = gated_s[...].reshape(-1, channels)
        split = part_a.shape[-1]
        for n in range(chunks):
            fetch(n).wait()
            cols = slice(n * tile, (n + 1) * tile)
            out = jnp.dot(
                rows, weight_s[:, cols], preferred_element_type=jnp.float32
            ).astype(jnp.bfloat16)
            if n * tile < split:
                part_a[:, :, cols] = out.reshape(part_a.shape[0], half, tile)
            else:
                for d, ref in enumerate((part_b0, part_b1, part_b2, part_b3)):
                    ref[:, n * tile - split : (n + 1) * tile - split] = out[
                        d * half : (d + 1) * half
                    ]


def scan_gate(
    far, scalars, projected, signal, gate, weight, bias, decay, here, there, skip, out_weight
):
    tokens, channels = signal.shape
    states = decay.shape[0]
    blocks = channels // 128
    width = projected.shape[-1]
    features = out_weight.shape[1]
    split = features // 2
    bias = bias.reshape(1, channels)
    skip = skip.reshape(1, channels)

    def by_session(g, meta, prompts, slots):
        return session_of(g + 2 * far, meta), 0

    def by_row(g, *refs):
        return row_of(g + 2 * far, *refs), 0, 0

    return pl.pallas_call(
        functools.partial(scan_kernel, far=far),
        grid_spec=pltpu.PrefetchScalarGridSpec(
            num_scalar_prefetch=3,
            grid=(2,),
            in_specs=[
                pl.BlockSpec((NEW, width), by_session),
                pl.BlockSpec((NEW, channels), by_session),
                pl.BlockSpec((NEW, channels), by_session),
                whole(weight),
                whole(bias),
                whole(decay),
                pl.BlockSpec((1,) + here.shape[1:], by_row),
                pl.BlockSpec((1,) + here.shape[1:], by_row),
                whole(skip),
                pl.BlockSpec(memory_space=pltpu.HBM),
            ],
            out_specs=[pl.BlockSpec((4, OWN, split), lambda g, *_: (0, 0, 0))]
            + [pl.BlockSpec((OWN, features - split), lambda g, *_: (0, 0))] * 4,
            scratch_shapes=[
                pltpu.VMEM((states, blocks, 128), jnp.float32),
                pltpu.VMEM((states, blocks, 128), jnp.float32),
                pltpu.VMEM((NEW // 8, blocks, 8, 128), jnp.float32),
                pltpu.VMEM((NEW // 8, blocks, 8, 128), jnp.float32),
                pltpu.VMEM((NEW // 8, blocks, 8, 128), jnp.float32),
                pltpu.VMEM((NEW, 2 * states, 128), jnp.float32),
                pltpu.VMEM((4, OWN, channels), jnp.bfloat16),
                pltpu.VMEM((channels, features), jnp.bfloat16),
                pltpu.SemaphoreType.DMA((4,)),
            ],
        ),
        out_shape=[jax.ShapeDtypeStruct((4, OWN, split), jnp.bfloat16)]
        + [jax.ShapeDtypeStruct((OWN, features - split), jnp.bfloat16)] * 4,
        compiler_params=pltpu.CompilerParams(vmem_limit_bytes=60 * MIB),
        name="scan_far" if far else "scan_near",
    )(*scalars, projected, signal, gate, weight, bias, decay, here, there, skip, out_weight)


def pick_kernel(meta, prompts, slots, row_ref, out_ref):
    out_ref[...] = row_ref[...]


def pick_far(scalars, cached):
    shape = cached.shape[1:]
    return pl.pallas_call(
        pick_kernel,
        grid_spec=pltpu.PrefetchScalarGridSpec(
            num_scalar_prefetch=3,
            grid=(2,),
            in_specs=[
                pl.BlockSpec((1,) + shape, lambda g, *refs: (cache_row_of(g + 2, *refs), 0, 0))
            ],
            out_specs=pl.BlockSpec((1,) + shape, lambda g, *_: (g, 0, 0)),
        ),
        out_shape=jax.ShapeDtypeStruct((2,) + shape, cached.dtype),
        compiler_params=pltpu.CompilerParams(vmem_limit_bytes=60 * MIB),
        name="pick_far",
    )(*scalars, cached)


def serve_kernel(meta, prompts, slots, *refs):
    tokens, refs = refs[:8], refs[8:]
    (query, key, value, others, head, own_cache, far_cache), refs = refs[:7], refs[7:]
    outs, refs = refs[:4], refs[4:]
    (rows_s, weight_s, head_s, cache_s, total, heads_s, row_sem, weight_sem, cache_sem, head_sem) = refs
    features = rows_s.shape[1]
    side = features // 2
    depth = features // weight_sem.shape[0]
    lent = head.shape[0]
    widths = (query.shape[1], key.shape[1], value.shape[1])
    width = sum(widths)

    def token_copy(n):
        rows = pl.ds(n % 4 * OWN, OWN)
        return pltpu.make_async_copy(
            tokens[n], rows_s.at[rows, pl.ds(n // 4 * side, side)], row_sem.at[n]
        )

    def weight_copies(n):
        rows = pl.ds(n * depth, depth)
        copies, column = [], 0
        for k, (ref, size) in enumerate(zip((query, key, value), widths)):
            copies.append((ref.at[rows], column, size, k))
            column += size
        copies.append((others.at[rows, pl.ds(lent, width)], width, width, 3))
        return [
            pltpu.make_async_copy(
                source, weight_s.at[rows, pl.ds(at, size)], weight_sem.at[n, k]
            )
            for source, at, size, k in copies
        ]

    def cache_copies():
        return [
            pltpu.make_async_copy(
                own_cache.at[cache_row_of(g, meta, prompts, slots)], cache_s.at[0, g], cache_sem.at[0, g]
            )
            for g in range(2)
        ] + [
            pltpu.make_async_copy(far_cache.at[g], cache_s.at[1, g], cache_sem.at[1, g])
            for g in range(2)
        ]

    def head_copies(n):
        cols = pl.ds(n * lent, lent)
        return [
            pltpu.make_async_copy(head.at[:, cols], head_s.at[pl.ds(0, lent), cols], head_sem.at[0, n]),
            pltpu.make_async_copy(
                others.at[pl.ds(n * lent, lent), pl.ds(0, lent)],
                head_s.at[pl.ds(lent, lent), cols],
                head_sem.at[1, n],
            ),
        ]

    for n in range(8):
        token_copy(n).start()
    for n in range(features // depth):
        for copy in weight_copies(n):
            copy.start()
    for copy in cache_copies():
        copy.start()
    for n in range(features // lent):
        for copy in head_copies(n):
            copy.start()

    squares = None
    for n in range(features // depth):
        if n * depth % side == 0:
            for k in range(4):
                token_copy(n * depth // side * 4 + k).wait()
        for copy in weight_copies(n):
            copy.wait()
        rows = rows_s[:, n * depth : (n + 1) * depth]
        wide_rows = rows.astype(jnp.float32)
        wide_rows = wide_rows * wide_rows
        part = sum(wide_rows[:, b * 128 : (b + 1) * 128] for b in range(depth // 128))
        squares = part if squares is None else squares + part
        product = jnp.dot(
            rows, weight_s[n * depth : (n + 1) * depth], preferred_element_type=jnp.float32
        )
        if n == 0:
            total[...] = product
        else:
            total[...] += product
    scale = lax.rsqrt(jnp.sum(squares, axis=-1, keepdims=True) / features + EPSILON)

    for copy in cache_copies():
        copy.wait()
    new = 2 * OWN
    heads = widths[0] // HEAD_SIZE
    contract = (((1,), (1,)), ((), ()))
    shrink = 1.0 / math.sqrt(HEAD_SIZE)
    total[...] = total[...] * scale
    for g in range(2):
        steps = [pl.multiple_of(z_step(g, half, meta) * OWN, OWN) for half in range(2)]
        for side_of_y in range(2):
            cols = slice(side_of_y * width, (side_of_y + 1) * width)
            rows = jnp.concatenate(
                [total[pl.ds(at, OWN), cols] for at in steps], axis=0
            ).astype(jnp.bfloat16)
            old = cache_s[side_of_y, g]
            cached = old.shape[0] // 2
            old_keys, old_values = old[:cached], old[cached:]
            new_keys = rows[:, widths[0] : widths[0] + HEAD_SIZE]
            new_values = rows[:, widths[0] + HEAD_SIZE :]
            queries = jnp.concatenate(
                [rows[:, k * HEAD_SIZE : (k + 1) * HEAD_SIZE] for k in range(heads)], axis=0
            )
            before = (
                lax.dot_general(queries, old_keys, contract, preferred_element_type=jnp.float32)
                * shrink
            )
            fresh = (
                lax.dot_general(queries, new_keys, contract, preferred_element_type=jnp.float32)
                * shrink
            )
            at = lax.broadcasted_iota(jnp.int32, fresh.shape, 0) & (new - 1)
            fresh = jnp.where(lax.broadcasted_iota(jnp.int32, fresh.shape, 1) <= at, fresh, -1e30)
            top = jnp.maximum(
                jnp.max(before, axis=-1, keepdims=True), jnp.max(fresh, axis=-1, keepdims=True)
            )
            before = jnp.exp(before - top)
            fresh = jnp.exp(fresh - top)
            inverse = 1.0 / (
                jnp.sum(before, axis=-1, keepdims=True) + jnp.sum(fresh, axis=-1, keepdims=True)
            )
            attended = jnp.dot(
                (before * inverse).astype(jnp.bfloat16),
                old_values,
                preferred_element_type=jnp.float32,
            ) + jnp.dot(
                (fresh * inverse).astype(jnp.bfloat16),
                new_values,
                preferred_element_type=jnp.float32,
            )
            attended = attended.astype(jnp.bfloat16)
            for half in range(2):
                for k in range(heads):
                    column = side_of_y * widths[0] + k * HEAD_SIZE
                    heads_s[pl.ds(steps[half], OWN), column : column + HEAD_SIZE] = attended[
                        k * new + half * OWN : k * new + (half + 1) * OWN
                    ]

    for n in range(features // lent):
        for copy in head_copies(n):
            copy.wait()
        cols = slice(n * lent, (n + 1) * lent)
        out = jnp.dot(
            heads_s[...], head_s[:, cols], preferred_element_type=jnp.float32
        ).astype(jnp.bfloat16)
        for d, ref in enumerate(outs):
            ref[:, cols] = out[d * OWN : (d + 1) * OWN]


def serve(scalars, first, second, query, key, value, others, head, own_cache, far_cache):
    features = query.shape[0]
    width = query.shape[1] + key.shape[1] + value.shape[1]
    hbm = pl.BlockSpec(memory_space=pltpu.HBM)
    return pl.pallas_call(
        serve_kernel,
        grid_spec=pltpu.PrefetchScalarGridSpec(
            num_scalar_prefetch=3,
            grid=(1,),
            in_specs=[hbm] * 15,
            out_specs=[pl.BlockSpec((OWN, features), lambda *_: (0, 0))] * 4,
            scratch_shapes=[
                pltpu.VMEM((4 * OWN, features), jnp.bfloat16),
                pltpu.VMEM((features, 2 * width), jnp.bfloat16),
                pltpu.VMEM((2 * head.shape[0], features), jnp.bfloat16),
                pltpu.VMEM((2, 2) + own_cache.shape[1:], jnp.bfloat16),
                pltpu.VMEM((4 * OWN, 2 * width), jnp.float32),
                pltpu.VMEM((4 * OWN, 2 * query.shape[1]), jnp.bfloat16),
                pltpu.SemaphoreType.DMA((8,)),
                pltpu.SemaphoreType.DMA((4, 4)),
                pltpu.SemaphoreType.DMA((2, 2)),
                pltpu.SemaphoreType.DMA((2, features // head.shape[0])),
            ],
        ),
        out_shape=[jax.ShapeDtypeStruct((OWN, features), jnp.bfloat16)] * 4,
        compiler_params=pltpu.CompilerParams(vmem_limit_bytes=60 * MIB),
        name="serve",
    )(
        *scalars, *first, *second, query, key, value, others, head, own_cache, far_cache
    )


def after(value, *others):
    return lax.optimization_barrier((value,) + others)[0]


def wide(value):
    return value.astype(jnp.float32)


def send_far(part_a, *parts_b):
    got_b = [lax.ppermute(parts_b[d], "exp", z_shift(d)) for d in (1, 3, 2)]
    return lax.ppermute(part_a, "exp", y_swap()), parts_b[0], got_b


def finish(near, got_a, own_b, got_b):
    own_a, *parts_b = near
    near_b = [lax.ppermute(parts_b[d], "exp", z_shift(d)) for d in (1, 3, 2)]
    far_b = (wide(own_b) + sum(wide(v) for v in got_b)).astype(jnp.bfloat16)
    later_b = lax.ppermute(after(far_b, got_a), "exp", y_swap())
    sums_a = wide(own_a) + wide(got_a)
    rest_a = after(sums_a.astype(jnp.bfloat16), near_b[0], near_b[1], near_b[2])
    later_a = [lax.ppermute(rest_a[d], "exp", z_shift(d)) for d in (1, 3, 2)]
    sum_b = wide(parts_b[0]) + sum(wide(v) for v in near_b) + wide(later_b)
    sum_a = sums_a[0] + sum(wide(v) for v in later_a)
    return sum_a, sum_b


def z_gather(value):
    got = [value] + [None] * 3
    for d in (1, 3, 2):
        got[d] = lax.ppermute(value, "exp", z_shift(-d))
    return got


def shards(
    residual,
    mamba_input,
    mamba_gate,
    filter_taps,
    filter_bias,
    input_select,
    step_weight,
    step_bias,
    decay_log,
    skip_scale,
    output_weight,
    query_weight,
    key_matrix,
    value_matrix,
    head_weight,
    cache_keys,
    stored_cache_values,
    cache_state,
    cache_filter,
    prompt_slot,
    session_prompt,
):
    meta = jnp.stack([lax.axis_index("sess"), lax.axis_index("exp")]).astype(jnp.int32)
    scalars = (meta, session_prompt, prompt_slot)
    by_tap = jnp.swapaxes(cache_filter, 0, 1)
    copies = jnp.broadcast_to(by_tap[None], (16,) + by_tap.shape)
    prefixes = lax.all_to_all(copies, "sess", 0, 0, tiled=True)
    start = after(cache_state.astype(jnp.bfloat16), prefixes)
    start_far = lax.ppermute(start, "sess", sess_shift(1, 0, 0))
    groups = [list(range(8)), list(range(8, 16))]
    cached = jnp.concatenate([cache_keys, stored_cache_values], axis=1)
    cached = after(cached, prefixes)
    cached_far = lax.ppermute(cached, "sess", sess_shift(1, 0, 0))
    signal, part = conv_project(
        scalars,
        mamba_input,
        prefixes,
        filter_taps,
        filter_bias,
        input_select.T,
    )
    start_pair = jnp.concatenate(
        [start, after(start_far, part)], axis=0
    )
    start_here = jnp.concatenate(
        [start_pair] + [lax.ppermute(start_pair, "sess", sess_shift(0, -d, 0)) for d in (1, 2, 3)],
        axis=0,
    )
    start_there = lax.ppermute(start_here, "sess", sess_shift(0, 0, 1))
    cached = lax.all_gather(
        jnp.concatenate([cached, after(cached_far, part)], axis=0),
        "sess",
        axis=0,
        tiled=True,
        axis_index_groups=groups,
    )
    pieces = lax.all_to_all(part.reshape(8, OWN, -1), "exp", 0, 0, tiled=True)
    own = jnp.sum(wide(pieces), axis=0).astype(jnp.bfloat16)
    projected = copies_to_all(own, "exp", 8).reshape(8 * OWN, -1)
    eighth = lax.axis_index("sess") % 8
    share = query_weight.shape[0] // 8
    lent = jnp.concatenate(
        [lax.dynamic_slice_in_dim(head_weight, eighth * share, share, 1)]
        + [
            lax.dynamic_slice_in_dim(w, eighth * share, share, 0)
            for w in (query_weight, key_matrix, value_matrix)
        ],
        axis=1,
    )
    lent = from_y(after(lent, projected))

    def scan(far, projected):
        return scan_gate(
            far,
            scalars,
            projected,
            signal,
            mamba_gate,
            step_weight,
            step_bias,
            decay_log,
            start_here,
            start_there,
            skip_scale,
            output_weight,
        )

    far = scan(1, projected)
    others = lax.all_gather(
        after(lent, cached, far[0]), "sess", axis=0, tiled=True, axis_index_groups=groups
    )
    sent = send_far(*far)
    near = scan(0, after(projected, *far))
    sum_a, sum_b = finish(near, *sent)
    split = residual.shape[1] // 2
    after_a = wide(residual[:, :split]) + sum_a
    after_b = wide(residual[:, split:]) + sum_b
    far_cache = lax.ppermute(after(pick_far(scalars, cached), sum_b), "exp", y_swap())
    tokens_b = z_gather(after_b.astype(jnp.bfloat16))
    tokens_a = z_gather(after_a.astype(jnp.bfloat16))
    products = serve(
        scalars,
        tokens_a,
        tokens_b,
        query_weight,
        key_matrix,
        value_matrix,
        others,
        head_weight,
        cached,
        far_cache,
    )
    got = [lax.ppermute(products[d], "exp", z_shift(d)) for d in (1, 3, 2)]
    head_total = sum(wide(v) for v in [products[0]] + got)
    return (jnp.concatenate([after_a, after_b], axis=1) + head_total).astype(jnp.bfloat16)


def solution(mesh):
    return jax.shard_map(
        shards,
        mesh=mesh,
        in_specs=(
            P(("sess", "exp"), None),
            P("sess", "exp"),
            P("sess", "exp"),
            P(None, "exp"),
            P("exp"),
            P("exp", None),
            P(None, "exp"),
            P("exp"),
            P(None, "exp"),
            P("exp"),
            P("exp", None),
            P(None, "exp"),
            P(None, "exp"),
            P(None, "exp"),
            P("exp", None),
            P("sess", None, "exp"),
            P("sess", None, "exp"),
            P("sess", None, "exp"),
            P("sess", None, "exp"),
            P(),
            P(),
        ),
        out_specs=P(("sess", "exp"), None),
        check_vma=False,
    )
```

time: 221 us -> 220 us (level)
  Pallas kernels: 24.6 us -> 54.7 us
  waiting for transfers between devices: 92.9 us -> 74.7 us
  between operations: 0.66 us -> 13.7 us
  matrix products: 12.3 us -> 0 us
  starting transfers between devices: 66.3 us -> 55.4 us
  local copies, waits for them, and re-layouts: 16.4 us -> 10.2 us
  other arithmetic: 7.22 us -> 9.43 us
    ppermute x48 -> x29, waiting for transfers between devices: 90.7 us -> 61.8 us  [the longest x3 22.2 us: shards(): got = [lax.ppermute(products[d], 'exp', z_shift(d)) for d in (1, 3, 2)]]
    pallas_call x2 -> x4, Pallas kernels: 21.2 us -> 48.9 us  [the longest x2 29.2 us: scan_gate(): pl.pallas_call(functools.partial(scan_kernel, far=far), grid_spec=pltpu.P...]
    ppermute x48 -> x29, starting transfers between devices: 60 us -> 37.3 us  [the longest x6 10 us: z_gather(): got[d] = lax.ppermute(value, 'exp', z_shift(-d))]
    all_to_all x0 -> x2, waiting for transfers between devices: none -> 12.9 us  [the longest x1 7.56 us: shards(): prefixes = lax.all_to_all(copies, 'sess', 0, 0, tiled=True)]
    all_to_all x0 -> x2, starting transfers between devices: none -> 12.6 us  [the longest x1 7.12 us: shards(): prefixes = lax.all_to_all(copies, 'sess', 0, 0, tiled=True)]
    dot_general x13 -> x0, matrix products: 12.3 us -> none  [the longest x12 8.82 us: times(): jnp.dot(rows.reshape(-1, depth), w, preferred_element_type=jnp.float32)]
    unnamed x53 -> x41, local copies, waits for them, and re-layouts: 13.8 us -> 4 us
    concatenate x1 -> x4, other arithmetic: 0.67 us -> 4.23 us  [the longest x1 2.28 us: from_y(): jnp.concatenate([lax.ppermute(value[:half], ('sess', 'exp'), direct), lax...]
  transfers between devices with their start and end apart: 49 -> 34, of which waited for: 24 -> 20; matrix products, arithmetic and copies ran while one was open for 11% -> 6% of each run, Pallas kernels for 10% -> 17%
where the time goes in v2:
time: 220 us; the launch traced here: 218 us
  waiting for transfers between devices  74.7 us (34%)
  starting transfers between devices  55.4 us (25%)
  Pallas kernels  54.7 us (25%)
  between operations  13.7 us (6%)
  local copies, waits for them, and re-layouts  10.2 us (5%)
  other arithmetic  9.43 us (4%)
    pallas_call x2, Pallas kernels, scan_gate(): pl.pallas_call(functools.partial(scan_kernel, far=far), grid_spec=pltpu.P...  29.2 us
    ppermute x3, waiting for transfers between devices, shards(): got = [lax.ppermute(products[d], 'exp', z_shift(d)) for d in (1, 3, 2)]  22.2 us
    pallas_call x1, Pallas kernels, serve(): pl.pallas_call(serve_kernel, grid_spec=pltpu.PrefetchScalarGridSpec(num_s...  17.4 us
    ppermute x6, waiting for transfers between devices, z_gather(): got[d] = lax.ppermute(value, 'exp', z_shift(-d))  12.4 us
    ppermute x6, starting transfers between devices, z_gather(): got[d] = lax.ppermute(value, 'exp', z_shift(-d))  10 us
    ppermute x3, waiting for transfers between devices, finish(): later_a = [lax.ppermute(rest_a[d], 'exp', z_shift(d)) for d in (1, 3, 2)]  8.92 us
    ppermute x3, waiting for transfers between devices, finish(): near_b = [lax.ppermute(parts_b[d], 'exp', z_shift(d)) for d in (1, 3, 2)]  8.85 us
    all_to_all x1, waiting for transfers between devices, shards(): prefixes = lax.all_to_all(copies, 'sess', 0, 0, tiled=True)  7.56 us
  transfers between devices with their start and end apart: 34, of which 20 were waited for; matrix products, arithmetic and copies ran while one was open for 6% of the time, Pallas kernels for 17%

profile of v2, /device:TPU:0, one launch (start us, length us, event | category | flops | bytes accessed | tf_op | source)
XLA Modules:
  0.0 218.2 jit_solution(12533030226504844559)
XLA Ops:
  6.5 1.5 broadcast_in_dim.4
  8.0 7.1 %all-to-all-start = ((bf16[16,3,2,1024]{3,2,1,0:T(2,128)(2,1)}), bf16[16,3,2,1024]{3,2,1,0:T(2,128)(2,1)S(1)}, u32[]{:S(2)}, u32[]{:S(2)}) async-start(bf16[16,3,2,1024]{3,2,1,0:T(2,128)(2,1)} %broadcast_in_dim.4), calls=%async_computation | async-start | bytes 393216 | tf_op jit(solution)/shard_map/all_to_all | solution.py:613
  15.2 1.0 pad_maximum_fusion.3
  16.2 7.6 %all-to-all-done.prefix_ref = bf16[16,3,2,1024]{3,2,1,0:T(2,128)(2,1)S(1)} async-done(((bf16[16,3,2,1024]{3,2,1,0:T(2,128)(2,1)}), bf16[16,3,2,1024]{3,2,1,0:T(2,128)(2,1)S(1)}, u32[]{:S(2)}, u32[]{:S(2)}) %all-to-all-start) | async-done | bytes 196640 | tf_op jit(solution)/shard_map/all_to_all | solution.py:613
  24.9 5.8 %conv_project.1 = (bf16[512,1024]{1,0:T(8,128)(2,1)}, bf16[512,288]{1,0:T(8,128)(2,1)}) custom-call(s32[2]{0:T(128)} %pad_add_fusion.meta, s32[64]{0:T(128)} %prompts.9, s32[32]{0:T(128)} %slots.9, bf16[512,1024]{1,0:T(8,128)(2,1)} %x_ref.1, bf16[16,3,2,1024]{3,2,1,0:T(2,128)(2,1)} %copy-done.5, f32[4,1024]{1,0:T(4,128)} %taps_ref.1, f32[1,1024]{1,0:T(1,128)} %bitcast.30, ...), custom_call_target="tpu_custom_call" | custom-call | tf_op jit(solution)/shard_map/conv_project/pallas_call | solution.py:141
  30.7 2.7 %collective-permute-done.24 = bf16[2,512,128]{2,1,0:T(8,128)(2,1)S(1)} collective-permute-done((bf16[2,512,128]{2,1,0:T(8,128)(2,1)S(1)}, bf16[2,512,128]{2,1,0:T(8,128)(2,1)S(1)}, u32[]{:S(2)}, u32[]{:S(2)}) %collective-permute-start.24) | collective-permute-done | bytes 262176 | tf_op jit(solution)/shard_map/ppermute | solution.py:619
  33.4 0.8 pad_maximum_fusion.2
  34.3 1.3 constant_dynamic-slice_fusion.2
  35.6 5.4 %all-to-all-start.1 = ((bf16[8,64,288]{2,1,0:T(8,128)(2,1)}), bf16[8,64,288]{2,1,0:T(8,128)(2,1)S(1)}, u32[]{:S(2)}, u32[]{:S(2)}) async-start(bf16[8,64,288]{2,1,0:T(8,128)(2,1)} %bitcast.5), calls=%async_computation.1 | async-start | bytes 786432 | tf_op jit(solution)/shard_map/all_to_all | solution.py:643
  41.0 1.0 constant_dynamic-slice_fusion
  42.1 1.5 collective-permute-start
  43.6 0.6 constant_dynamic-update-slice_fusion.1
  44.2 4.1 %collective-permute-done = bf16[2,16,1024]{2,1,0:T(8,128)(2,1)S(1)} collective-permute-done((bf16[2,16,1024]{2,1,0:T(8,128)(2,1)S(1)}, bf16[2,16,1024]{2,1,0:T(8,128)(2,1)S(1)}, u32[]{:S(2)}, u32[]{:S(2)}) %collective-permute-start) | collective-permute-done | bytes 65568 | tf_op jit(solution)/shard_map/ppermute | solution.py:615
  48.3 0.6 constant_dynamic-update-slice_fusion
  49.0 1.2 collective-permute-start.1
  50.3 0.8 broadcast_in_dim.5
  51.0 5.5 %all-to-all-start.2 = ((bf16[8,64,288]{2,1,0:T(8,128)(2,1)}), bf16[8,64,288]{2,1,0:T(8,128)(2,1)S(1)}, u32[]{:S(2)}, u32[]{:S(2)}) async-start(bf16[8,64,288]{2,1,0:T(8,128)(2,1)} %broadcast_in_dim.5), calls=%async_computation.2 | async-start | bytes 786432 | tf_op jit(solution)/shard_map/all_to_all | solution.py:56
  56.7 1.3 collective-permute-start.2
  58.1 0.9 constant_dynamic-update-slice_fusion.4
  59.0 5.3 %all-to-all-done.2 = bf16[8,64,288]{2,1,0:T(8,128)(2,1)S(1)} async-done(((bf16[8,64,288]{2,1,0:T(8,128)(2,1)}), bf16[8,64,288]{2,1,0:T(8,128)(2,1)S(1)}, u32[]{:S(2)}, u32[]{:S(2)}) %all-to-all-start.2) | async-done | bytes 294944 | tf_op jit(solution)/shard_map/all_to_all | solution.py:56
  64.4 2.3 %collective-permute-start.23 = (bf16[256,1280]{1,0:T(8,128)(2,1)S(1)}, bf16[256,1280]{1,0:T(8,128)(2,1)S(1)}, u32[]{:S(2)}, u32[]{:S(2)}) collective-permute-start(bf16[256,1280]{1,0:T(8,128)(2,1)S(1)} %get-tuple-element.65), channel_id=1, source_target_pairs={{0,68},{1,69},{2,70},{3,71},{4,64},{5,65},{6,66},{7,67},{8,76},{9,... | collective-permute-start | bytes 1966088 | tf_op jit(solution)/shard_map/ppermute | solution.py:49
  67.3 0.9 constant_dynamic-update-slice_fusion.3
  68.3 0.6 collective-permute-done.3
  68.9 0.9 constant_dynamic-update-slice_fusion.2.here_ref
  69.9 1.9 collective-permute-done.4.there_ref
  71.8 0.8 copy-done.2
  72.6 14.4 %scan_far.1 = (bf16[4,64,2048]{2,1,0:T(8,128)(2,1)}, bf16[64,2048]{1,0:T(8,128)(2,1)}, bf16[64,2048]{1,0:T(8,128)(2,1)}, bf16[64,2048]{1,0:T(8,128)(2,1)}, bf16[64,2048]{1,0:T(8,128)(2,1)}) custom-call(s32[2]{0:T(128)} %pad_add_fusion.meta, s32[64]{0:T(128)} %prompts.9, s32[32]{0:T(128)} %slots.9, bf16[512,288]{1,0:T(8,128)(2,1)} %bitcast.22, ...), custom_call_target="tpu_custom_call" | custom-call | tf_op jit(solution)/shard_map/scan_far/pallas_call | solution.py:307
  87.1 2.3 %pad_maximum_fusion.1 = bf16[512,1280]{1,0:T(8,128)(2,1)} fusion(bf16[256,1280]{1,0:T(8,128)(2,1)S(1)} %collective-permute-done.23, bf16[256,1280]{1,0:T(8,128)(2,1)} %collective-permute-done.22), kind=kLoop, calls=%fused_computation.2 | loop fusion | flops 2621440 | bytes 2621440 | tf_op jit(solution)/shard_map/concatenate | solution.py:46
  89.4 1.6 collective-permute-start.5
  91.0 3.1 %collective-permute-start.14 = (bf16[64,2048]{1,0:T(8,128)(2,1)}, bf16[64,2048]{1,0:T(8,128)(2,1)S(1)}, u32[]{:S(2)}, u32[]{:S(2)}) collective-permute-start(bf16[64,2048]{1,0:T(8,128)(2,1)} %get-tuple-element.38), channel_id=1, source_target_pairs={{0,2},{1,3},{2,0},{3,1},{4,6},{5,7},{6,4},{7,5},{8,10},{9,11},{10,... | collective-permute-start | bytes 786440 | tf_op jit(solution)/shard_map/ppermute | solution.py:562
  94.1 1.1 collective-permute-start.13
  95.2 0.9 collective-permute-start.12
  96.1 14.7 %scan_near.1 = (bf16[4,64,2048]{2,1,0:T(8,128)(2,1)}, bf16[64,2048]{1,0:T(8,128)(2,1)}, bf16[64,2048]{1,0:T(8,128)(2,1)}, bf16[64,2048]{1,0:T(8,128)(2,1)}, bf16[64,2048]{1,0:T(8,128)(2,1)}) custom-call(s32[2]{0:T(128)} %pad_add_fusion.meta, s32[64]{0:T(128)} %prompts.9, s32[32]{0:T(128)} %slots.9, bf16[512,288]{1,0:T(8,128)(2,1)} %bitcast.23, ...), custom_call_target="tpu_custom_call" | custom-call | tf_op jit(solution)/shard_map/scan_near/pallas_call | solution.py:307
  110.9 0.6 collective-permute-start.6
  111.5 2.7 %collective-permute-start.7 = (bf16[64,2048]{1,0:T(8,128)(2,1)}, bf16[64,2048]{1,0:T(8,128)(2,1)S(1)}, u32[]{:S(2)}, u32[]{:S(2)}) collective-permute-start(bf16[64,2048]{1,0:T(8,128)(2,1)} %get-tuple-element.43), channel_id=1, source_target_pairs={{0,3},{1,0},{2,1},{3,2},{4,7},{5,4},{6,5},{7,6},{8,11},{9,8},{10,9... | collective-permute-start | bytes 786440 | tf_op jit(solution)/shard_map/ppermute | solution.py:568
  115.0 1.8 convert_add_fusion
  116.8 4.4 %collective-permute-done.6 = bf16[64,2048]{1,0:T(8,128)(2,1)S(1)} collective-permute-done((bf16[64,2048]{1,0:T(8,128)(2,1)}, bf16[64,2048]{1,0:T(8,128)(2,1)S(1)}, u32[]{:S(2)}, u32[]{:S(2)}) %collective-permute-start.6) | collective-permute-done | bytes 262176 | tf_op jit(solution)/shard_map/ppermute | solution.py:568
  121.2 3.4 %collective-permute-done.7 = bf16[64,2048]{1,0:T(8,128)(2,1)S(1)} collective-permute-done((bf16[64,2048]{1,0:T(8,128)(2,1)}, bf16[64,2048]{1,0:T(8,128)(2,1)S(1)}, u32[]{:S(2)}, u32[]{:S(2)}) %collective-permute-start.7) | collective-permute-done | bytes 262176 | tf_op jit(solution)/shard_map/ppermute | solution.py:568
  124.5 1.1 collective-permute-done.8
  126.2 3.4 %collective-permute-start.10 = (bf16[64,2048]{1,0:T(8,128)(2,1)S(1)}, bf16[64,2048]{1,0:T(8,128)(2,1)S(1)}, u32[]{:S(2)}, u32[]{:S(2)}) collective-permute-start(bf16[64,2048]{1,0:T(8,128)(2,1)S(1)} %get-tuple-element.68), channel_id=1, source_target_pairs={{0,3},{1,0},{2,1},{3,2},{4,7},{5,4},{6,5},{7,6},{8,11},{9,8},{10,9... | collective-permute-start | bytes 786440 | tf_op jit(solution)/shard_map/ppermute | solution.py:573
  130.1 6.1 %collective-permute-done.11 = bf16[64,2048]{1,0:T(8,128)(2,1)S(1)} collective-permute-done((bf16[64,2048]{1,0:T(8,128)(2,1)S(1)}, bf16[64,2048]{1,0:T(8,128)(2,1)S(1)}, u32[]{:S(2)}, u32[]{:S(2)}) %collective-permute-start.11) | collective-permute-done | bytes 262176 | tf_op jit(solution)/shard_map/ppermute | solution.py:573
  136.3 1.2 collective-permute-done.10
  137.5 1.5 collective-permute-done.9
  139.5 1.2 collective-permute-start.16
  140.7 1.1 collective-permute-start.17
  141.9 0.8 collective-permute-start.18
  142.7 2.4 %collective-permute-start.19 = (bf16[64,2048]{1,0:T(8,128)(2,1)S(1)}, bf16[64,2048]{1,0:T(8,128)(2,1)S(1)}, u32[]{:S(2)}, u32[]{:S(2)}) collective-permute-start(bf16[64,2048]{1,0:T(8,128)(2,1)S(1)} %get-tuple-element.69.refs_4_), channel_id=1, source_target_pairs={{0,3},{1,0},{2,1},{3,2},{4,7},{5,4},{6,5},{7,6},{8,11},{9,8},{10,9... | collective-permute-start | bytes 786440 | tf_op jit(solution)/shard_map/ppermute | solution.py:582
  145.1 1.2 collective-permute-start.20
  146.3 2.4 %pick_far.1 = bf16[2,512,128]{2,1,0:T(8,128)(2,1)} custom-call(s32[2]{0:T(128)} %pad_add_fusion.meta, s32[64]{0:T(128)} %prompts.9, s32[32]{0:T(128)} %slots.9, bf16[32,512,128]{2,1,0:T(8,128)(2,1)} %all-gather.3.cloned.1.call-done.row_ref.refs_13_), custom_call_target="tpu_custom_call" | custom-call | tf_op jit(solution)/shard_map/pick_far/pallas_call | solution.py:351
  148.6 2.0 collective-permute-done.16.refs_1_
  150.6 3.3 %collective-permute-start.21 = (bf16[64,2048]{1,0:T(8,128)(2,1)S(1)}, bf16[64,2048]{1,0:T(8,128)(2,1)S(1)}, u32[]{:S(2)}, u32[]{:S(2)}) collective-permute-start(bf16[64,2048]{1,0:T(8,128)(2,1)S(1)} %get-tuple-element.69.refs_4_), channel_id=1, source_target_pairs={{0,1},{1,2},{2,3},{3,0},{4,5},{5,6},{6,7},{7,4},{8,9},{9,10},{10,1... | collective-permute-start | bytes 786440 | tf_op jit(solution)/shard_map/ppermute | solution.py:582
  153.9 0.6 collective-permute-start.25
  154.6 3.4 %collective-permute-done.18.refs_3_ = bf16[64,2048]{1,0:T(8,128)(2,1)S(1)} collective-permute-done((bf16[64,2048]{1,0:T(8,128)(2,1)S(1)}, bf16[64,2048]{1,0:T(8,128)(2,1)S(1)}, u32[]{:S(2)}, u32[]{:S(2)}) %collective-permute-start.18) | collective-permute-done | bytes 262176 | tf_op jit(solution)/shard_map/ppermute | solution.py:582
  158.0 2.0 collective-permute-done.19.refs_5_
  160.0 2.2 %collective-permute-done.20.refs_6_ = bf16[64,2048]{1,0:T(8,128)(2,1)S(1)} collective-permute-done((bf16[64,2048]{1,0:T(8,128)(2,1)S(1)}, bf16[64,2048]{1,0:T(8,128)(2,1)S(1)}, u32[]{:S(2)}, u32[]{:S(2)}) %collective-permute-start.20) | collective-permute-done | bytes 262176 | tf_op jit(solution)/shard_map/ppermute | solution.py:582
  162.3 2.7 %collective-permute-done.21.refs_7_ = bf16[64,2048]{1,0:T(8,128)(2,1)S(1)} collective-permute-done((bf16[64,2048]{1,0:T(8,128)(2,1)S(1)}, bf16[64,2048]{1,0:T(8,128)(2,1)S(1)}, u32[]{:S(2)}, u32[]{:S(2)}) %collective-permute-start.21) | collective-permute-done | bytes 262176 | tf_op jit(solution)/shard_map/ppermute | solution.py:582
  165.8 17.4 %serve.1 = (bf16[64,4096]{1,0:T(8,128)(2,1)}, bf16[64,4096]{1,0:T(8,128)(2,1)}, bf16[64,4096]{1,0:T(8,128)(2,1)}, bf16[64,4096]{1,0:T(8,128)(2,1)}) custom-call(s32[2]{0:T(128)} %pad_add_fusion.meta, s32[64]{0:T(128)} %prompts.9, s32[32]{0:T(128)} %slots.9, bf16[64,2048]{1,0:T(8,128)(2,1)} %copy-done.3, bf16[64,2048]{1,0:T(8,128)(2,1)} %copy-done.7, ...), custom_call_target="tpu_custom_call" | custom-call | tf_op jit(solution)/shard_map/serve/pallas_call | solution.py:525
  183.2 1.8 collective-permute-start.28
  185.0 1.2 collective-permute-start.27
  186.3 0.8 collective-permute-start.26
  187.1 12.9 %collective-permute-done.28 = bf16[64,4096]{1,0:T(8,128)(2,1)S(1)} collective-permute-done((bf16[64,4096]{1,0:T(8,128)(2,1)}, bf16[64,4096]{1,0:T(8,128)(2,1)S(1)}, u32[]{:S(2)}, u32[]{:S(2)}) %collective-permute-start.28) | collective-permute-done | bytes 524320 | tf_op jit(solution)/shard_map/ppermute | solution.py:699
  199.9 6.2 %collective-permute-done.27 = bf16[64,4096]{1,0:T(8,128)(2,1)S(1)} collective-permute-done((bf16[64,4096]{1,0:T(8,128)(2,1)}, bf16[64,4096]{1,0:T(8,128)(2,1)S(1)}, u32[]{:S(2)}, u32[]{:S(2)}) %collective-permute-start.27) | collective-permute-done | bytes 524320 | tf_op jit(solution)/shard_map/ppermute | solution.py:699
  206.2 3.1 %collective-permute-done.26 = bf16[64,4096]{1,0:T(8,128)(2,1)S(1)} collective-permute-done((bf16[64,4096]{1,0:T(8,128)(2,1)}, bf16[64,4096]{1,0:T(8,128)(2,1)S(1)}, u32[]{:S(2)}, u32[]{:S(2)}) %collective-permute-start.26) | collective-permute-done | bytes 524320 | tf_op jit(solution)/shard_map/ppermute | solution.py:699
  209.2 2.2 fusion
  (71 shorter events, 5.4 us)
Async XLA Ops:
  8.0 15.7 %all-to-all-start = ((bf16[16,3,2,1024]{3,2,1,0:T(2,128)(2,1)}), bf16[16,3,2,1024]{3,2,1,0:T(2,128)(2,1)S(1)}, u32[]{:S(2)}, u32[]{:S(2)}) async-start(bf16[16,3,2,1024]{3,2,1,0:T(2,128)(2,1)} %broadcast_in_dim.4), calls=%async_computation | async-start | bytes 393216 | tf_op jit(solution)/shard_map/all_to_all | solution.py:613
  15.1 74.2 %all-gather.3.cloned.1.call-start = ((), (), s32[]{:S(2)}) async-start(), calls=%async_computation.3 | async-start | bytes 4718592 | tf_op jit(solution)/shard_map/all_gather | solution.py:636
  23.8 1.2 copy-start.5
  23.8 9.7 %collective-permute-start.24 = (bf16[2,512,128]{2,1,0:T(8,128)(2,1)S(1)}, bf16[2,512,128]{2,1,0:T(8,128)(2,1)S(1)}, u32[]{:S(2)}, u32[]{:S(2)}) collective-permute-start(bf16[2,512,128]{2,1,0:T(8,128)(2,1)S(1)} %pad_maximum_fusion.3), channel_id=1, source_target_pairs={{0,64},{8,72},{16,80},{24,88},{32,96},{40,104},{48,112},{56,120},{... | collective-permute-start | bytes 786440 | tf_op jit(solution)/shard_map/ppermute | solution.py:619
  30.7 11.3 %copy-start.16 = (f32[2,16,1024]{2,1,0:T(8,128)S(1)}, f32[2,16,1024]{2,1,0:T(8,128)}, u32[]{:S(2)}) copy-start(f32[2,16,1024]{2,1,0:T(8,128)} %param.38) | copy-start | bytes 393220
  35.6 14.6 %all-to-all-start.1 = ((bf16[8,64,288]{2,1,0:T(8,128)(2,1)}), bf16[8,64,288]{2,1,0:T(8,128)(2,1)S(1)}, u32[]{:S(2)}, u32[]{:S(2)}) async-start(bf16[8,64,288]{2,1,0:T(8,128)(2,1)} %bitcast.5), calls=%async_computation.1 | async-start | bytes 786432 | tf_op jit(solution)/shard_map/all_to_all | solution.py:643
  42.1 6.2 %collective-permute-start = (bf16[2,16,1024]{2,1,0:T(8,128)(2,1)S(1)}, bf16[2,16,1024]{2,1,0:T(8,128)(2,1)S(1)}, u32[]{:S(2)}, u32[]{:S(2)}) collective-permute-start(bf16[2,16,1024]{2,1,0:T(8,128)(2,1)S(1)} %convert_element_type.81), channel_id=1, source_target_pairs={{0,64},{8,72},{16,80},{24,88},{32,96},{40,104},{48,112},{56,120},{... | collective-permute-start | bytes 196616 | tf_op jit(solution)/shard_map/ppermute | solution.py:615
  49.0 9.1 %collective-permute-start.1 = (bf16[4,16,1024]{2,1,0:T(8,128)(2,1)}, bf16[4,16,1024]{2,1,0:T(8,128)(2,1)}, u32[]{:S(2)}, u32[]{:S(2)}) collective-permute-start(bf16[4,16,1024]{2,1,0:T(8,128)(2,1)} %get-tuple-element.72), channel_id=1, source_target_pairs={{0,48},{8,56},{16,0},{24,8},{32,16},{40,24},{48,32},{56,40},{64,11... | collective-permute-start | bytes 393224 | tf_op jit(solution)/shard_map/ppermute | solution.py:632
  51.0 13.2 %all-to-all-start.2 = ((bf16[8,64,288]{2,1,0:T(8,128)(2,1)}), bf16[8,64,288]{2,1,0:T(8,128)(2,1)S(1)}, u32[]{:S(2)}, u32[]{:S(2)}) async-start(bf16[8,64,288]{2,1,0:T(8,128)(2,1)} %broadcast_in_dim.5), calls=%async_computation.2 | async-start | bytes 786432 | tf_op jit(solution)/shard_map/all_to_all | solution.py:56
  56.5 108.5 %all-gather.5.cloned.1.call-start = ((), (), s32[]{:S(2)}) async-start(), calls=%async_computation.4 | async-start | bytes 11796480 | tf_op jit(solution)/shard_map/all_gather | solution.py:675
  56.7 10.7 %collective-permute-start.2 = (bf16[4,16,1024]{2,1,0:T(8,128)(2,1)}, bf16[4,16,1024]{2,1,0:T(8,128)(2,1)}, u32[]{:S(2)}, u32[]{:S(2)}) collective-permute-start(bf16[4,16,1024]{2,1,0:T(8,128)(2,1)} %get-tuple-element.72), channel_id=1, source_target_pairs={{0,32},{8,40},{16,48},{24,56},{32,0},{40,8},{48,16},{56,24},{64,96... | collective-permute-start | bytes 393224 | tf_op jit(solution)/shard_map/ppermute | solution.py:632
  58.0 10.9 %collective-permute-start.3 = (bf16[4,16,1024]{2,1,0:T(8,128)(2,1)}, bf16[4,16,1024]{2,1,0:T(8,128)(2,1)}, u32[]{:S(2)}, u32[]{:S(2)}) collective-permute-start(bf16[4,16,1024]{2,1,0:T(8,128)(2,1)} %get-tuple-element.72), channel_id=1, source_target_pairs={{0,16},{8,24},{16,32},{24,40},{32,48},{40,56},{48,0},{56,8},{64,80... | collective-permute-start | bytes 393224 | tf_op jit(solution)/shard_map/ppermute | solution.py:632
  64.3 7.5 %copy-start = (bf16[8,64,288]{2,1,0:T(8,128)(2,1)}, bf16[8,64,288]{2,1,0:T(8,128)(2,1)S(1)}, u32[]{:S(2)}) copy-start(bf16[8,64,288]{2,1,0:T(8,128)(2,1)S(1)} %all-to-all-done.2) | copy-start | bytes 884740
  64.4 22.7 %collective-permute-start.23 = (bf16[256,1280]{1,0:T(8,128)(2,1)S(1)}, bf16[256,1280]{1,0:T(8,128)(2,1)S(1)}, u32[]{:S(2)}, u32[]{:S(2)}) collective-permute-start(bf16[256,1280]{1,0:T(8,128)(2,1)S(1)} %get-tuple-element.65), channel_id=1, source_target_pairs={{0,68},{1,69},{2,70},{3,71},{4,64},{5,65},{6,66},{7,67},{8,76},{9,... | collective-permute-start | bytes 1966088 | tf_op jit(solution)/shard_map/ppermute | solution.py:49
  66.7 20.4 %collective-permute-start.22 = (bf16[256,1280]{1,0:T(8,128)(2,1)S(1)}, bf16[256,1280]{1,0:T(8,128)(2,1)}, u32[]{:S(2)}, u32[]{:S(2)}) collective-permute-start(bf16[256,1280]{1,0:T(8,128)(2,1)S(1)} %get-tuple-element.64), channel_id=1, source_target_pairs={{0,4},{1,5},{2,6},{3,7},{4,0},{5,1},{6,2},{7,3},{8,12},{9,13},{10,... | collective-permute-start | bytes 1966088 | tf_op jit(solution)/shard_map/ppermute | solution.py:48
  69.8 2.0 copy-start.1
  69.8 2.0 collective-permute-start.4
  71.8 0.8 copy-start.2
  87.0 7.1 %copy-start.18 = (bf16[64,2048]{1,0:T(8,128)(2,1)S(1)}, bf16[64,2048]{1,0:T(8,128)(2,1)}, u32[]{:S(2)}) copy-start(bf16[64,2048]{1,0:T(8,128)(2,1)} %get-tuple-element.39) | copy-start | bytes 786436
  87.1 8.2 %copy-start.17 = (bf16[64,2048]{1,0:T(8,128)(2,1)S(1)}, bf16[64,2048]{1,0:T(8,128)(2,1)}, u32[]{:S(2)}) copy-start(bf16[64,2048]{1,0:T(8,128)(2,1)} %get-tuple-element.37) | copy-start | bytes 786436
  89.4 25.6 %collective-permute-start.5 = (bf16[4,64,2048]{2,1,0:T(8,128)(2,1)}, bf16[4,64,2048]{2,1,0:T(8,128)(2,1)S(1)}, u32[]{:S(2)}, u32[]{:S(2)}) collective-permute-start(bf16[4,64,2048]{2,1,0:T(8,128)(2,1)} %get-tuple-element.35), channel_id=1, source_target_pairs={{0,4},{1,5},{2,6},{3,7},{4,0},{5,1},{6,2},{7,3},{8,12},{9,13},{10,... | collective-permute-start | bytes 3145736 | tf_op jit(solution)/shard_map/ppermute | solution.py:563
  91.0 20.5 %collective-permute-start.14 = (bf16[64,2048]{1,0:T(8,128)(2,1)}, bf16[64,2048]{1,0:T(8,128)(2,1)S(1)}, u32[]{:S(2)}, u32[]{:S(2)}) collective-permute-start(bf16[64,2048]{1,0:T(8,128)(2,1)} %get-tuple-element.38), channel_id=1, source_target_pairs={{0,2},{1,3},{2,0},{3,1},{4,6},{5,7},{6,4},{7,5},{8,10},{9,11},{10,... | collective-permute-start | bytes 786440 | tf_op jit(solution)/shard_map/ppermute | solution.py:562
  94.1 20.1 %collective-permute-start.13 = (bf16[64,2048]{1,0:T(8,128)(2,1)S(1)}, bf16[64,2048]{1,0:T(8,128)(2,1)S(1)}, u32[]{:S(2)}, u32[]{:S(2)}) collective-permute-start(bf16[64,2048]{1,0:T(8,128)(2,1)S(1)} %copy-done.18), channel_id=1, source_target_pairs={{0,3},{1,0},{2,1},{3,2},{4,7},{5,4},{6,5},{7,6},{8,11},{9,8},{10,9... | collective-permute-start | bytes 786440 | tf_op jit(solution)/shard_map/ppermute | solution.py:562
  95.2 19.6 %collective-permute-start.12 = (bf16[64,2048]{1,0:T(8,128)(2,1)S(1)}, bf16[64,2048]{1,0:T(8,128)(2,1)S(1)}, u32[]{:S(2)}, u32[]{:S(2)}) collective-permute-start(bf16[64,2048]{1,0:T(8,128)(2,1)S(1)} %copy-done.17), channel_id=1, source_target_pairs={{0,1},{1,2},{2,3},{3,0},{4,5},{5,6},{6,7},{7,4},{8,9},{9,10},{10,1... | collective-permute-start | bytes 786440 | tf_op jit(solution)/shard_map/ppermute | solution.py:562
  96.1 18.7 %copy-start.15 = (bf16[64,2048]{1,0:T(8,128)(2,1)S(1)}, bf16[64,2048]{1,0:T(8,128)(2,1)}, u32[]{:S(2)}) copy-start(bf16[64,2048]{1,0:T(8,128)(2,1)} %get-tuple-element.36) | copy-start | bytes 786436
  110.9 10.3 %collective-permute-start.6 = (bf16[64,2048]{1,0:T(8,128)(2,1)}, bf16[64,2048]{1,0:T(8,128)(2,1)S(1)}, u32[]{:S(2)}, u32[]{:S(2)}) collective-permute-start(bf16[64,2048]{1,0:T(8,128)(2,1)} %get-tuple-element.42), channel_id=1, source_target_pairs={{0,1},{1,2},{2,3},{3,0},{4,5},{5,6},{6,7},{7,4},{8,9},{9,10},{10,1... | collective-permute-start | bytes 786440 | tf_op jit(solution)/shard_map/ppermute | solution.py:568
  111.5 13.0 %collective-permute-start.7 = (bf16[64,2048]{1,0:T(8,128)(2,1)}, bf16[64,2048]{1,0:T(8,128)(2,1)S(1)}, u32[]{:S(2)}, u32[]{:S(2)}) collective-permute-start(bf16[64,2048]{1,0:T(8,128)(2,1)} %get-tuple-element.43), channel_id=1, source_target_pairs={{0,3},{1,0},{2,1},{3,2},{4,7},{5,4},{6,5},{7,6},{8,11},{9,8},{10,9... | collective-permute-start | bytes 786440 | tf_op jit(solution)/shard_map/ppermute | solution.py:568
  114.2 11.4 %collective-permute-start.8 = (bf16[64,2048]{1,0:T(8,128)(2,1)}, bf16[64,2048]{1,0:T(8,128)(2,1)S(1)}, u32[]{:S(2)}, u32[]{:S(2)}) collective-permute-start(bf16[64,2048]{1,0:T(8,128)(2,1)} %get-tuple-element.44), channel_id=1, source_target_pairs={{0,2},{1,3},{2,0},{3,1},{4,6},{5,7},{6,4},{7,5},{8,10},{9,11},{10,... | collective-permute-start | bytes 786440 | tf_op jit(solution)/shard_map/ppermute | solution.py:568
  115.0 24.1 %copy-start.6 = (bf16[64,4096]{1,0:T(8,128)(2,1)S(1)}, bf16[64,4096]{1,0:T(8,128)(2,1)}, u32[]{:S(2)}) copy-start(bf16[64,4096]{1,0:T(8,128)(2,1)} %param.21) | copy-start | bytes 1572868
  115.0 24.1 %copy-start.14 = (bf16[64,2048]{1,0:T(8,128)(2,1)S(1)}, bf16[64,2048]{1,0:T(8,128)(2,1)}, u32[]{:S(2)}) copy-start(bf16[64,2048]{1,0:T(8,128)(2,1)} %get-tuple-element.46) | copy-start | bytes 786436
  125.7 10.6 %collective-permute-start.11 = (bf16[64,2048]{1,0:T(8,128)(2,1)S(1)}, bf16[64,2048]{1,0:T(8,128)(2,1)S(1)}, u32[]{:S(2)}, u32[]{:S(2)}) collective-permute-start(bf16[64,2048]{1,0:T(8,128)(2,1)S(1)} %get-tuple-element.67), channel_id=1, source_target_pairs={{0,2},{1,3},{2,0},{3,1},{4,6},{5,7},{6,4},{7,5},{8,10},{9,11},{10,... | collective-permute-start | bytes 786440 | tf_op jit(solution)/shard_map/ppermute | solution.py:573
  126.2 11.3 %collective-permute-start.10 = (bf16[64,2048]{1,0:T(8,128)(2,1)S(1)}, bf16[64,2048]{1,0:T(8,128)(2,1)S(1)}, u32[]{:S(2)}, u32[]{:S(2)}) collective-permute-start(bf16[64,2048]{1,0:T(8,128)(2,1)S(1)} %get-tuple-element.68), channel_id=1, source_target_pairs={{0,3},{1,0},{2,1},{3,2},{4,7},{5,4},{6,5},{7,6},{8,11},{9,8},{10,9... | collective-permute-start | bytes 786440 | tf_op jit(solution)/shard_map/ppermute | solution.py:573
  129.6 9.5 %collective-permute-start.9 = (bf16[64,2048]{1,0:T(8,128)(2,1)S(1)}, bf16[64,2048]{1,0:T(8,128)(2,1)S(1)}, u32[]{:S(2)}, u32[]{:S(2)}) collective-permute-start(bf16[64,2048]{1,0:T(8,128)(2,1)S(1)} %get-tuple-element.66), channel_id=1, source_target_pairs={{0,1},{1,2},{2,3},{3,0},{4,5},{5,6},{6,7},{7,4},{8,9},{9,10},{10,1... | collective-permute-start | bytes 786440 | tf_op jit(solution)/shard_map/ppermute | solution.py:573
  129.6 9.5 %collective-permute-start.15 = (bf16[64,2048]{1,0:T(8,128)(2,1)S(1)}, bf16[64,2048]{1,0:T(8,128)(2,1)S(1)}, u32[]{:S(2)}, u32[]{:S(2)}) collective-permute-start(bf16[64,2048]{1,0:T(8,128)(2,1)S(1)} %add_convert_fusion), channel_id=1, source_target_pairs={{0,4},{1,5},{2,6},{3,7},{4,0},{5,1},{6,2},{7,3},{8,12},{9,13},{10,... | collective-permute-start | bytes 786440 | tf_op jit(solution)/shard_map/ppermute | solution.py:570
  139.5 25.5 %copy-start.3 = (bf16[64,2048]{1,0:T(8,128)(2,1)}, bf16[64,2048]{1,0:T(8,128)(2,1)S(1)}, u32[]{:S(2)}) copy-start(bf16[64,2048]{1,0:T(8,128)(2,1)S(1)} %get-tuple-element.60.refs_0_) | copy-start | bytes 786436
  139.5 25.5 %copy-start.4 = (bf16[64,2048]{1,0:T(8,128)(2,1)}, bf16[64,2048]{1,0:T(8,128)(2,1)S(1)}, u32[]{:S(2)}) copy-start(bf16[64,2048]{1,0:T(8,128)(2,1)S(1)} %get-tuple-element.69.refs_4_) | copy-start | bytes 786436
  139.5 11.1 %collective-permute-start.16 = (bf16[64,2048]{1,0:T(8,128)(2,1)S(1)}, bf16[64,2048]{1,0:T(8,128)(2,1)S(1)}, u32[]{:S(2)}, u32[]{:S(2)}) collective-permute-start(bf16[64,2048]{1,0:T(8,128)(2,1)S(1)} %get-tuple-element.60.refs_0_), channel_id=1, source_target_pairs={{0,3},{1,0},{2,1},{3,2},{4,7},{5,4},{6,5},{7,6},{8,11},{9,8},{10,9... | collective-permute-start | bytes 786440 | tf_op jit(solution)/shard_map/ppermute | solution.py:582
  140.7 13.2 %collective-permute-start.17 = (bf16[64,2048]{1,0:T(8,128)(2,1)S(1)}, bf16[64,2048]{1,0:T(8,128)(2,1)S(1)}, u32[]{:S(2)}, u32[]{:S(2)}) collective-permute-start(bf16[64,2048]{1,0:T(8,128)(2,1)S(1)} %get-tuple-element.60.refs_0_), channel_id=1, source_target_pairs={{0,2},{1,3},{2,0},{3,1},{4,6},{5,7},{6,4},{7,5},{8,10},{9,11},{10,... | collective-permute-start | bytes 786440 | tf_op jit(solution)/shard_map/ppermute | solution.py:582
  141.9 16.1 %collective-permute-start.18 = (bf16[64,2048]{1,0:T(8,128)(2,1)S(1)}, bf16[64,2048]{1,0:T(8,128)(2,1)S(1)}, u32[]{:S(2)}, u32[]{:S(2)}) collective-permute-start(bf16[64,2048]{1,0:T(8,128)(2,1)S(1)} %get-tuple-element.60.refs_0_), channel_id=1, source_target_pairs={{0,1},{1,2},{2,3},{3,0},{4,5},{5,6},{6,7},{7,4},{8,9},{9,10},{10,1... | collective-permute-start | bytes 786440 | tf_op jit(solution)/shard_map/ppermute | solution.py:582
  142.7 17.3 %collective-permute-start.19 = (bf16[64,2048]{1,0:T(8,128)(2,1)S(1)}, bf16[64,2048]{1,0:T(8,128)(2,1)S(1)}, u32[]{:S(2)}, u32[]{:S(2)}) collective-permute-start(bf16[64,2048]{1,0:T(8,128)(2,1)S(1)} %get-tuple-element.69.refs_4_), channel_id=1, source_target_pairs={{0,3},{1,0},{2,1},{3,2},{4,7},{5,4},{6,5},{7,6},{8,11},{9,8},{10,9... | collective-permute-start | bytes 786440 | tf_op jit(solution)/shard_map/ppermute | solution.py:582
  145.1 17.2 %collective-permute-start.20 = (bf16[64,2048]{1,0:T(8,128)(2,1)S(1)}, bf16[64,2048]{1,0:T(8,128)(2,1)S(1)}, u32[]{:S(2)}, u32[]{:S(2)}) collective-permute-start(bf16[64,2048]{1,0:T(8,128)(2,1)S(1)} %get-tuple-element.69.refs_4_), channel_id=1, source_target_pairs={{0,2},{1,3},{2,0},{3,1},{4,6},{5,7},{6,4},{7,5},{8,10},{9,11},{10,... | collective-permute-start | bytes 786440 | tf_op jit(solution)/shard_map/ppermute | solution.py:582
  150.6 14.4 %copy-start.7 = (bf16[64,2048]{1,0:T(8,128)(2,1)}, bf16[64,2048]{1,0:T(8,128)(2,1)S(1)}, u32[]{:S(2)}) copy-start(bf16[64,2048]{1,0:T(8,128)(2,1)S(1)} %collective-permute-done.16.refs_1_) | copy-start | bytes 786436
  150.6 14.4 %collective-permute-start.21 = (bf16[64,2048]{1,0:T(8,128)(2,1)S(1)}, bf16[64,2048]{1,0:T(8,128)(2,1)S(1)}, u32[]{:S(2)}, u32[]{:S(2)}) collective-permute-start(bf16[64,2048]{1,0:T(8,128)(2,1)S(1)} %get-tuple-element.69.refs_4_), channel_id=1, source_target_pairs={{0,1},{1,2},{2,3},{3,0},{4,5},{5,6},{6,7},{7,4},{8,9},{9,10},{10,1... | collective-permute-start | bytes 786440 | tf_op jit(solution)/shard_map/ppermute | solution.py:582
  153.9 11.2 %copy-start.8 = (bf16[64,2048]{1,0:T(8,128)(2,1)}, bf16[64,2048]{1,0:T(8,128)(2,1)S(1)}, u32[]{:S(2)}) copy-start(bf16[64,2048]{1,0:T(8,128)(2,1)S(1)} %collective-permute-done.17.refs_2_) | copy-start | bytes 786436
  153.9 11.1 %collective-permute-start.25 = (bf16[2,512,128]{2,1,0:T(8,128)(2,1)}, bf16[2,512,128]{2,1,0:T(8,128)(2,1)S(1)}, u32[]{:S(2)}, u32[]{:S(2)}) collective-permute-start(bf16[2,512,128]{2,1,0:T(8,128)(2,1)} %pick_far.1), channel_id=1, source_target_pairs={{0,4},{1,5},{2,6},{3,7},{4,0},{5,1},{6,2},{7,3},{8,12},{9,13},{10,... | collective-permute-start | bytes 786440 | tf_op jit(solution)/shard_map/ppermute | solution.py:684
  158.0 7.1 %copy-start.9 = (bf16[64,2048]{1,0:T(8,128)(2,1)}, bf16[64,2048]{1,0:T(8,128)(2,1)S(1)}, u32[]{:S(2)}) copy-start(bf16[64,2048]{1,0:T(8,128)(2,1)S(1)} %collective-permute-done.18.refs_3_) | copy-start | bytes 786436
  160.0 5.1 %copy-start.10 = (bf16[64,2048]{1,0:T(8,128)(2,1)}, bf16[64,2048]{1,0:T(8,128)(2,1)S(1)}, u32[]{:S(2)}) copy-start(bf16[64,2048]{1,0:T(8,128)(2,1)S(1)} %collective-permute-done.19.refs_5_) | copy-start | bytes 786436
  162.3 2.8 %copy-start.11 = (bf16[64,2048]{1,0:T(8,128)(2,1)}, bf16[64,2048]{1,0:T(8,128)(2,1)S(1)}, u32[]{:S(2)}) copy-start(bf16[64,2048]{1,0:T(8,128)(2,1)S(1)} %collective-permute-done.20.refs_6_) | copy-start | bytes 786436
  165.0 0.7 copy-start.12
  165.0 0.8 copy-start.13
  183.2 16.7 %collective-permute-start.28 = (bf16[64,4096]{1,0:T(8,128)(2,1)}, bf16[64,4096]{1,0:T(8,128)(2,1)S(1)}, u32[]{:S(2)}, u32[]{:S(2)}) collective-permute-start(bf16[64,4096]{1,0:T(8,128)(2,1)} %get-tuple-element.56), channel_id=1, source_target_pairs={{0,2},{1,3},{2,0},{3,1},{4,6},{5,7},{6,4},{7,5},{8,10},{9,11},{10,... | collective-permute-start | bytes 1572872 | tf_op jit(solution)/shard_map/ppermute | solution.py:699
  185.0 21.1 %collective-permute-start.27 = (bf16[64,4096]{1,0:T(8,128)(2,1)}, bf16[64,4096]{1,0:T(8,128)(2,1)S(1)}, u32[]{:S(2)}, u32[]{:S(2)}) collective-permute-start(bf16[64,4096]{1,0:T(8,128)(2,1)} %get-tuple-element.55), channel_id=1, source_target_pairs={{0,3},{1,0},{2,1},{3,2},{4,7},{5,4},{6,5},{7,6},{8,11},{9,8},{10,9... | collective-permute-start | bytes 1572872 | tf_op jit(solution)/shard_map/ppermute | solution.py:699
  186.3 23.0 %collective-permute-start.26 = (bf16[64,4096]{1,0:T(8,128)(2,1)}, bf16[64,4096]{1,0:T(8,128)(2,1)S(1)}, u32[]{:S(2)}, u32[]{:S(2)}) collective-permute-start(bf16[64,4096]{1,0:T(8,128)(2,1)} %get-tuple-element.54), channel_id=1, source_target_pairs={{0,1},{1,2},{2,3},{3,0},{4,5},{5,6},{6,7},{7,4},{8,9},{9,10},{10,1... | collective-permute-start | bytes 1572872 | tf_op jit(solution)/shard_map/ppermute | solution.py:699
Sparse Core Ops, SparseCore 0:
  34.4 35.7 all-gather.2
  89.5 57.6 all-gather.4

commit v3 on v2

v3 whole, which is shorter than its diff:
```python
import functools
import math

import jax
import jax.numpy as jnp
from jax import lax
from jax.experimental import pallas as pl
from jax.experimental.pallas import tpu as pltpu
from jax.sharding import PartitionSpec as P

HEAD_SIZE = 128
NEW = 128
OWN = 64
EPSILON = 1e-06
LOG2E = math.log2(math.e)
MIB = 1 << 20


def y_swap():
    return [(y * 4 + z, (1 - y) * 4 + z) for y in range(2) for z in range(4)]


def z_shift(d):
    return [(y * 4 + z, y * 4 + (z + d) % 4) for y in range(2) for z in range(4)]


def sess_shift(far, x, core):
    return [
        (f * 8 + a * 2 + c, (f ^ far) * 8 + ((a + x) % 4) * 2 + (c ^ core))
        for f in range(2)
        for a in range(4)
        for c in range(2)
    ]


def around():
    return [
        ((f * 8 + low) * 8 + y * 4 + z, ((1 - f) * 8 + low) * 8 + (1 - y) * 4 + z)
        for f in range(2)
        for low in range(8)
        for y in range(2)
        for z in range(4)
    ]


def copies_to_all(value, axis, count):
    return lax.all_to_all(
        jnp.broadcast_to(value[None], (count,) + value.shape), axis, 0, 0, tiled=True
    )


def session_of(g, meta):
    return ((meta[1] >> 2) ^ (g >> 1)) * 2 + (g & 1)


def slot_of(g, meta, prompts, slots):
    return slots[prompts[meta[0] * 4 + session_of(g, meta)]]


def place_of(g, meta, prompts, slots):
    slot = slot_of(g, meta, prompts, slots)
    holder = slot >> 1
    far = (holder >> 3) ^ (meta[0] >> 3)
    x = ((holder >> 1) - (meta[0] >> 1)) & 3
    return (x * 2 + far) * 2 + (slot & 1), (holder ^ meta[0]) & 1


def z_step(g, half, meta):
    return ((g & 1) * 2 + half - meta[1]) & 3


def cache_row_of(g, meta, prompts, slots):
    slot = slot_of(g, meta, prompts, slots)
    holder = slot >> 1
    far = (holder >> 3) ^ (meta[0] >> 3)
    return ((holder & 7) * 2 + far) * 2 + (slot & 1)


def row_of(g, meta, prompts, slots):
    return place_of(g, meta, prompts, slots)[0]


def side_of(g, meta, prompts, slots):
    return place_of(g, meta, prompts, slots)[1]


def in_smem():
    return pl.BlockSpec(memory_space=pltpu.SMEM)


def in_vmem():
    return pl.BlockSpec(memory_space=pltpu.VMEM)


def silu(value):
    return 0.5 * value * (1.0 + jnp.tanh(0.5 * value))


def in_any():
    return pl.BlockSpec(memory_space=pl.ANY)


def filtered(series, taps, bias, first, count):
    total = jnp.broadcast_to(bias, (count, series.shape[1]))
    for k in range(taps.shape[0]):
        total += taps[k : k + 1] * series[first + k : first + k + count]
    return silu(total).astype(jnp.bfloat16)


def times_select(out, select):
    return lax.dot_general(
        out, select, (((1,), (1,)), ((), ())), preferred_element_type=jnp.float32
    ).astype(jnp.bfloat16)


def conv_kernel(
    x_any, taps_any, bias_any, select_any, out_ref, part_ref, series, x_s, taps_s, bias_s, select_s, sems
):
    sessions = x_s.shape[0]
    shared = [
        pltpu.make_async_copy(source, target, sems.at[n])
        for n, (source, target) in enumerate(
            ((taps_any, taps_s), (bias_any, bias_s), (select_any, select_s))
        )
    ]
    own = [
        pltpu.make_async_copy(x_any.at[pl.ds(g * NEW, NEW)], x_s.at[g], sems.at[3 + g])
        for g in range(sessions)
    ]
    for copy in shared + own:
        copy.start()
    series[:8] = jnp.zeros((8, series.shape[1]), jnp.float32)
    for copy in shared:
        copy.wait()
    for g in range(sessions):
        at = slice(g * NEW, (g + 1) * NEW)
        own[g].wait()
        series[8:] = x_s[g].astype(jnp.float32)
        out = filtered(series, taps_s, bias_s[...], 9 - taps_s.shape[0], NEW)
        out_ref[at] = out
        part_ref[at] = times_select(out, select_s[...])


def conv_project(x, taps, bias, select):
    tokens, channels = x.shape
    sessions = tokens // NEW
    return pl.pallas_call(
        conv_kernel,
        in_specs=[in_any()] * 4,
        out_specs=[in_vmem()] * 2,
        out_shape=[
            jax.ShapeDtypeStruct((tokens, channels), jnp.bfloat16),
            jax.ShapeDtypeStruct((tokens, select.shape[0]), jnp.bfloat16),
        ],
        scratch_shapes=[
            pltpu.VMEM((NEW + 8, channels), jnp.float32),
            pltpu.VMEM((sessions, NEW, channels), jnp.bfloat16),
            pltpu.VMEM(taps.shape, jnp.float32),
            pltpu.VMEM((1, channels), jnp.float32),
            pltpu.VMEM(select.shape, jnp.bfloat16),
            pltpu.SemaphoreType.DMA((3 + sessions,)),
        ],
        compiler_params=pltpu.CompilerParams(vmem_limit_bytes=56 * MIB),
        cost_estimate=pl.CostEstimate(flops=4 * 10**9, bytes_accessed=16 * MIB, transcendentals=0),
        name="conv_project",
    )(x, taps, bias.reshape(1, channels), select)


def head_rows_kernel(
    meta,
    prompts,
    slots,
    x_any,
    prefix_any,
    taps_any,
    bias_any,
    select_any,
    signal_ref,
    products_ref,
    out_ref,
    part_ref,
    series,
    x_s,
    prefix_s,
    taps_s,
    bias_s,
    select_s,
    sems,
):
    sessions, count = x_s.shape[:2]
    rows = prefix_s.shape[1]

    def slot(g):
        return slot_of(g, meta, prompts, slots)

    def place(g):
        return pl.ds(pl.multiple_of(session_of(g, meta) * NEW, NEW), count)

    copies = [
        pltpu.make_async_copy(source, target, sems.at[n])
        for n, (source, target) in enumerate(
            ((taps_any, taps_s), (bias_any, bias_s), (select_any, select_s))
        )
    ]
    for g in range(sessions):
        copies += [
            pltpu.make_async_copy(prefix_any.at[slot(g) >> 1], prefix_s.at[g], sems.at[3 + 2 * g]),
            pltpu.make_async_copy(x_any.at[place(g)], x_s.at[g], sems.at[4 + 2 * g]),
        ]
    for copy in copies:
        copy.start()
    out_ref[...] = signal_ref[...]
    part_ref[...] = products_ref[...]
    for copy in copies:
        copy.wait()
    outs = []
    for g in range(sessions):
        odd = (slot(g) & 1) == 1
        for k in range(rows):
            pair = prefix_s[g, k].astype(jnp.float32)
            series[8 - rows + k : 9 - rows + k] = jnp.where(odd, pair[1:2], pair[0:1])
        series[8:] = x_s[g].astype(jnp.float32)
        outs.append(filtered(series, taps_s, bias_s[...], 8 - rows, count))
    products = times_select(jnp.concatenate(outs, axis=0), select_s[...])
    for g in range(sessions):
        out_ref[place(g)] = outs[g]
        part_ref[place(g)] = products[g * count : (g + 1) * count]


def head_rows(scalars, x, prefixes, taps, bias, select, signal, products):
    tokens, channels = x.shape
    sessions = tokens // NEW
    return pl.pallas_call(
        head_rows_kernel,
        in_specs=[in_smem()] * 3 + [in_any()] * 5 + [in_vmem()] * 2,
        out_specs=[in_vmem()] * 2,
        out_shape=[
            jax.ShapeDtypeStruct(signal.shape, signal.dtype),
            jax.ShapeDtypeStruct(products.shape, products.dtype),
        ],
        scratch_shapes=[
            pltpu.VMEM((16 + 8, channels), jnp.float32),
            pltpu.VMEM((sessions, 16, channels), jnp.bfloat16),
            pltpu.VMEM((sessions,) + prefixes.shape[1:], jnp.bfloat16),
            pltpu.VMEM(taps.shape, jnp.float32),
            pltpu.VMEM((1, channels), jnp.float32),
            pltpu.VMEM(select.shape, jnp.bfloat16),
            pltpu.SemaphoreType.DMA((3 + 2 * sessions,)),
        ],
        compiler_params=pltpu.CompilerParams(vmem_limit_bytes=56 * MIB),
        name="head_rows",
    )(*scalars, x, prefixes, taps, bias.reshape(1, channels), select, signal, products)


def scan_kernel(
    meta,
    prompts,
    slots,
    projected_ref,
    signal_ref,
    gate_ref,
    weight_ref,
    bias_ref,
    decay_ref,
    here_ref,
    there_ref,
    skip_ref,
    out_weight_any,
    part_a,
    part_b0,
    part_b1,
    part_b2,
    part_b3,
    rate_s,
    state_s,
    step_s,
    drive_s,
    emit_s,
    mix_s,
    gated_s,
    out_weight,
    sems,
    *,
    far,
):
    channels = signal_ref.shape[1]
    tile = 1024
    def out_copy(n):
        cols = pl.ds(n * tile, tile)
        return pltpu.make_async_copy(
            out_weight_any.at[:, cols], out_weight.at[:, cols], sems.at[n]
        )

    states = decay_ref.shape[0]
    blocks = channels // 128
    rank = weight_ref.shape[0]
    new = NEW
    half = OWN

    rate = jnp.exp(decay_ref[...]) * (-LOG2E)
    for b in range(blocks):
        rate_s[:, b, :] = rate[:, b * 128 : (b + 1) * 128]

    for i in range(2):
        g = 2 * far + i
        if i == 1:
            for n in range(out_weight.shape[1] // tile):
                out_copy(n).start()
        at = pl.ds(pl.multiple_of(session_of(g, meta) * new, new), new)
        row = row_of(g, meta, prompts, slots)
        start = jnp.where(
            side_of(g, meta, prompts, slots) == 1,
            there_ref[row, :states].astype(jnp.float32),
            here_ref[row, :states].astype(jnp.float32),
        )
        for b in range(blocks):
            state_s[:, b, :] = start[:, b * 128 : (b + 1) * 128]
        projected = projected_ref[at]
        before = (
            jnp.dot(projected[:, :rank], weight_ref[...], preferred_element_type=jnp.float32)
            + bias_ref[...]
        )
        size = jnp.maximum(before, 0.0) + jnp.log1p(jnp.exp(-jnp.abs(before)))
        drive = size * signal_ref[at].astype(jnp.float32)
        for b in range(blocks):
            cols = slice(b * 128, (b + 1) * 128)
            step_s[:, b] = size[:, cols].reshape(new // 8, 8, 128)
            drive_s[:, b] = drive[:, cols].reshape(new // 8, 8, 128)
        mix = jnp.transpose(projected[:, rank:].astype(jnp.float32))
        for t in range(new):
            mix_s[t] = jnp.broadcast_to(mix[:, t : t + 1], (2 * states, 128))

        def advance(block, state):
            state = list(state)
            rates = [rate_s[n] for n in range(states)]
            for s in range(8):
                d = step_s[block, :, s, :]
                u = drive_s[block, :, s, :]
                t = block * 8 + s
                total = None
                for n in range(states):
                    state[n] = jnp.exp2(d * rates[n]) * state[n] + u * mix_s[t, n : n + 1, :]
                    term = state[n] * mix_s[t, states + n : states + n + 1, :]
                    total = term if total is None else total + term
                emit_s[block, :, s, :] = total
            return tuple(state)

        lax.fori_loop(
            0, new // 8, advance, tuple(state_s[n] for n in range(states)), unroll=2
        )
        for b in range(blocks):
            cols = slice(b * 128, (b + 1) * 128)
            emitted = emit_s[:, b].reshape(new, 128)
            gate = gate_ref[at, cols].astype(jnp.float32)
            signal = signal_ref[at, cols].astype(jnp.float32)
            gated = ((emitted + skip_ref[:, cols] * signal) * silu(gate)).astype(jnp.bfloat16)
            for k in range(2):
                gated_s[z_step(g, k, meta), :, cols] = gated[k * half : (k + 1) * half]

    rows = gated_s[...].reshape(-1, channels)
    split = part_a.shape[-1]
    for n in range(out_weight.shape[1] // tile):
        out_copy(n).wait()
        cols = slice(n * tile, (n + 1) * tile)
        out = jnp.dot(
            rows, out_weight[:, cols], preferred_element_type=jnp.float32
        ).astype(jnp.bfloat16)
        if n * tile < split:
            part_a[:, :, cols] = out.reshape(part_a.shape[0], half, tile)
        else:
            for d, ref in enumerate((part_b0, part_b1, part_b2, part_b3)):
                ref[:, n * tile - split : (n + 1) * tile - split] = out[d * half : (d + 1) * half]


def scan_gate(
    far, scalars, projected, signal, gate, weight, bias, decay, here, there, skip, out_weight
):
    channels = signal.shape[1]
    states = decay.shape[0]
    blocks = channels // 128
    features = out_weight.shape[1]
    split = features // 2
    return pl.pallas_call(
        functools.partial(scan_kernel, far=far),
        in_specs=[in_smem()] * 3 + [in_vmem()] * 9 + [in_any()],
        out_specs=[in_vmem()] * 5,
        out_shape=[jax.ShapeDtypeStruct((4, OWN, split), jnp.bfloat16)]
        + [jax.ShapeDtypeStruct((OWN, features - split), jnp.bfloat16)] * 4,
        scratch_shapes=[
            pltpu.VMEM((states, blocks, 128), jnp.float32),
            pltpu.VMEM((states, blocks, 128), jnp.float32),
            pltpu.VMEM((NEW // 8, blocks, 8, 128), jnp.float32),
            pltpu.VMEM((NEW // 8, blocks, 8, 128), jnp.float32),
            pltpu.VMEM((NEW // 8, blocks, 8, 128), jnp.float32),
            pltpu.VMEM((NEW, 2 * states, 128), jnp.float32),
            pltpu.VMEM((4, OWN, channels), jnp.bfloat16),
            pltpu.VMEM(out_weight.shape, jnp.bfloat16),
            pltpu.SemaphoreType.DMA((features // 1024,)),
        ],
        compiler_params=pltpu.CompilerParams(vmem_limit_bytes=50 * MIB),
        name="scan_far" if far else "scan_near",
    )(
        *scalars,
        projected,
        signal,
        gate,
        weight,
        bias.reshape(1, channels),
        decay,
        here,
        there,
        skip.reshape(1, channels),
        out_weight,
    )


def pick_kernel(meta, prompts, slots, row_ref, out_ref):
    out_ref[...] = row_ref[...]


def pick_far(scalars, cached):
    shape = cached.shape[1:]
    return pl.pallas_call(
        pick_kernel,
        grid_spec=pltpu.PrefetchScalarGridSpec(
            num_scalar_prefetch=3,
            grid=(2,),
            in_specs=[
                pl.BlockSpec((1,) + shape, lambda g, *refs: (cache_row_of(g + 2, *refs), 0, 0))
            ],
            out_specs=pl.BlockSpec((1,) + shape, lambda g, *_: (g, 0, 0)),
        ),
        out_shape=jax.ShapeDtypeStruct((2,) + shape, cached.dtype),
        compiler_params=pltpu.CompilerParams(vmem_limit_bytes=58 * MIB),
        name="pick_far",
    )(*scalars, cached)


def serve_kernel(meta, prompts, slots, *refs):
    tokens, refs = refs[:8], refs[8:]
    (query, key, value, others, head, far_cache, own_cache), refs = refs[:7], refs[7:]
    outs, refs = refs[:4], refs[4:]
    rows_s, weight_s, total, heads_s, cache_s, head_s, row_sem, weight_sem, cache_sem, head_sem = refs
    features = query.shape[0]
    side = features // 2
    lent = head.shape[0]
    widths = (query.shape[1], key.shape[1], value.shape[1])
    width = sum(widths)
    pieces = weight_sem.shape[0]
    depth = features // pieces

    token_copies = [
        pltpu.make_async_copy(
            ref, rows_s.at[pl.ds(n % 4 * OWN, OWN), pl.ds(n // 4 * side, side)], row_sem.at[n]
        )
        for n, ref in enumerate(tokens)
    ]

    def weight_copies(n):
        rows = pl.ds(n * depth, depth)
        copies, column = [], 0
        for k, ref in enumerate((query, key, value, others)):
            skip = lent if k == 3 else 0
            size = ref.shape[1] - skip
            copies.append(
                pltpu.make_async_copy(
                    ref.at[rows, pl.ds(skip, size)],
                    weight_s.at[rows, pl.ds(column, size)],
                    weight_sem.at[n, k],
                )
            )
            column += size
        return copies

    cache_copies = [
        pltpu.make_async_copy(
            own_cache.at[cache_row_of(g, meta, prompts, slots)], cache_s.at[0, g], cache_sem.at[0, g]
        )
        for g in range(2)
    ] + [
        pltpu.make_async_copy(far_cache.at[g], cache_s.at[1, g], cache_sem.at[1, g])
        for g in range(2)
    ]

    def head_copies(n):
        cols = pl.ds(n * lent, lent)
        return [
            pltpu.make_async_copy(
                head.at[:, cols], head_s.at[pl.ds(0, lent), cols], head_sem.at[0, n]
            ),
            pltpu.make_async_copy(
                others.at[cols, pl.ds(0, lent)], head_s.at[pl.ds(lent, lent), cols], head_sem.at[1, n]
            ),
        ]

    def begin(copies):
        for copy in copies:
            copy.start()

    blocks = features // lent
    begin(token_copies)
    begin(weight_copies(0))
    begin(weight_copies(1))
    squares = 0.0
    for n in range(pieces):
        if n * depth % side == 0:
            for copy in token_copies[n * depth // side * 4 :][:4]:
                copy.wait()
        for copy in weight_copies(n):
            copy.wait()
        if n + 2 < pieces:
            begin(weight_copies(n + 2))
        elif n + 2 == pieces:
            begin(cache_copies)
            for m in range(blocks // 2):
                begin(head_copies(m))
        else:
            for m in range(blocks // 2, blocks):
                begin(head_copies(m))
        deep = slice(n * depth, (n + 1) * depth)
        rows = rows_s[:, deep]
        wide_rows = rows.astype(jnp.float32)
        wide_rows = wide_rows * wide_rows
        squares += sum(wide_rows[:, b * 128 : (b + 1) * 128] for b in range(depth // 128))
        product = jnp.dot(rows, weight_s[deep], preferred_element_type=jnp.float32)
        if n == 0:
            total[...] = product
        else:
            total[...] += product
    scale = lax.rsqrt(jnp.sum(squares, axis=-1, keepdims=True) / features + EPSILON)
    total[...] = total[...] * scale
    for copy in cache_copies:
        copy.wait()
    new = 2 * OWN
    heads = widths[0] // HEAD_SIZE
    contract = (((1,), (1,)), ((), ()))
    shrink = LOG2E / math.sqrt(HEAD_SIZE)
    for g in range(2):
        steps = [pl.multiple_of(z_step(g, half, meta) * OWN, OWN) for half in range(2)]
        for side_of_y in range(2):
            cols = slice(side_of_y * width, (side_of_y + 1) * width)
            rows = jnp.concatenate(
                [total[pl.ds(at, OWN), cols] for at in steps], axis=0
            ).astype(jnp.bfloat16)
            old = cache_s[side_of_y, g]
            cached = old.shape[0] // 2
            old_keys, old_values = old[:cached], old[cached:]
            new_keys = rows[:, widths[0] : widths[0] + HEAD_SIZE]
            new_values = rows[:, widths[0] + HEAD_SIZE :]
            queries = jnp.concatenate(
                [rows[:, k * HEAD_SIZE : (k + 1) * HEAD_SIZE] for k in range(heads)], axis=0
            )
            before = lax.dot_general(
                queries, old_keys, contract, preferred_element_type=jnp.float32
            )
            fresh = lax.dot_general(queries, new_keys, contract, preferred_element_type=jnp.float32)
            at = lax.broadcasted_iota(jnp.int32, fresh.shape, 0) & (new - 1)
            fresh = jnp.where(lax.broadcasted_iota(jnp.int32, fresh.shape, 1) <= at, fresh, -1e30)
            top = shrink * jnp.maximum(
                jnp.max(before, axis=-1, keepdims=True), jnp.max(fresh, axis=-1, keepdims=True)
            )
            before = jnp.exp2(before * shrink - top).astype(jnp.bfloat16)
            fresh = jnp.exp2(fresh * shrink - top).astype(jnp.bfloat16)
            ones = jnp.ones((cached, HEAD_SIZE), jnp.bfloat16)
            attended = jnp.dot(
                before,
                jnp.concatenate([old_values, ones], axis=1),
                preferred_element_type=jnp.float32,
            ) + jnp.dot(
                fresh,
                jnp.concatenate([new_values, ones[:new]], axis=1),
                preferred_element_type=jnp.float32,
            )
            attended = (attended[:, :HEAD_SIZE] / attended[:, HEAD_SIZE:]).astype(jnp.bfloat16)
            for half in range(2):
                for k in range(heads):
                    column = side_of_y * widths[0] + k * HEAD_SIZE
                    heads_s[pl.ds(steps[half], OWN), column : column + HEAD_SIZE] = attended[
                        k * new + half * OWN : k * new + (half + 1) * OWN
                    ]

    for n in range(blocks):
        for copy in head_copies(n):
            copy.wait()
        cols = slice(n * lent, (n + 1) * lent)
        out = jnp.dot(
            heads_s[...], head_s[:, cols], preferred_element_type=jnp.float32
        ).astype(jnp.bfloat16)
        for d, ref in enumerate(outs):
            ref[:, cols] = out[d * OWN : (d + 1) * OWN]


def serve(scalars, first, second, query, key, value, others, head, own_cache, far_cache):
    features = query.shape[0]
    width = query.shape[1] + key.shape[1] + value.shape[1]
    return pl.pallas_call(
        serve_kernel,
        in_specs=[in_smem()] * 3 + [in_any()] * 15,
        out_specs=[in_vmem()] * 4,
        out_shape=[jax.ShapeDtypeStruct((OWN, features), jnp.bfloat16)] * 4,
        scratch_shapes=[
            pltpu.VMEM((4 * OWN, features), jnp.bfloat16),
            pltpu.VMEM((features, 2 * width), jnp.bfloat16),
            pltpu.VMEM((4 * OWN, 2 * width), jnp.float32),
            pltpu.VMEM((4 * OWN, 2 * query.shape[1]), jnp.bfloat16),
            pltpu.VMEM((2, 2) + own_cache.shape[1:], jnp.bfloat16),
            pltpu.VMEM((2 * head.shape[0], features), jnp.bfloat16),
            pltpu.SemaphoreType.DMA((8,)),
            pltpu.SemaphoreType.DMA((8, 4)),
            pltpu.SemaphoreType.DMA((2, 2)),
            pltpu.SemaphoreType.DMA((2, features // head.shape[0])),
        ],
        compiler_params=pltpu.CompilerParams(vmem_limit_bytes=56 * MIB),
        name="serve",
    )(*scalars, *first, *second, query, key, value, others, head, far_cache, own_cache)


def after(value, *others):
    return lax.optimization_barrier((value,) + others)[0]


def wide(value):
    return value.astype(jnp.float32)


def send_far(part_a, *parts_b):
    got_b = [lax.ppermute(parts_b[d], "exp", z_shift(d)) for d in (1, 3, 2)]
    return lax.ppermute(part_a, "exp", y_swap()), parts_b[0], got_b


def finish(near, got_a, own_b, got_b):
    own_a, *parts_b = near
    near_b = [lax.ppermute(parts_b[d], "exp", z_shift(d)) for d in (1, 3, 2)]
    far_b = (wide(own_b) + sum(wide(v) for v in got_b)).astype(jnp.bfloat16)
    later_b = lax.ppermute(after(far_b, got_a), "exp", y_swap())
    sums_a = wide(own_a) + wide(got_a)
    rest_a = after(sums_a.astype(jnp.bfloat16), near_b[0], near_b[1], near_b[2])
    later_a = [lax.ppermute(rest_a[d], "exp", z_shift(d)) for d in (1, 3, 2)]
    sum_b = wide(parts_b[0]) + sum(wide(v) for v in near_b) + wide(later_b)
    sum_a = sums_a[0] + sum(wide(v) for v in later_a)
    return sum_a, sum_b


def z_gather(value):
    got = [value] + [None] * 3
    for d in (1, 3, 2):
        got[d] = lax.ppermute(value, "exp", z_shift(-d))
    return got


def shards(
    residual,
    mamba_input,
    mamba_gate,
    filter_taps,
    filter_bias,
    input_select,
    step_weight,
    step_bias,
    decay_log,
    skip_scale,
    output_weight,
    query_weight,
    key_matrix,
    value_matrix,
    head_weight,
    cache_keys,
    stored_cache_values,
    cache_state,
    cache_filter,
    prompt_slot,
    session_prompt,
):
    meta = jnp.stack([lax.axis_index("sess"), lax.axis_index("exp")]).astype(jnp.int32)
    scalars = (meta, session_prompt, prompt_slot)
    by_tap = jnp.swapaxes(cache_filter, 0, 1)
    copies = jnp.broadcast_to(by_tap[None], (16,) + by_tap.shape)
    prefixes = lax.all_to_all(copies, "sess", 0, 0, tiled=True)
    start = after(cache_state.astype(jnp.bfloat16), copies)
    start_far = lax.ppermute(start, "sess", sess_shift(1, 0, 0))
    start_pair = jnp.concatenate([start, start_far], axis=0)
    start_x = [lax.ppermute(start_pair, "sess", sess_shift(0, -d, 0)) for d in (1, 2, 3)]
    signal, part = conv_project(after(mamba_input, start_pair), filter_taps, filter_bias, input_select.T)
    cached = jnp.concatenate([cache_keys, stored_cache_values], axis=1)
    cached = after(cached, start_far)
    cached_far = lax.ppermute(cached, "sess", sess_shift(1, 0, 0))
    signal, part = head_rows(
        scalars,
        mamba_input,
        prefixes,
        filter_taps,
        filter_bias,
        input_select.T,
        signal,
        part,
    )
    part = after(part, *start_x)
    start_here = jnp.concatenate([start_pair] + start_x, axis=0)
    start_there = lax.ppermute(start_here, "sess", sess_shift(0, 0, 1))
    pieces = lax.all_to_all(part.reshape(8, OWN, -1), "exp", 0, 0, tiled=True)
    own = jnp.sum(wide(pieces), axis=0).astype(jnp.bfloat16)
    projected = copies_to_all(own, "exp", 8).reshape(8 * OWN, -1)
    groups = [list(range(8)), list(range(8, 16))]
    cached = lax.all_gather(
        jnp.concatenate([cached, after(cached_far, part)], axis=0),
        "sess",
        axis=0,
        tiled=True,
        axis_index_groups=groups,
    )
    eighth = lax.axis_index("sess") % 8
    share = query_weight.shape[0] // 8
    lent = jnp.concatenate(
        [lax.dynamic_slice_in_dim(head_weight, eighth * share, share, 1)]
        + [
            lax.dynamic_slice_in_dim(w, eighth * share, share, 0)
            for w in (query_weight, key_matrix, value_matrix)
        ],
        axis=1,
    )
    lent = lax.ppermute(after(lent, own), ("sess", "exp"), around())

    def scan(far, projected):
        return scan_gate(
            far,
            scalars,
            projected,
            signal,
            mamba_gate,
            step_weight,
            step_bias,
            decay_log,
            start_here,
            start_there,
            skip_scale,
            output_weight,
        )

    far = scan(1, projected)
    def scan(far, projected):
        return scan_gate(
            far,
            scalars,
            projected,
            signal,
            mamba_gate,
            step_weight,
            step_bias,
            decay_log,
            start_here,
            start_there,
            skip_scale,
            output_weight,
        )

    far = scan(1, projected)
    others = lax.all_gather(
        after(lent, cached, projected), "sess", axis=0, tiled=True, axis_index_groups=groups
    )

    others = lax.all_gather(
        after(lent, far[0]), "sess", axis=0, tiled=True, axis_index_groups=groups
    )
    sent = send_far(*far)
    near = scan(0, after(projected, *far))
    sum_a, sum_b = finish(near, *sent)
    split = residual.shape[1] // 2
    after_a = wide(residual[:, :split]) + sum_a
    after_b = wide(residual[:, split:]) + sum_b
    far_cache = lax.ppermute(after(pick_far(scalars, cached), sum_b), "exp", y_swap())
    tokens_b = z_gather(after_b.astype(jnp.bfloat16))
    tokens_a = z_gather(after_a.astype(jnp.bfloat16))
    products = serve(
        scalars,
        tokens_a,
        tokens_b,
        query_weight,
        key_matrix,
        value_matrix,
        others,
        head_weight,
        cached,
        far_cache,
    )
    got = [lax.ppermute(products[d], "exp", z_shift(d)) for d in (1, 3, 2)]
    head_total = sum(wide(v) for v in [products[0]] + got)
    return (jnp.concatenate([after_a, after_b], axis=1) + head_total).astype(jnp.bfloat16)


def solution(mesh):
    return jax.shard_map(
        shards,
        mesh=mesh,
        in_specs=(
            P(("sess", "exp"), None),
            P("sess", "exp"),
            P("sess", "exp"),
            P(None, "exp"),
            P("exp"),
            P("exp", None),
            P(None, "exp"),
            P("exp"),
            P(None, "exp"),
            P("exp"),
            P("exp", None),
            P(None, "exp"),
            P(None, "exp"),
            P(None, "exp"),
            P("exp", None),
            P("sess", None, "exp"),
            P("sess", None, "exp"),
            P("sess", None, "exp"),
            P("sess", None, "exp"),
            P(),
            P(),
        ),
        out_specs=P(("sess", "exp"), None),
        check_vma=False,
    )
```

time: 220 us -> 196 us (0.89)
  waiting for transfers between devices: 74.7 us -> 52.7 us
  blocking collectives: 0 us -> 12 us
  starting transfers between devices: 55.4 us -> 49.7 us
  local copies, waits for them, and re-layouts: 10.2 us -> 5.38 us
  Pallas kernels: 54.7 us -> 52.2 us
    all_to_all x0 -> x1, blocking collectives: none -> 12 us  [copies_to_all(): lax.all_to_all(jnp.broadcast_to(value[None], (count,) + value.shape), axi...]
    ppermute x3, waiting for transfers between devices: 22.2 us -> 14 us  [shards(): got = [lax.ppermute(products[d], 'exp', z_shift(d)) for d in (1, 3, 2)]]
    all_to_all x1, waiting for transfers between devices: 7.56 us -> 0.01 us  [shards(): prefixes = lax.all_to_all(copies, 'sess', 0, 0, tiled=True)]
    all_to_all x1, waiting for transfers between devices: 0.01 us -> 6.44 us  [shards(): pieces = lax.all_to_all(part.reshape(8, OWN, -1), 'exp', 0, 0, tiled=True)]
    all_to_all x1 -> x0, starting transfers between devices: 5.49 us -> none  [copies_to_all(): lax.all_to_all(jnp.broadcast_to(value[None], (count,) + value.shape), axi...]
    all_to_all x1 -> x0, waiting for transfers between devices: 5.31 us -> none  [copies_to_all(): lax.all_to_all(jnp.broadcast_to(value[None], (count,) + value.shape), axi...]
    ppermute x6, waiting for transfers between devices: 12.4 us -> 7.73 us  [z_gather(): got[d] = lax.ppermute(value, 'exp', z_shift(-d))]
    ppermute x2 -> x1, waiting for transfers between devices: 0.01 us -> 2.74 us  [shards(): lent = lax.ppermute(after(lent, own), ('sess', 'exp'), around())]
  transfers between devices with their start and end apart: 34 -> 32, of which waited for: 20 -> 14; matrix products, arithmetic and copies ran while one was open for 6% -> 4% of each run, Pallas kernels for 17% -> 18%
where the time goes in v3:
time: 196 us; the launch traced here: 195 us
  waiting for transfers between devices  52.7 us (27%)
  Pallas kernels  52.2 us (27%)
  starting transfers between devices  49.7 us (25%)
  between operations  13.8 us (7%)
  blocking collectives  12 us (6%)
  other arithmetic  9.14 us (5%)
  local copies, waits for them, and re-layouts  5.38 us (3%)
    pallas_call x2, Pallas kernels, scan_gate(): pl.pallas_call(functools.partial(scan_kernel, far=far), in_specs=[in_smem...  24.5 us
    pallas_call x1, Pallas kernels, serve(): pl.pallas_call(serve_kernel, in_specs=[in_smem()] * 3 + [in_any()] * 15,...  16.2 us
    ppermute x3, waiting for transfers between devices, shards(): got = [lax.ppermute(products[d], 'exp', z_shift(d)) for d in (1, 3, 2)]  14 us
    all_to_all x1, blocking collectives, copies_to_all(): lax.all_to_all(jnp.broadcast_to(value[None], (count,) + value.shape), axi...  12 us
    ppermute x3, waiting for transfers between devices, finish(): later_a = [lax.ppermute(rest_a[d], 'exp', z_shift(d)) for d in (1, 3, 2)]  11.4 us
    ppermute x6, waiting for transfers between devices, z_gather(): got[d] = lax.ppermute(value, 'exp', z_shift(-d))  7.73 us
    ppermute x6, starting transfers between devices, z_gather(): got[d] = lax.ppermute(value, 'exp', z_shift(-d))  7.68 us
    ppermute x3, waiting for transfers between devices, finish(): near_b = [lax.ppermute(parts_b[d], 'exp', z_shift(d)) for d in (1, 3, 2)]  7.67 us
  transfers between devices with their start and end apart: 32, of which 14 were waited for; matrix products, arithmetic and copies ran while one was open for 4% of the time, Pallas kernels for 18%

profile of v3, /device:TPU:0, one launch (start us, length us, event | category | flops | bytes accessed | tf_op | source)
XLA Modules:
  0.0 195.0 jit_solution(11588829219770223105)
XLA Ops:
  6.5 1.5 broadcast_in_dim.4
  8.0 7.1 %all-to-all-start = ((bf16[16,3,2,1024]{3,2,1,0:T(2,128)(2,1)}), bf16[16,3,2,1024]{3,2,1,0:T(2,128)(2,1)S(1)}, u32[]{:S(2)}, u32[]{:S(2)}) async-start(bf16[16,3,2,1024]{3,2,1,0:T(2,128)(2,1)} %broadcast_in_dim.4), calls=%async_computation | async-start | bytes 393216 | tf_op jit(solution)/shard_map/all_to_all | solution.py:678
  15.2 0.9 convert_element_type.81
  16.1 3.5 %collective-permute-start = (bf16[2,16,1024]{2,1,0:T(8,128)(2,1)S(1)}, bf16[2,16,1024]{2,1,0:T(8,128)(2,1)S(1)}, u32[]{:S(2)}, u32[]{:S(2)}) collective-permute-start(bf16[2,16,1024]{2,1,0:T(8,128)(2,1)S(1)} %convert_element_type.81), channel_id=1, source_target_pairs={{0,64},{8,72},{16,80},{24,88},{32,96},{40,104},{48,112},{56,120},{... | collective-permute-start | bytes 196616 | tf_op jit(solution)/shard_map/ppermute | solution.py:680
  19.7 1.0 pad_maximum_fusion.2
  20.6 0.7 pad_add_fusion.meta
  21.3 2.2 %collective-permute-done = bf16[2,16,1024]{2,1,0:T(8,128)(2,1)S(1)} collective-permute-done((bf16[2,16,1024]{2,1,0:T(8,128)(2,1)S(1)}, bf16[2,16,1024]{2,1,0:T(8,128)(2,1)S(1)}, u32[]{:S(2)}, u32[]{:S(2)}) %collective-permute-start) | collective-permute-done | bytes 65568 | tf_op jit(solution)/shard_map/ppermute | solution.py:680
  23.5 2.6 %collective-permute-start.1 = (bf16[4,16,1024]{2,1,0:T(8,128)(2,1)S(1)}, bf16[4,16,1024]{2,1,0:T(8,128)(2,1)S(1)}, u32[]{:S(2)}, u32[]{:S(2)}) collective-permute-start(bf16[4,16,1024]{2,1,0:T(8,128)(2,1)S(1)} %get-tuple-element.77), channel_id=1, source_target_pairs={{0,48},{8,56},{16,0},{24,8},{32,16},{40,24},{48,32},{56,40},{64,11... | collective-permute-start | bytes 393224 | tf_op jit(solution)/shard_map/ppermute | solution.py:682
  26.1 1.0 collective-permute-start.2
  27.1 0.7 collective-permute-start.3
  27.8 2.1 %collective-permute-start.23 = (bf16[2,512,128]{2,1,0:T(8,128)(2,1)S(1)}, bf16[2,512,128]{2,1,0:T(8,128)(2,1)S(1)}, u32[]{:S(2)}, u32[]{:S(2)}) collective-permute-start(bf16[2,512,128]{2,1,0:T(8,128)(2,1)S(1)} %pad_maximum_fusion.2), channel_id=1, source_target_pairs={{0,64},{8,72},{16,80},{24,88},{32,96},{40,104},{48,112},{56,120},{... | collective-permute-start | bytes 786440 | tf_op jit(solution)/shard_map/ppermute | solution.py:686
  29.9 5.1 %conv_project.1 = (bf16[512,1024]{1,0:T(8,128)(2,1)}, bf16[512,288]{1,0:T(8,128)(2,1)}) custom-call(bf16[512,1024]{1,0:T(8,128)(2,1)} %x_any.2, f32[4,1024]{1,0:T(4,128)} %taps_any.3, f32[1,1024]{1,0:T(1,128)} %bitcast.31, bf16[288,1024]{1,0:T(8,128)(2,1)} %bitcast.28), custom_call_target="tpu_custom_call" | custom-call | flops 4000000000 | bytes 16777216 | tf_op jit(solution)/shard_map/conv_project/pallas_call | solution.py:147
  35.0 0.7 copy-done.9
  35.7 4.1 %head_rows.1 = (bf16[512,1024]{1,0:T(8,128)(2,1)}, bf16[512,288]{1,0:T(8,128)(2,1)}) custom-call(s32[2]{0:T(128)} %pad_add_fusion.meta, s32[64]{0:T(128)} %prompts.9, s32[32]{0:T(128)} %slots.9, bf16[512,1024]{1,0:T(8,128)(2,1)} %x_any.2, bf16[16,3,2,1024]{3,2,1,0:T(2,128)(2,1)} %copy-done.9, f32[4,1024]{1,0:T(4,128)} %taps_any.3, f32[1,1024]{1,0:T(1,128)} %bitcast.32, ...), custom_call_target="tpu_custom_call" | custom-call | tf_op jit(solution)/shard_map/head_rows/pallas_call | solution.py:233
  39.8 0.8 pad_maximum_fusion.1
  40.7 1.0 constant_dynamic-slice_fusion
  41.7 1.3 constant_dynamic-slice_fusion.2
  43.0 5.4 %all-to-all-start.1 = ((bf16[8,64,288]{2,1,0:T(8,128)(2,1)}), bf16[8,64,288]{2,1,0:T(8,128)(2,1)S(1)}, u32[]{:S(2)}, u32[]{:S(2)}) async-start(bf16[8,64,288]{2,1,0:T(8,128)(2,1)} %bitcast.5), calls=%async_computation.1 | async-start | bytes 786432 | tf_op jit(solution)/shard_map/all_to_all | solution.py:700
  48.5 1.2 pad_maximum_fusion
  49.7 6.4 %all-to-all-done.1 = bf16[8,64,288]{2,1,0:T(8,128)(2,1)S(1)} async-done(((bf16[8,64,288]{2,1,0:T(8,128)(2,1)}), bf16[8,64,288]{2,1,0:T(8,128)(2,1)S(1)}, u32[]{:S(2)}, u32[]{:S(2)}) %all-to-all-start.1) | async-done | bytes 294944 | tf_op jit(solution)/shard_map/all_to_all | solution.py:700
  56.2 1.5 collective-permute-start.22
  57.9 12.0 %all_to_all.15 = bf16[8,64,288]{2,1,0:T(8,128)(2,1)S(1)} all-to-all(bf16[8,64,288]{2,1,0:T(8,128)(2,1)S(1)} %broadcast_in_dim.5), channel_id=1, replica_groups=mesh['sess'=16,'exp'=8] {'exp'}, dimensions={0} | all-to-all | bytes 589824 | tf_op jit(solution)/shard_map/all_to_all | solution.py:47
  70.0 12.3 %scan_far.1 = (bf16[4,64,2048]{2,1,0:T(8,128)(2,1)}, bf16[64,2048]{1,0:T(8,128)(2,1)S(1)}, bf16[64,2048]{1,0:T(8,128)(2,1)S(1)}, bf16[64,2048]{1,0:T(8,128)(2,1)S(1)}, bf16[64,2048]{1,0:T(8,128)(2,1)S(1)}) custom-call(s32[2]{0:T(128)S(1)} %copy-done.6, s32[64]{0:T(128)S(1)} %copy-done.4, s32[32]{0:T(128)S(1)} %copy-done.5, bf16[512,288]{1,0:T(8,128)(2,1)S(1)} %bitcast.22, ...), custom_call_target="tpu_custom_call" | custom-call | tf_op jit(solution)/shard_map/scan_far/pallas_call | solution.py:383
  82.2 2.7 %collective-permute-done.22 = bf16[512,1280]{1,0:T(8,128)(2,1)} collective-permute-done((bf16[512,1280]{1,0:T(8,128)(2,1)}, bf16[512,1280]{1,0:T(8,128)(2,1)}, u32[]{:S(2)}, u32[]{:S(2)}) %collective-permute-start.22) | collective-permute-done | bytes 1310752 | tf_op jit(solution)/shard_map/ppermute | solution.py:721
  85.0 0.2 collective-permute-start.5
  85.2 1.6 collective-permute-start.14
  86.7 2.1 %collective-permute-start.13 = (bf16[64,2048]{1,0:T(8,128)(2,1)S(1)}, bf16[64,2048]{1,0:T(8,128)(2,1)S(1)}, u32[]{:S(2)}, u32[]{:S(2)}) collective-permute-start(bf16[64,2048]{1,0:T(8,128)(2,1)S(1)} %get-tuple-element.45), channel_id=1, source_target_pairs={{0,3},{1,0},{2,1},{3,2},{4,7},{5,4},{6,5},{7,6},{8,11},{9,8},{10,9... | collective-permute-start | bytes 786440 | tf_op jit(solution)/shard_map/ppermute | solution.py:627
  88.8 12.2 %scan_near.1 = (bf16[4,64,2048]{2,1,0:T(8,128)(2,1)}, bf16[64,2048]{1,0:T(8,128)(2,1)S(1)}, bf16[64,2048]{1,0:T(8,128)(2,1)S(1)}, bf16[64,2048]{1,0:T(8,128)(2,1)S(1)}, bf16[64,2048]{1,0:T(8,128)(2,1)S(1)}) custom-call(s32[2]{0:T(128)S(1)} %copy-done.6, s32[64]{0:T(128)S(1)} %copy-done.4, s32[32]{0:T(128)S(1)} %copy-done.5, bf16[512,288]{1,0:T(8,128)(2,1)S(1)} %bitcast.23, ...), custom_call_target="tpu_custom_call" | custom-call | tf_op jit(solution)/shard_map/scan_near/pallas_call | solution.py:383
  101.0 0.6 collective-permute-start.6
  101.7 2.8 %collective-permute-start.7 = (bf16[64,2048]{1,0:T(8,128)(2,1)S(1)}, bf16[64,2048]{1,0:T(8,128)(2,1)S(1)}, u32[]{:S(2)}, u32[]{:S(2)}) collective-permute-start(bf16[64,2048]{1,0:T(8,128)(2,1)S(1)} %get-tuple-element.49), channel_id=1, source_target_pairs={{0,3},{1,0},{2,1},{3,2},{4,7},{5,4},{6,5},{7,6},{8,11},{9,8},{10,9... | collective-permute-start | bytes 786440 | tf_op jit(solution)/shard_map/ppermute | solution.py:633
  104.4 1.5 collective-permute-start.8
  105.9 0.1 add_convert_fusion
  106.0 0.5 collective-permute-done.5
  106.6 1.7 convert_add_fusion
  108.3 3.2 %collective-permute-done.6 = bf16[64,2048]{1,0:T(8,128)(2,1)S(1)} collective-permute-done((bf16[64,2048]{1,0:T(8,128)(2,1)S(1)}, bf16[64,2048]{1,0:T(8,128)(2,1)S(1)}, u32[]{:S(2)}, u32[]{:S(2)}) %collective-permute-start.6) | collective-permute-done | bytes 262176 | tf_op jit(solution)/shard_map/ppermute | solution.py:633
  111.5 4.5 %collective-permute-done.7 = bf16[64,2048]{1,0:T(8,128)(2,1)S(1)} collective-permute-done((bf16[64,2048]{1,0:T(8,128)(2,1)S(1)}, bf16[64,2048]{1,0:T(8,128)(2,1)S(1)}, u32[]{:S(2)}, u32[]{:S(2)}) %collective-permute-start.7) | collective-permute-done | bytes 262176 | tf_op jit(solution)/shard_map/ppermute | solution.py:633
  116.1 0.1 collective-permute-start.11
  116.2 3.8 %collective-permute-start.10 = (bf16[64,2048]{1,0:T(8,128)(2,1)S(1)}, bf16[64,2048]{1,0:T(8,128)(2,1)S(1)}, u32[]{:S(2)}, u32[]{:S(2)}) collective-permute-start(bf16[64,2048]{1,0:T(8,128)(2,1)S(1)} %get-tuple-element.72), channel_id=1, source_target_pairs={{0,3},{1,0},{2,1},{3,2},{4,7},{5,4},{6,5},{7,6},{8,11},{9,8},{10,9... | collective-permute-start | bytes 786440 | tf_op jit(solution)/shard_map/ppermute | solution.py:638
  119.9 0.8 collective-permute-start.9
  120.7 0.4 collective-permute-start.15
  121.1 2.9 %collective-permute-done.11 = bf16[64,2048]{1,0:T(8,128)(2,1)S(1)} collective-permute-done((bf16[64,2048]{1,0:T(8,128)(2,1)S(1)}, bf16[64,2048]{1,0:T(8,128)(2,1)S(1)}, u32[]{:S(2)}, u32[]{:S(2)}) %collective-permute-start.11) | collective-permute-done | bytes 262176 | tf_op jit(solution)/shard_map/ppermute | solution.py:638
  124.0 8.5 %collective-permute-done.10 = bf16[64,2048]{1,0:T(8,128)(2,1)S(1)} collective-permute-done((bf16[64,2048]{1,0:T(8,128)(2,1)S(1)}, bf16[64,2048]{1,0:T(8,128)(2,1)S(1)}, u32[]{:S(2)}, u32[]{:S(2)}) %collective-permute-start.10) | collective-permute-done | bytes 262176 | tf_op jit(solution)/shard_map/ppermute | solution.py:638
  132.5 0.4 fusion.5
  133.0 1.2 collective-permute-start.16
  134.1 0.5 collective-permute-start.17
  134.7 0.4 collective-permute-start.18
  135.1 2.8 %collective-permute-start.19 = (bf16[64,2048]{1,0:T(8,128)(2,1)S(1)}, bf16[64,2048]{1,0:T(8,128)(2,1)S(1)}, u32[]{:S(2)}, u32[]{:S(2)}) collective-permute-start(bf16[64,2048]{1,0:T(8,128)(2,1)S(1)} %get-tuple-element.73.refs_4_), channel_id=1, source_target_pairs={{0,3},{1,0},{2,1},{3,2},{4,7},{5,4},{6,5},{7,6},{8,11},{9,8},{10,9... | collective-permute-start | bytes 786440 | tf_op jit(solution)/shard_map/ppermute | solution.py:647
  137.9 1.8 collective-permute-start.20
  139.7 2.4 %pick_far.1 = bf16[2,512,128]{2,1,0:T(8,128)(2,1)} custom-call(s32[2]{0:T(128)} %pad_add_fusion.meta, s32[64]{0:T(128)} %prompts.9, s32[32]{0:T(128)} %slots.9, bf16[32,512,128]{2,1,0:T(8,128)(2,1)} %all-gather.5.cloned.1.call-done.row_ref.refs_14_), custom_call_target="tpu_custom_call" | custom-call | tf_op jit(solution)/shard_map/pick_far/pallas_call | solution.py:423
  142.1 0.9 collective-permute-start.21
  143.0 0.2 collective-permute-start.24
  143.3 1.7 collective-permute-done.18.refs_3_
  145.0 2.6 %collective-permute-done.19.refs_5_ = bf16[64,2048]{1,0:T(8,128)(2,1)S(1)} collective-permute-done((bf16[64,2048]{1,0:T(8,128)(2,1)S(1)}, bf16[64,2048]{1,0:T(8,128)(2,1)S(1)}, u32[]{:S(2)}, u32[]{:S(2)}) %collective-permute-start.19) | collective-permute-done | bytes 262176 | tf_op jit(solution)/shard_map/ppermute | solution.py:647
  147.6 0.7 collective-permute-done.20.refs_6_
  148.3 2.7 %collective-permute-done.21.refs_7_ = bf16[64,2048]{1,0:T(8,128)(2,1)S(1)} collective-permute-done((bf16[64,2048]{1,0:T(8,128)(2,1)S(1)}, bf16[64,2048]{1,0:T(8,128)(2,1)S(1)}, u32[]{:S(2)}, u32[]{:S(2)}) %collective-permute-start.21) | collective-permute-done | bytes 262176 | tf_op jit(solution)/shard_map/ppermute | solution.py:647
  151.1 0.6 copy-done.16
  151.7 0.1 copy-done.17
  151.8 16.2 %serve.1 = (bf16[64,4096]{1,0:T(8,128)(2,1)}, bf16[64,4096]{1,0:T(8,128)(2,1)}, bf16[64,4096]{1,0:T(8,128)(2,1)}, bf16[64,4096]{1,0:T(8,128)(2,1)}) custom-call(s32[2]{0:T(128)} %pad_add_fusion.meta, s32[64]{0:T(128)} %prompts.9, s32[32]{0:T(128)} %slots.9, bf16[64,2048]{1,0:T(8,128)(2,1)} %copy-done.7, bf16[64,2048]{1,0:T(8,128)(2,1)} %copy-done.11, ...), custom_call_target="tpu_custom_call" | custom-call | tf_op jit(solution)/shard_map/serve/pallas_call | solution.py:596
  168.0 1.6 collective-permute-start.27
  169.6 1.6 collective-permute-start.26
  171.2 0.8 collective-permute-start.25
  172.0 8.2 %collective-permute-done.27 = bf16[64,4096]{1,0:T(8,128)(2,1)S(1)} collective-permute-done((bf16[64,4096]{1,0:T(8,128)(2,1)}, bf16[64,4096]{1,0:T(8,128)(2,1)S(1)}, u32[]{:S(2)}, u32[]{:S(2)}) %collective-permute-start.27) | collective-permute-done | bytes 524320 | tf_op jit(solution)/shard_map/ppermute | solution.py:785
  180.1 5.8 %collective-permute-done.26 = bf16[64,4096]{1,0:T(8,128)(2,1)S(1)} collective-permute-done((bf16[64,4096]{1,0:T(8,128)(2,1)}, bf16[64,4096]{1,0:T(8,128)(2,1)S(1)}, u32[]{:S(2)}, u32[]{:S(2)}) %collective-permute-start.26) | collective-permute-done | bytes 524320 | tf_op jit(solution)/shard_map/ppermute | solution.py:785
  186.0 2.2 %fusion = bf16[64,4096]{1,0:T(8,128)(2,1)} fusion(f32[64,2048]{1,0:T(8,128)S(1)} %get-tuple-element.74, f32[64,2048]{1,0:T(8,128)S(1)} %get-tuple-element.67, bf16[64,4096]{1,0:T(8,128)(2,1)S(1)} %collective-permute-done.27, bf16[64,4096]{1,0:T(8,128)(2,1)S(1)} %collective-permute-done.26, bf16[64,4096]{1,0:T(8,128)(2,1)S(1)} %collective-permute-done.25, ...), kind=kLoop, calls=%fused_computation.3 | loop fusion | flops 2621440 | bytes 3670016 | tf_op jit(solution)/shard_map/convert_element_type | solution.py:787
  (65 shorter events, 0.6 us)
Async XLA Ops:
  8.0 27.0 %all-to-all-start = ((bf16[16,3,2,1024]{3,2,1,0:T(2,128)(2,1)}), bf16[16,3,2,1024]{3,2,1,0:T(2,128)(2,1)S(1)}, u32[]{:S(2)}, u32[]{:S(2)}) async-start(bf16[16,3,2,1024]{3,2,1,0:T(2,128)(2,1)} %broadcast_in_dim.4), calls=%async_computation | async-start | bytes 393216 | tf_op jit(solution)/shard_map/all_to_all | solution.py:678
  15.2 124.5 %all-gather.5.cloned.1.call-start = ((), (), s32[]{:S(2)}) async-start(), calls=%async_computation.4 | async-start | bytes 4718592 | tf_op jit(solution)/shard_map/all_gather | solution.py:704
  16.1 7.3 %collective-permute-start = (bf16[2,16,1024]{2,1,0:T(8,128)(2,1)S(1)}, bf16[2,16,1024]{2,1,0:T(8,128)(2,1)S(1)}, u32[]{:S(2)}, u32[]{:S(2)}) collective-permute-start(bf16[2,16,1024]{2,1,0:T(8,128)(2,1)S(1)} %convert_element_type.81), channel_id=1, source_target_pairs={{0,64},{8,72},{16,80},{24,88},{32,96},{40,104},{48,112},{56,120},{... | collective-permute-start | bytes 196616 | tf_op jit(solution)/shard_map/ppermute | solution.py:680
  23.5 16.3 %collective-permute-start.1 = (bf16[4,16,1024]{2,1,0:T(8,128)(2,1)S(1)}, bf16[4,16,1024]{2,1,0:T(8,128)(2,1)S(1)}, u32[]{:S(2)}, u32[]{:S(2)}) collective-permute-start(bf16[4,16,1024]{2,1,0:T(8,128)(2,1)S(1)} %get-tuple-element.77), channel_id=1, source_target_pairs={{0,48},{8,56},{16,0},{24,8},{32,16},{40,24},{48,32},{56,40},{64,11... | collective-permute-start | bytes 393224 | tf_op jit(solution)/shard_map/ppermute | solution.py:682
  26.1 13.7 %collective-permute-start.2 = (bf16[4,16,1024]{2,1,0:T(8,128)(2,1)S(1)}, bf16[4,16,1024]{2,1,0:T(8,128)(2,1)S(1)}, u32[]{:S(2)}, u32[]{:S(2)}) collective-permute-start(bf16[4,16,1024]{2,1,0:T(8,128)(2,1)S(1)} %get-tuple-element.77), channel_id=1, source_target_pairs={{0,32},{8,40},{16,48},{24,56},{32,0},{40,8},{48,16},{56,24},{64,96... | collective-permute-start | bytes 393224 | tf_op jit(solution)/shard_map/ppermute | solution.py:682
  27.1 12.7 %collective-permute-start.3 = (bf16[4,16,1024]{2,1,0:T(8,128)(2,1)S(1)}, bf16[4,16,1024]{2,1,0:T(8,128)(2,1)S(1)}, u32[]{:S(2)}, u32[]{:S(2)}) collective-permute-start(bf16[4,16,1024]{2,1,0:T(8,128)(2,1)S(1)} %get-tuple-element.77), channel_id=1, source_target_pairs={{0,16},{8,24},{16,32},{24,40},{32,48},{40,56},{48,0},{56,8},{64,80... | collective-permute-start | bytes 393224 | tf_op jit(solution)/shard_map/ppermute | solution.py:682
  27.8 12.0 %collective-permute-start.23 = (bf16[2,512,128]{2,1,0:T(8,128)(2,1)S(1)}, bf16[2,512,128]{2,1,0:T(8,128)(2,1)S(1)}, u32[]{:S(2)}, u32[]{:S(2)}) collective-permute-start(bf16[2,512,128]{2,1,0:T(8,128)(2,1)S(1)} %pad_maximum_fusion.2), channel_id=1, source_target_pairs={{0,64},{8,72},{16,80},{24,88},{32,96},{40,104},{48,112},{56,120},{... | collective-permute-start | bytes 786440 | tf_op jit(solution)/shard_map/ppermute | solution.py:686
  35.0 0.7 copy-start.9
  43.0 13.2 %all-to-all-start.1 = ((bf16[8,64,288]{2,1,0:T(8,128)(2,1)}), bf16[8,64,288]{2,1,0:T(8,128)(2,1)S(1)}, u32[]{:S(2)}, u32[]{:S(2)}) async-start(bf16[8,64,288]{2,1,0:T(8,128)(2,1)} %bitcast.5), calls=%async_computation.1 | async-start | bytes 786432 | tf_op jit(solution)/shard_map/all_to_all | solution.py:700
  48.4 21.5 %copy-start = (bf16[256,1024]{1,0:T(8,128)(2,1)S(1)}, bf16[256,1024]{1,0:T(8,128)(2,1)}, u32[]{:S(2)}) copy-start(bf16[256,1024]{1,0:T(8,128)(2,1)} %weight_ref.3) | copy-start | bytes 1572868
  48.4 21.5 %copy-start.1 = (f32[16,1024]{1,0:T(8,128)S(1)}, f32[16,1024]{1,0:T(8,128)}, u32[]{:S(2)}) copy-start(f32[16,1024]{1,0:T(8,128)} %decay_ref.3) | copy-start | bytes 196612
  48.4 21.5 %copy-start.2 = (f32[1024]{0:T(1024)S(1)}, f32[1024]{0:T(1024)}, u32[]{:S(2)}) copy-start(f32[1024]{0:T(1024)} %param.28) | copy-start | bytes 12292
  48.4 21.5 %copy-start.3 = (f32[1024]{0:T(1024)S(1)}, f32[1024]{0:T(1024)}, u32[]{:S(2)}) copy-start(f32[1024]{0:T(1024)} %param.30) | copy-start | bytes 12292
  48.5 21.5 %copy-start.4 = (s32[64]{0:T(128)S(1)}, s32[64]{0:T(128)}, u32[]{:S(2)}) copy-start(s32[64]{0:T(128)} %prompts.9) | copy-start | bytes 772
  48.5 21.5 %copy-start.5 = (s32[32]{0:T(128)S(1)}, s32[32]{0:T(128)}, u32[]{:S(2)}) copy-start(s32[32]{0:T(128)} %slots.9) | copy-start | bytes 388
  48.5 21.5 %copy-start.6 = (s32[2]{0:T(128)S(1)}, s32[2]{0:T(128)}, u32[]{:S(2)}) copy-start(s32[2]{0:T(128)} %pad_add_fusion.meta) | copy-start | bytes 28
  48.5 102.5 %all-gather.3.cloned.1.call-start = ((), (), s32[]{:S(2)}) async-start(), calls=%async_computation.3 | async-start | bytes 11796480 | tf_op jit(solution)/shard_map/all_gather | solution.py:761
  56.2 28.7 %collective-permute-start.22 = (bf16[512,1280]{1,0:T(8,128)(2,1)}, bf16[512,1280]{1,0:T(8,128)(2,1)}, u32[]{:S(2)}, u32[]{:S(2)}) collective-permute-start(bf16[512,1280]{1,0:T(8,128)(2,1)} %pad_maximum_fusion), channel_id=1, source_target_pairs={{0,68},{1,69},{2,70},{3,71},{4,64},{5,65},{6,66},{7,67},{8,76},{9,... | collective-permute-start | bytes 3932168 | tf_op jit(solution)/shard_map/ppermute | solution.py:721
  57.8 12.1 %collective-permute-start.4 = (bf16[16,16,1024]{2,1,0:T(8,128)(2,1)S(1)}, bf16[16,16,1024]{2,1,0:T(8,128)(2,1)S(1)}, u32[]{:S(2)}, u32[]{:S(2)}) collective-permute-start(bf16[16,16,1024]{2,1,0:T(8,128)(2,1)S(1)} %constant_dynamic-update-slice_fusion.2.here_ref), channel_id=1, source_target_pairs={{0,8},{8,0},{16,24},{24,16},{32,40},{40,32},{48,56},{56,48},{64,72... | collective-permute-start | bytes 1572872 | tf_op jit(solution)/shard_map/ppermute | solution.py:699
  85.0 21.6 %collective-permute-start.5 = (bf16[4,64,2048]{2,1,0:T(8,128)(2,1)}, bf16[4,64,2048]{2,1,0:T(8,128)(2,1)S(1)}, u32[]{:S(2)}, u32[]{:S(2)}) collective-permute-start(bf16[4,64,2048]{2,1,0:T(8,128)(2,1)} %get-tuple-element.41), channel_id=1, source_target_pairs={{0,4},{1,5},{2,6},{3,7},{4,0},{5,1},{6,2},{7,3},{8,12},{9,13},{10,... | collective-permute-start | bytes 3145736 | tf_op jit(solution)/shard_map/ppermute | solution.py:628
  85.2 16.5 %collective-permute-start.14 = (bf16[64,2048]{1,0:T(8,128)(2,1)S(1)}, bf16[64,2048]{1,0:T(8,128)(2,1)S(1)}, u32[]{:S(2)}, u32[]{:S(2)}) collective-permute-start(bf16[64,2048]{1,0:T(8,128)(2,1)S(1)} %get-tuple-element.44), channel_id=1, source_target_pairs={{0,2},{1,3},{2,0},{3,1},{4,6},{5,7},{6,4},{7,5},{8,10},{9,11},{10,... | collective-permute-start | bytes 786440 | tf_op jit(solution)/shard_map/ppermute | solution.py:627
  86.7 17.7 %collective-permute-start.13 = (bf16[64,2048]{1,0:T(8,128)(2,1)S(1)}, bf16[64,2048]{1,0:T(8,128)(2,1)S(1)}, u32[]{:S(2)}, u32[]{:S(2)}) collective-permute-start(bf16[64,2048]{1,0:T(8,128)(2,1)S(1)} %get-tuple-element.45), channel_id=1, source_target_pairs={{0,3},{1,0},{2,1},{3,2},{4,7},{5,4},{6,5},{7,6},{8,11},{9,8},{10,9... | collective-permute-start | bytes 786440 | tf_op jit(solution)/shard_map/ppermute | solution.py:627
  88.8 17.1 %collective-permute-start.12 = (bf16[64,2048]{1,0:T(8,128)(2,1)S(1)}, bf16[64,2048]{1,0:T(8,128)(2,1)S(1)}, u32[]{:S(2)}, u32[]{:S(2)}) collective-permute-start(bf16[64,2048]{1,0:T(8,128)(2,1)S(1)} %get-tuple-element.43), channel_id=1, source_target_pairs={{0,1},{1,2},{2,3},{3,0},{4,5},{5,6},{6,7},{7,4},{8,9},{9,10},{10,1... | collective-permute-start | bytes 786440 | tf_op jit(solution)/shard_map/ppermute | solution.py:627
  101.0 10.5 %collective-permute-start.6 = (bf16[64,2048]{1,0:T(8,128)(2,1)S(1)}, bf16[64,2048]{1,0:T(8,128)(2,1)S(1)}, u32[]{:S(2)}, u32[]{:S(2)}) collective-permute-start(bf16[64,2048]{1,0:T(8,128)(2,1)S(1)} %get-tuple-element.48), channel_id=1, source_target_pairs={{0,1},{1,2},{2,3},{3,0},{4,5},{5,6},{6,7},{7,4},{8,9},{9,10},{10,1... | collective-permute-start | bytes 786440 | tf_op jit(solution)/shard_map/ppermute | solution.py:633
  101.7 14.3 %collective-permute-start.7 = (bf16[64,2048]{1,0:T(8,128)(2,1)S(1)}, bf16[64,2048]{1,0:T(8,128)(2,1)S(1)}, u32[]{:S(2)}, u32[]{:S(2)}) collective-permute-start(bf16[64,2048]{1,0:T(8,128)(2,1)S(1)} %get-tuple-element.49), channel_id=1, source_target_pairs={{0,3},{1,0},{2,1},{3,2},{4,7},{5,4},{6,5},{7,6},{8,11},{9,8},{10,9... | collective-permute-start | bytes 786440 | tf_op jit(solution)/shard_map/ppermute | solution.py:633
  104.4 11.5 %collective-permute-start.8 = (bf16[64,2048]{1,0:T(8,128)(2,1)S(1)}, bf16[64,2048]{1,0:T(8,128)(2,1)S(1)}, u32[]{:S(2)}, u32[]{:S(2)}) collective-permute-start(bf16[64,2048]{1,0:T(8,128)(2,1)S(1)} %get-tuple-element.50), channel_id=1, source_target_pairs={{0,2},{1,3},{2,0},{3,1},{4,6},{5,7},{6,4},{7,5},{8,10},{9,11},{10,... | collective-permute-start | bytes 786440 | tf_op jit(solution)/shard_map/ppermute | solution.py:633
  106.6 25.9 %copy-start.10 = (bf16[64,4096]{1,0:T(8,128)(2,1)S(1)}, bf16[64,4096]{1,0:T(8,128)(2,1)}, u32[]{:S(2)}) copy-start(bf16[64,4096]{1,0:T(8,128)(2,1)} %param.21) | copy-start | bytes 1572868
  116.1 8.0 %collective-permute-start.11 = (bf16[64,2048]{1,0:T(8,128)(2,1)S(1)}, bf16[64,2048]{1,0:T(8,128)(2,1)S(1)}, u32[]{:S(2)}, u32[]{:S(2)}) collective-permute-start(bf16[64,2048]{1,0:T(8,128)(2,1)S(1)} %get-tuple-element.71), channel_id=1, source_target_pairs={{0,2},{1,3},{2,0},{3,1},{4,6},{5,7},{6,4},{7,5},{8,10},{9,11},{10,... | collective-permute-start | bytes 786440 | tf_op jit(solution)/shard_map/ppermute | solution.py:638
  116.2 16.3 %collective-permute-start.10 = (bf16[64,2048]{1,0:T(8,128)(2,1)S(1)}, bf16[64,2048]{1,0:T(8,128)(2,1)S(1)}, u32[]{:S(2)}, u32[]{:S(2)}) collective-permute-start(bf16[64,2048]{1,0:T(8,128)(2,1)S(1)} %get-tuple-element.72), channel_id=1, source_target_pairs={{0,3},{1,0},{2,1},{3,2},{4,7},{5,4},{6,5},{7,6},{8,11},{9,8},{10,9... | collective-permute-start | bytes 786440 | tf_op jit(solution)/shard_map/ppermute | solution.py:638
  119.9 12.6 %collective-permute-start.9 = (bf16[64,2048]{1,0:T(8,128)(2,1)S(1)}, bf16[64,2048]{1,0:T(8,128)(2,1)S(1)}, u32[]{:S(2)}, u32[]{:S(2)}) collective-permute-start(bf16[64,2048]{1,0:T(8,128)(2,1)S(1)} %get-tuple-element.70), channel_id=1, source_target_pairs={{0,1},{1,2},{2,3},{3,0},{4,5},{5,6},{6,7},{7,4},{8,9},{9,10},{10,1... | collective-permute-start | bytes 786440 | tf_op jit(solution)/shard_map/ppermute | solution.py:638
  120.7 11.8 %collective-permute-start.15 = (bf16[64,2048]{1,0:T(8,128)(2,1)S(1)}, bf16[64,2048]{1,0:T(8,128)(2,1)S(1)}, u32[]{:S(2)}, u32[]{:S(2)}) collective-permute-start(bf16[64,2048]{1,0:T(8,128)(2,1)S(1)} %add_convert_fusion), channel_id=1, source_target_pairs={{0,4},{1,5},{2,6},{3,7},{4,0},{5,1},{6,2},{7,3},{8,12},{9,13},{10,... | collective-permute-start | bytes 786440 | tf_op jit(solution)/shard_map/ppermute | solution.py:635
  133.0 18.1 %copy-start.7 = (bf16[64,2048]{1,0:T(8,128)(2,1)}, bf16[64,2048]{1,0:T(8,128)(2,1)S(1)}, u32[]{:S(2)}) copy-start(bf16[64,2048]{1,0:T(8,128)(2,1)S(1)} %get-tuple-element.66.refs_0_) | copy-start | bytes 786436
  133.0 18.1 %copy-start.8 = (bf16[64,2048]{1,0:T(8,128)(2,1)}, bf16[64,2048]{1,0:T(8,128)(2,1)S(1)}, u32[]{:S(2)}) copy-start(bf16[64,2048]{1,0:T(8,128)(2,1)S(1)} %get-tuple-element.73.refs_4_) | copy-start | bytes 786436
  133.0 9.1 %collective-permute-start.16 = (bf16[64,2048]{1,0:T(8,128)(2,1)S(1)}, bf16[64,2048]{1,0:T(8,128)(2,1)S(1)}, u32[]{:S(2)}, u32[]{:S(2)}) collective-permute-start(bf16[64,2048]{1,0:T(8,128)(2,1)S(1)} %get-tuple-element.66.refs_0_), channel_id=1, source_target_pairs={{0,3},{1,0},{2,1},{3,2},{4,7},{5,4},{6,5},{7,6},{8,11},{9,8},{10,9... | collective-permute-start | bytes 786440 | tf_op jit(solution)/shard_map/ppermute | solution.py:647
  134.1 8.9 %collective-permute-start.17 = (bf16[64,2048]{1,0:T(8,128)(2,1)S(1)}, bf16[64,2048]{1,0:T(8,128)(2,1)S(1)}, u32[]{:S(2)}, u32[]{:S(2)}) collective-permute-start(bf16[64,2048]{1,0:T(8,128)(2,1)S(1)} %get-tuple-element.66.refs_0_), channel_id=1, source_target_pairs={{0,2},{1,3},{2,0},{3,1},{4,6},{5,7},{6,4},{7,5},{8,10},{9,11},{10,... | collective-permute-start | bytes 786440 | tf_op jit(solution)/shard_map/ppermute | solution.py:647
  134.7 10.3 %collective-permute-start.18 = (bf16[64,2048]{1,0:T(8,128)(2,1)S(1)}, bf16[64,2048]{1,0:T(8,128)(2,1)S(1)}, u32[]{:S(2)}, u32[]{:S(2)}) collective-permute-start(bf16[64,2048]{1,0:T(8,128)(2,1)S(1)} %get-tuple-element.66.refs_0_), channel_id=1, source_target_pairs={{0,1},{1,2},{2,3},{3,0},{4,5},{5,6},{6,7},{7,4},{8,9},{9,10},{10,1... | collective-permute-start | bytes 786440 | tf_op jit(solution)/shard_map/ppermute | solution.py:647
  135.1 12.5 %collective-permute-start.19 = (bf16[64,2048]{1,0:T(8,128)(2,1)S(1)}, bf16[64,2048]{1,0:T(8,128)(2,1)S(1)}, u32[]{:S(2)}, u32[]{:S(2)}) collective-permute-start(bf16[64,2048]{1,0:T(8,128)(2,1)S(1)} %get-tuple-element.73.refs_4_), channel_id=1, source_target_pairs={{0,3},{1,0},{2,1},{3,2},{4,7},{5,4},{6,5},{7,6},{8,11},{9,8},{10,9... | collective-permute-start | bytes 786440 | tf_op jit(solution)/shard_map/ppermute | solution.py:647
  137.9 10.4 %collective-permute-start.20 = (bf16[64,2048]{1,0:T(8,128)(2,1)S(1)}, bf16[64,2048]{1,0:T(8,128)(2,1)S(1)}, u32[]{:S(2)}, u32[]{:S(2)}) collective-permute-start(bf16[64,2048]{1,0:T(8,128)(2,1)S(1)} %get-tuple-element.73.refs_4_), channel_id=1, source_target_pairs={{0,2},{1,3},{2,0},{3,1},{4,6},{5,7},{6,4},{7,5},{8,10},{9,11},{10,... | collective-permute-start | bytes 786440 | tf_op jit(solution)/shard_map/ppermute | solution.py:647
  142.1 9.0 %copy-start.11 = (bf16[64,2048]{1,0:T(8,128)(2,1)}, bf16[64,2048]{1,0:T(8,128)(2,1)S(1)}, u32[]{:S(2)}) copy-start(bf16[64,2048]{1,0:T(8,128)(2,1)S(1)} %collective-permute-done.16.refs_1_) | copy-start | bytes 786436
  142.1 8.9 %collective-permute-start.21 = (bf16[64,2048]{1,0:T(8,128)(2,1)S(1)}, bf16[64,2048]{1,0:T(8,128)(2,1)S(1)}, u32[]{:S(2)}, u32[]{:S(2)}) collective-permute-start(bf16[64,2048]{1,0:T(8,128)(2,1)S(1)} %get-tuple-element.73.refs_4_), channel_id=1, source_target_pairs={{0,1},{1,2},{2,3},{3,0},{4,5},{5,6},{6,7},{7,4},{8,9},{9,10},{10,1... | collective-permute-start | bytes 786440 | tf_op jit(solution)/shard_map/ppermute | solution.py:647
  143.0 8.0 %copy-start.12 = (bf16[64,2048]{1,0:T(8,128)(2,1)}, bf16[64,2048]{1,0:T(8,128)(2,1)S(1)}, u32[]{:S(2)}) copy-start(bf16[64,2048]{1,0:T(8,128)(2,1)S(1)} %collective-permute-done.17.refs_2_) | copy-start | bytes 786436
  143.0 8.0 %collective-permute-start.24 = (bf16[2,512,128]{2,1,0:T(8,128)(2,1)}, bf16[2,512,128]{2,1,0:T(8,128)(2,1)S(1)}, u32[]{:S(2)}, u32[]{:S(2)}) collective-permute-start(bf16[2,512,128]{2,1,0:T(8,128)(2,1)} %pick_far.1), channel_id=1, source_target_pairs={{0,4},{1,5},{2,6},{3,7},{4,0},{5,1},{6,2},{7,3},{8,12},{9,13},{10,... | collective-permute-start | bytes 786440 | tf_op jit(solution)/shard_map/ppermute | solution.py:770
  145.0 6.1 %copy-start.13 = (bf16[64,2048]{1,0:T(8,128)(2,1)}, bf16[64,2048]{1,0:T(8,128)(2,1)S(1)}, u32[]{:S(2)}) copy-start(bf16[64,2048]{1,0:T(8,128)(2,1)S(1)} %collective-permute-done.18.refs_3_) | copy-start | bytes 786436
  147.6 3.5 %copy-start.14 = (bf16[64,2048]{1,0:T(8,128)(2,1)}, bf16[64,2048]{1,0:T(8,128)(2,1)S(1)}, u32[]{:S(2)}) copy-start(bf16[64,2048]{1,0:T(8,128)(2,1)S(1)} %collective-permute-done.19.refs_5_) | copy-start | bytes 786436
  148.3 2.8 %copy-start.15 = (bf16[64,2048]{1,0:T(8,128)(2,1)}, bf16[64,2048]{1,0:T(8,128)(2,1)S(1)}, u32[]{:S(2)}) copy-start(bf16[64,2048]{1,0:T(8,128)(2,1)S(1)} %collective-permute-done.20.refs_6_) | copy-start | bytes 786436
  151.0 0.7 copy-start.16
  151.0 0.8 copy-start.17
  168.0 12.1 %collective-permute-start.27 = (bf16[64,4096]{1,0:T(8,128)(2,1)}, bf16[64,4096]{1,0:T(8,128)(2,1)S(1)}, u32[]{:S(2)}, u32[]{:S(2)}) collective-permute-start(bf16[64,4096]{1,0:T(8,128)(2,1)} %get-tuple-element.62), channel_id=1, source_target_pairs={{0,2},{1,3},{2,0},{3,1},{4,6},{5,7},{6,4},{7,5},{8,10},{9,11},{10,... | collective-permute-start | bytes 1572872 | tf_op jit(solution)/shard_map/ppermute | solution.py:785
  169.6 16.4 %collective-permute-start.26 = (bf16[64,4096]{1,0:T(8,128)(2,1)}, bf16[64,4096]{1,0:T(8,128)(2,1)S(1)}, u32[]{:S(2)}, u32[]{:S(2)}) collective-permute-start(bf16[64,4096]{1,0:T(8,128)(2,1)} %get-tuple-element.61), channel_id=1, source_target_pairs={{0,3},{1,0},{2,1},{3,2},{4,7},{5,4},{6,5},{7,6},{8,11},{9,8},{10,9... | collective-permute-start | bytes 1572872 | tf_op jit(solution)/shard_map/ppermute | solution.py:785
  171.2 14.8 %collective-permute-start.25 = (bf16[64,4096]{1,0:T(8,128)(2,1)}, bf16[64,4096]{1,0:T(8,128)(2,1)S(1)}, u32[]{:S(2)}, u32[]{:S(2)}) collective-permute-start(bf16[64,4096]{1,0:T(8,128)(2,1)} %get-tuple-element.60), channel_id=1, source_target_pairs={{0,1},{1,2},{2,3},{3,0},{4,5},{5,6},{6,7},{7,4},{8,9},{9,10},{10,1... | collective-permute-start | bytes 1572872 | tf_op jit(solution)/shard_map/ppermute | solution.py:785
Sparse Core Ops, SparseCore 0:
  40.8 32.1 all-gather.4
  85.1 57.0 all-gather.2

commit v4 on v3

--- a/solution.py
+++ b/solution.py
@@ -582,6 +582,7 @@
     for n in range(blocks):
         for copy in head_copies(n):
             copy.wait()
+    for n in range(blocks):
         cols = slice(n * lent, (n + 1) * lent)
         out = jnp.dot(
             heads_s[...], head_s[:, cols], preferred_element_type=jnp.float32
@@ -606,7 +607,7 @@
             pltpu.VMEM((2, 2) + own_cache.shape[1:], jnp.bfloat16),
             pltpu.VMEM((2 * head.shape[0], features), jnp.bfloat16),
             pltpu.SemaphoreType.DMA((8,)),
-            pltpu.SemaphoreType.DMA((8, 4)),
+            pltpu.SemaphoreType.DMA((4, 4)),
             pltpu.SemaphoreType.DMA((2, 2)),
             pltpu.SemaphoreType.DMA((2, features // head.shape[0])),
         ],

time: 196 us -> 193 us (0.985)
  Pallas kernels: 52.2 us -> 49.3 us
    pallas_call x1, Pallas kernels: 16.2 us -> 13.3 us  [serve(): pl.pallas_call(serve_kernel, in_specs=[in_smem()] * 3 + [in_any()] * 15,...]
  transfers between devices with their start and end apart: 32 -> 32, of which waited for: 14 -> 14; matrix products, arithmetic and copies ran while one was open for 4% -> 4% of each run, Pallas kernels for 18% -> 19%
where the time goes in v4:
time: 193 us; the launch traced here: 192 us
  waiting for transfers between devices  52.7 us (27%)
  starting transfers between devices  49.7 us (26%)
  Pallas kernels  49.3 us (26%)
  between operations  13.8 us (7%)
  blocking collectives  12 us (6%)
  other arithmetic  9.14 us (5%)
  local copies, waits for them, and re-layouts  5.38 us (3%)
    pallas_call x2, Pallas kernels, scan_gate(): pl.pallas_call(functools.partial(scan_kernel, far=far), in_specs=[in_smem...  24.5 us
    ppermute x3, waiting for transfers between devices, shards(): got = [lax.ppermute(products[d], 'exp', z_shift(d)) for d in (1, 3, 2)]  14 us
    pallas_call x1, Pallas kernels, serve(): pl.pallas_call(serve_kernel, in_specs=[in_smem()] * 3 + [in_any()] * 15,...  13.3 us
    all_to_all x1, blocking collectives, copies_to_all(): lax.all_to_all(jnp.broadcast_to(value[None], (count,) + value.shape), axi...  12 us
    ppermute x3, waiting for transfers between devices, finish(): later_a = [lax.ppermute(rest_a[d], 'exp', z_shift(d)) for d in (1, 3, 2)]  11.4 us
    ppermute x6, waiting for transfers between devices, z_gather(): got[d] = lax.ppermute(value, 'exp', z_shift(-d))  7.73 us
    ppermute x6, starting transfers between devices, z_gather(): got[d] = lax.ppermute(value, 'exp', z_shift(-d))  7.68 us
    ppermute x3, waiting for transfers between devices, finish(): near_b = [lax.ppermute(parts_b[d], 'exp', z_shift(d)) for d in (1, 3, 2)]  7.67 us
  transfers between devices with their start and end apart: 32, of which 14 were waited for; matrix products, arithmetic and copies ran while one was open for 4% of the time, Pallas kernels for 19%

profile of v4, /device:TPU:0, one launch (start us, length us, event | category | flops | bytes accessed | tf_op | source)
XLA Modules:
  0.0 192.0 jit_solution(11103119930512760640)
XLA Ops:
  6.5 1.5 broadcast_in_dim.4
  8.0 7.1 %all-to-all-start = ((bf16[16,3,2,1024]{3,2,1,0:T(2,128)(2,1)}), bf16[16,3,2,1024]{3,2,1,0:T(2,128)(2,1)S(1)}, u32[]{:S(2)}, u32[]{:S(2)}) async-start(bf16[16,3,2,1024]{3,2,1,0:T(2,128)(2,1)} %broadcast_in_dim.4), calls=%async_computation | async-start | bytes 393216 | tf_op jit(solution)/shard_map/all_to_all | solution.py:679
  15.2 0.9 convert_element_type.81
  16.1 3.5 %collective-permute-start = (bf16[2,16,1024]{2,1,0:T(8,128)(2,1)S(1)}, bf16[2,16,1024]{2,1,0:T(8,128)(2,1)S(1)}, u32[]{:S(2)}, u32[]{:S(2)}) collective-permute-start(bf16[2,16,1024]{2,1,0:T(8,128)(2,1)S(1)} %convert_element_type.81), channel_id=1, source_target_pairs={{0,64},{8,72},{16,80},{24,88},{32,96},{40,104},{48,112},{56,120},{... | collective-permute-start | bytes 196616 | tf_op jit(solution)/shard_map/ppermute | solution.py:681
  19.7 1.0 pad_maximum_fusion.2
  20.6 0.7 pad_add_fusion.meta
  21.3 2.2 %collective-permute-done = bf16[2,16,1024]{2,1,0:T(8,128)(2,1)S(1)} collective-permute-done((bf16[2,16,1024]{2,1,0:T(8,128)(2,1)S(1)}, bf16[2,16,1024]{2,1,0:T(8,128)(2,1)S(1)}, u32[]{:S(2)}, u32[]{:S(2)}) %collective-permute-start) | collective-permute-done | bytes 65568 | tf_op jit(solution)/shard_map/ppermute | solution.py:681
  23.5 2.6 %collective-permute-start.1 = (bf16[4,16,1024]{2,1,0:T(8,128)(2,1)S(1)}, bf16[4,16,1024]{2,1,0:T(8,128)(2,1)S(1)}, u32[]{:S(2)}, u32[]{:S(2)}) collective-permute-start(bf16[4,16,1024]{2,1,0:T(8,128)(2,1)S(1)} %get-tuple-element.77), channel_id=1, source_target_pairs={{0,48},{8,56},{16,0},{24,8},{32,16},{40,24},{48,32},{56,40},{64,11... | collective-permute-start | bytes 393224 | tf_op jit(solution)/shard_map/ppermute | solution.py:683
  26.1 1.0 collective-permute-start.2
  27.1 0.7 collective-permute-start.3
  27.8 2.1 %collective-permute-start.23 = (bf16[2,512,128]{2,1,0:T(8,128)(2,1)S(1)}, bf16[2,512,128]{2,1,0:T(8,128)(2,1)S(1)}, u32[]{:S(2)}, u32[]{:S(2)}) collective-permute-start(bf16[2,512,128]{2,1,0:T(8,128)(2,1)S(1)} %pad_maximum_fusion.2), channel_id=1, source_target_pairs={{0,64},{8,72},{16,80},{24,88},{32,96},{40,104},{48,112},{56,120},{... | collective-permute-start | bytes 786440 | tf_op jit(solution)/shard_map/ppermute | solution.py:687
  29.9 5.1 %conv_project.1 = (bf16[512,1024]{1,0:T(8,128)(2,1)}, bf16[512,288]{1,0:T(8,128)(2,1)}) custom-call(bf16[512,1024]{1,0:T(8,128)(2,1)} %x_any.2, f32[4,1024]{1,0:T(4,128)} %taps_any.3, f32[1,1024]{1,0:T(1,128)} %bitcast.31, bf16[288,1024]{1,0:T(8,128)(2,1)} %bitcast.28), custom_call_target="tpu_custom_call" | custom-call | flops 4000000000 | bytes 16777216 | tf_op jit(solution)/shard_map/conv_project/pallas_call | solution.py:147
  35.0 0.7 copy-done.9
  35.7 4.1 %head_rows.1 = (bf16[512,1024]{1,0:T(8,128)(2,1)}, bf16[512,288]{1,0:T(8,128)(2,1)}) custom-call(s32[2]{0:T(128)} %pad_add_fusion.meta, s32[64]{0:T(128)} %prompts.9, s32[32]{0:T(128)} %slots.9, bf16[512,1024]{1,0:T(8,128)(2,1)} %x_any.2, bf16[16,3,2,1024]{3,2,1,0:T(2,128)(2,1)} %copy-done.9, f32[4,1024]{1,0:T(4,128)} %taps_any.3, f32[1,1024]{1,0:T(1,128)} %bitcast.32, ...), custom_call_target="tpu_custom_call" | custom-call | tf_op jit(solution)/shard_map/head_rows/pallas_call | solution.py:233
  39.8 0.8 pad_maximum_fusion.1
  40.7 1.0 constant_dynamic-slice_fusion
  41.7 1.3 constant_dynamic-slice_fusion.2
  43.0 5.4 %all-to-all-start.1 = ((bf16[8,64,288]{2,1,0:T(8,128)(2,1)}), bf16[8,64,288]{2,1,0:T(8,128)(2,1)S(1)}, u32[]{:S(2)}, u32[]{:S(2)}) async-start(bf16[8,64,288]{2,1,0:T(8,128)(2,1)} %bitcast.5), calls=%async_computation.1 | async-start | bytes 786432 | tf_op jit(solution)/shard_map/all_to_all | solution.py:701
  48.5 1.2 pad_maximum_fusion
  49.7 6.4 %all-to-all-done.1 = bf16[8,64,288]{2,1,0:T(8,128)(2,1)S(1)} async-done(((bf16[8,64,288]{2,1,0:T(8,128)(2,1)}), bf16[8,64,288]{2,1,0:T(8,128)(2,1)S(1)}, u32[]{:S(2)}, u32[]{:S(2)}) %all-to-all-start.1) | async-done | bytes 294944 | tf_op jit(solution)/shard_map/all_to_all | solution.py:701
  56.2 1.5 collective-permute-start.22
  57.9 12.0 %all_to_all.15 = bf16[8,64,288]{2,1,0:T(8,128)(2,1)S(1)} all-to-all(bf16[8,64,288]{2,1,0:T(8,128)(2,1)S(1)} %broadcast_in_dim.5), channel_id=1, replica_groups=mesh['sess'=16,'exp'=8] {'exp'}, dimensions={0} | all-to-all | bytes 589824 | tf_op jit(solution)/shard_map/all_to_all | solution.py:47
  70.0 12.3 %scan_far.1 = (bf16[4,64,2048]{2,1,0:T(8,128)(2,1)}, bf16[64,2048]{1,0:T(8,128)(2,1)S(1)}, bf16[64,2048]{1,0:T(8,128)(2,1)S(1)}, bf16[64,2048]{1,0:T(8,128)(2,1)S(1)}, bf16[64,2048]{1,0:T(8,128)(2,1)S(1)}) custom-call(s32[2]{0:T(128)S(1)} %copy-done.6, s32[64]{0:T(128)S(1)} %copy-done.4, s32[32]{0:T(128)S(1)} %copy-done.5, bf16[512,288]{1,0:T(8,128)(2,1)S(1)} %bitcast.22, ...), custom_call_target="tpu_custom_call" | custom-call | tf_op jit(solution)/shard_map/scan_far/pallas_call | solution.py:383
  82.2 2.7 %collective-permute-done.22 = bf16[512,1280]{1,0:T(8,128)(2,1)} collective-permute-done((bf16[512,1280]{1,0:T(8,128)(2,1)}, bf16[512,1280]{1,0:T(8,128)(2,1)}, u32[]{:S(2)}, u32[]{:S(2)}) %collective-permute-start.22) | collective-permute-done | bytes 1310752 | tf_op jit(solution)/shard_map/ppermute | solution.py:722
  85.0 0.2 collective-permute-start.5
  85.2 1.6 collective-permute-start.14
  86.7 2.1 %collective-permute-start.13 = (bf16[64,2048]{1,0:T(8,128)(2,1)S(1)}, bf16[64,2048]{1,0:T(8,128)(2,1)S(1)}, u32[]{:S(2)}, u32[]{:S(2)}) collective-permute-start(bf16[64,2048]{1,0:T(8,128)(2,1)S(1)} %get-tuple-element.45), channel_id=1, source_target_pairs={{0,3},{1,0},{2,1},{3,2},{4,7},{5,4},{6,5},{7,6},{8,11},{9,8},{10,9... | collective-permute-start | bytes 786440 | tf_op jit(solution)/shard_map/ppermute | solution.py:628
  88.8 12.2 %scan_near.1 = (bf16[4,64,2048]{2,1,0:T(8,128)(2,1)}, bf16[64,2048]{1,0:T(8,128)(2,1)S(1)}, bf16[64,2048]{1,0:T(8,128)(2,1)S(1)}, bf16[64,2048]{1,0:T(8,128)(2,1)S(1)}, bf16[64,2048]{1,0:T(8,128)(2,1)S(1)}) custom-call(s32[2]{0:T(128)S(1)} %copy-done.6, s32[64]{0:T(128)S(1)} %copy-done.4, s32[32]{0:T(128)S(1)} %copy-done.5, bf16[512,288]{1,0:T(8,128)(2,1)S(1)} %bitcast.23, ...), custom_call_target="tpu_custom_call" | custom-call | tf_op jit(solution)/shard_map/scan_near/pallas_call | solution.py:383
  101.0 0.6 collective-permute-start.6
  101.7 2.8 %collective-permute-start.7 = (bf16[64,2048]{1,0:T(8,128)(2,1)S(1)}, bf16[64,2048]{1,0:T(8,128)(2,1)S(1)}, u32[]{:S(2)}, u32[]{:S(2)}) collective-permute-start(bf16[64,2048]{1,0:T(8,128)(2,1)S(1)} %get-tuple-element.49), channel_id=1, source_target_pairs={{0,3},{1,0},{2,1},{3,2},{4,7},{5,4},{6,5},{7,6},{8,11},{9,8},{10,9... | collective-permute-start | bytes 786440 | tf_op jit(solution)/shard_map/ppermute | solution.py:634
  104.4 1.5 collective-permute-start.8
  105.9 0.1 add_convert_fusion
  106.0 0.5 collective-permute-done.5
  106.6 1.7 convert_add_fusion
  108.3 3.2 %collective-permute-done.6 = bf16[64,2048]{1,0:T(8,128)(2,1)S(1)} collective-permute-done((bf16[64,2048]{1,0:T(8,128)(2,1)S(1)}, bf16[64,2048]{1,0:T(8,128)(2,1)S(1)}, u32[]{:S(2)}, u32[]{:S(2)}) %collective-permute-start.6) | collective-permute-done | bytes 262176 | tf_op jit(solution)/shard_map/ppermute | solution.py:634
  111.5 4.5 %collective-permute-done.7 = bf16[64,2048]{1,0:T(8,128)(2,1)S(1)} collective-permute-done((bf16[64,2048]{1,0:T(8,128)(2,1)S(1)}, bf16[64,2048]{1,0:T(8,128)(2,1)S(1)}, u32[]{:S(2)}, u32[]{:S(2)}) %collective-permute-start.7) | collective-permute-done | bytes 262176 | tf_op jit(solution)/shard_map/ppermute | solution.py:634
  116.1 0.1 collective-permute-start.11
  116.2 3.8 %collective-permute-start.10 = (bf16[64,2048]{1,0:T(8,128)(2,1)S(1)}, bf16[64,2048]{1,0:T(8,128)(2,1)S(1)}, u32[]{:S(2)}, u32[]{:S(2)}) collective-permute-start(bf16[64,2048]{1,0:T(8,128)(2,1)S(1)} %get-tuple-element.72), channel_id=1, source_target_pairs={{0,3},{1,0},{2,1},{3,2},{4,7},{5,4},{6,5},{7,6},{8,11},{9,8},{10,9... | collective-permute-start | bytes 786440 | tf_op jit(solution)/shard_map/ppermute | solution.py:639
  119.9 0.8 collective-permute-start.9
  120.7 0.4 collective-permute-start.15
  121.1 2.9 %collective-permute-done.11 = bf16[64,2048]{1,0:T(8,128)(2,1)S(1)} collective-permute-done((bf16[64,2048]{1,0:T(8,128)(2,1)S(1)}, bf16[64,2048]{1,0:T(8,128)(2,1)S(1)}, u32[]{:S(2)}, u32[]{:S(2)}) %collective-permute-start.11) | collective-permute-done | bytes 262176 | tf_op jit(solution)/shard_map/ppermute | solution.py:639
  124.0 8.5 %collective-permute-done.10 = bf16[64,2048]{1,0:T(8,128)(2,1)S(1)} collective-permute-done((bf16[64,2048]{1,0:T(8,128)(2,1)S(1)}, bf16[64,2048]{1,0:T(8,128)(2,1)S(1)}, u32[]{:S(2)}, u32[]{:S(2)}) %collective-permute-start.10) | collective-permute-done | bytes 262176 | tf_op jit(solution)/shard_map/ppermute | solution.py:639
  132.5 0.4 fusion.5
  133.0 1.2 collective-permute-start.16
  134.1 0.5 collective-permute-start.17
  134.7 0.4 collective-permute-start.18
  135.1 2.8 %collective-permute-start.19 = (bf16[64,2048]{1,0:T(8,128)(2,1)S(1)}, bf16[64,2048]{1,0:T(8,128)(2,1)S(1)}, u32[]{:S(2)}, u32[]{:S(2)}) collective-permute-start(bf16[64,2048]{1,0:T(8,128)(2,1)S(1)} %get-tuple-element.73.refs_4_), channel_id=1, source_target_pairs={{0,3},{1,0},{2,1},{3,2},{4,7},{5,4},{6,5},{7,6},{8,11},{9,8},{10,9... | collective-permute-start | bytes 786440 | tf_op jit(solution)/shard_map/ppermute | solution.py:648
  137.9 1.8 collective-permute-start.20
  139.7 2.4 %pick_far.1 = bf16[2,512,128]{2,1,0:T(8,128)(2,1)} custom-call(s32[2]{0:T(128)} %pad_add_fusion.meta, s32[64]{0:T(128)} %prompts.9, s32[32]{0:T(128)} %slots.9, bf16[32,512,128]{2,1,0:T(8,128)(2,1)} %all-gather.5.cloned.1.call-done.row_ref.refs_14_), custom_call_target="tpu_custom_call" | custom-call | tf_op jit(solution)/shard_map/pick_far/pallas_call | solution.py:423
  142.1 0.9 collective-permute-start.21
  143.0 0.2 collective-permute-start.24
  143.3 1.7 collective-permute-done.18.refs_3_
  145.0 2.6 %collective-permute-done.19.refs_5_ = bf16[64,2048]{1,0:T(8,128)(2,1)S(1)} collective-permute-done((bf16[64,2048]{1,0:T(8,128)(2,1)S(1)}, bf16[64,2048]{1,0:T(8,128)(2,1)S(1)}, u32[]{:S(2)}, u32[]{:S(2)}) %collective-permute-start.19) | collective-permute-done | bytes 262176 | tf_op jit(solution)/shard_map/ppermute | solution.py:648
  147.6 0.7 collective-permute-done.20.refs_6_
  148.3 2.7 %collective-permute-done.21.refs_7_ = bf16[64,2048]{1,0:T(8,128)(2,1)S(1)} collective-permute-done((bf16[64,2048]{1,0:T(8,128)(2,1)S(1)}, bf16[64,2048]{1,0:T(8,128)(2,1)S(1)}, u32[]{:S(2)}, u32[]{:S(2)}) %collective-permute-start.21) | collective-permute-done | bytes 262176 | tf_op jit(solution)/shard_map/ppermute | solution.py:648
  151.1 0.6 copy-done.16
  151.7 0.1 copy-done.17
  151.8 13.3 %serve.1 = (bf16[64,4096]{1,0:T(8,128)(2,1)}, bf16[64,4096]{1,0:T(8,128)(2,1)}, bf16[64,4096]{1,0:T(8,128)(2,1)}, bf16[64,4096]{1,0:T(8,128)(2,1)}) custom-call(s32[2]{0:T(128)} %pad_add_fusion.meta, s32[64]{0:T(128)} %prompts.9, s32[32]{0:T(128)} %slots.9, bf16[64,2048]{1,0:T(8,128)(2,1)} %copy-done.7, bf16[64,2048]{1,0:T(8,128)(2,1)} %copy-done.11, ...), custom_call_target="tpu_custom_call" | custom-call | tf_op jit(solution)/shard_map/serve/pallas_call | solution.py:597
  165.1 1.6 collective-permute-start.27
  166.7 1.6 collective-permute-start.26
  168.3 0.8 collective-permute-start.25
  169.0 8.2 %collective-permute-done.27 = bf16[64,4096]{1,0:T(8,128)(2,1)S(1)} collective-permute-done((bf16[64,4096]{1,0:T(8,128)(2,1)}, bf16[64,4096]{1,0:T(8,128)(2,1)S(1)}, u32[]{:S(2)}, u32[]{:S(2)}) %collective-permute-start.27) | collective-permute-done | bytes 524320 | tf_op jit(solution)/shard_map/ppermute | solution.py:786
  177.2 5.8 %collective-permute-done.26 = bf16[64,4096]{1,0:T(8,128)(2,1)S(1)} collective-permute-done((bf16[64,4096]{1,0:T(8,128)(2,1)}, bf16[64,4096]{1,0:T(8,128)(2,1)S(1)}, u32[]{:S(2)}, u32[]{:S(2)}) %collective-permute-start.26) | collective-permute-done | bytes 524320 | tf_op jit(solution)/shard_map/ppermute | solution.py:786
  183.0 2.2 %fusion = bf16[64,4096]{1,0:T(8,128)(2,1)} fusion(f32[64,2048]{1,0:T(8,128)S(1)} %get-tuple-element.74, f32[64,2048]{1,0:T(8,128)S(1)} %get-tuple-element.67, bf16[64,4096]{1,0:T(8,128)(2,1)S(1)} %collective-permute-done.27, bf16[64,4096]{1,0:T(8,128)(2,1)S(1)} %collective-permute-done.26, bf16[64,4096]{1,0:T(8,128)(2,1)S(1)} %collective-permute-done.25, ...), kind=kLoop, calls=%fused_computation.3 | loop fusion | flops 2621440 | bytes 3670016 | tf_op jit(solution)/shard_map/convert_element_type | solution.py:788
  (65 shorter events, 0.6 us)
Async XLA Ops:
  8.0 27.0 %all-to-all-start = ((bf16[16,3,2,1024]{3,2,1,0:T(2,128)(2,1)}), bf16[16,3,2,1024]{3,2,1,0:T(2,128)(2,1)S(1)}, u32[]{:S(2)}, u32[]{:S(2)}) async-start(bf16[16,3,2,1024]{3,2,1,0:T(2,128)(2,1)} %broadcast_in_dim.4), calls=%async_computation | async-start | bytes 393216 | tf_op jit(solution)/shard_map/all_to_all | solution.py:679
  15.2 124.5 %all-gather.5.cloned.1.call-start = ((), (), s32[]{:S(2)}) async-start(), calls=%async_computation.4 | async-start | bytes 4718592 | tf_op jit(solution)/shard_map/all_gather | solution.py:705
  16.1 7.3 %collective-permute-start = (bf16[2,16,1024]{2,1,0:T(8,128)(2,1)S(1)}, bf16[2,16,1024]{2,1,0:T(8,128)(2,1)S(1)}, u32[]{:S(2)}, u32[]{:S(2)}) collective-permute-start(bf16[2,16,1024]{2,1,0:T(8,128)(2,1)S(1)} %convert_element_type.81), channel_id=1, source_target_pairs={{0,64},{8,72},{16,80},{24,88},{32,96},{40,104},{48,112},{56,120},{... | collective-permute-start | bytes 196616 | tf_op jit(solution)/shard_map/ppermute | solution.py:681
  23.5 16.3 %collective-permute-start.1 = (bf16[4,16,1024]{2,1,0:T(8,128)(2,1)S(1)}, bf16[4,16,1024]{2,1,0:T(8,128)(2,1)S(1)}, u32[]{:S(2)}, u32[]{:S(2)}) collective-permute-start(bf16[4,16,1024]{2,1,0:T(8,128)(2,1)S(1)} %get-tuple-element.77), channel_id=1, source_target_pairs={{0,48},{8,56},{16,0},{24,8},{32,16},{40,24},{48,32},{56,40},{64,11... | collective-permute-start | bytes 393224 | tf_op jit(solution)/shard_map/ppermute | solution.py:683
  26.1 13.7 %collective-permute-start.2 = (bf16[4,16,1024]{2,1,0:T(8,128)(2,1)S(1)}, bf16[4,16,1024]{2,1,0:T(8,128)(2,1)S(1)}, u32[]{:S(2)}, u32[]{:S(2)}) collective-permute-start(bf16[4,16,1024]{2,1,0:T(8,128)(2,1)S(1)} %get-tuple-element.77), channel_id=1, source_target_pairs={{0,32},{8,40},{16,48},{24,56},{32,0},{40,8},{48,16},{56,24},{64,96... | collective-permute-start | bytes 393224 | tf_op jit(solution)/shard_map/ppermute | solution.py:683
  27.1 12.7 %collective-permute-start.3 = (bf16[4,16,1024]{2,1,0:T(8,128)(2,1)S(1)}, bf16[4,16,1024]{2,1,0:T(8,128)(2,1)S(1)}, u32[]{:S(2)}, u32[]{:S(2)}) collective-permute-start(bf16[4,16,1024]{2,1,0:T(8,128)(2,1)S(1)} %get-tuple-element.77), channel_id=1, source_target_pairs={{0,16},{8,24},{16,32},{24,40},{32,48},{40,56},{48,0},{56,8},{64,80... | collective-permute-start | bytes 393224 | tf_op jit(solution)/shard_map/ppermute | solution.py:683
  27.8 12.0 %collective-permute-start.23 = (bf16[2,512,128]{2,1,0:T(8,128)(2,1)S(1)}, bf16[2,512,128]{2,1,0:T(8,128)(2,1)S(1)}, u32[]{:S(2)}, u32[]{:S(2)}) collective-permute-start(bf16[2,512,128]{2,1,0:T(8,128)(2,1)S(1)} %pad_maximum_fusion.2), channel_id=1, source_target_pairs={{0,64},{8,72},{16,80},{24,88},{32,96},{40,104},{48,112},{56,120},{... | collective-permute-start | bytes 786440 | tf_op jit(solution)/shard_map/ppermute | solution.py:687
  35.0 0.7 copy-start.9
  43.0 13.2 %all-to-all-start.1 = ((bf16[8,64,288]{2,1,0:T(8,128)(2,1)}), bf16[8,64,288]{2,1,0:T(8,128)(2,1)S(1)}, u32[]{:S(2)}, u32[]{:S(2)}) async-start(bf16[8,64,288]{2,1,0:T(8,128)(2,1)} %bitcast.5), calls=%async_computation.1 | async-start | bytes 786432 | tf_op jit(solution)/shard_map/all_to_all | solution.py:701
  48.4 21.5 %copy-start = (bf16[256,1024]{1,0:T(8,128)(2,1)S(1)}, bf16[256,1024]{1,0:T(8,128)(2,1)}, u32[]{:S(2)}) copy-start(bf16[256,1024]{1,0:T(8,128)(2,1)} %weight_ref.3) | copy-start | bytes 1572868
  48.4 21.5 %copy-start.1 = (f32[16,1024]{1,0:T(8,128)S(1)}, f32[16,1024]{1,0:T(8,128)}, u32[]{:S(2)}) copy-start(f32[16,1024]{1,0:T(8,128)} %decay_ref.3) | copy-start | bytes 196612
  48.4 21.5 %copy-start.2 = (f32[1024]{0:T(1024)S(1)}, f32[1024]{0:T(1024)}, u32[]{:S(2)}) copy-start(f32[1024]{0:T(1024)} %param.28) | copy-start | bytes 12292
  48.4 21.5 %copy-start.3 = (f32[1024]{0:T(1024)S(1)}, f32[1024]{0:T(1024)}, u32[]{:S(2)}) copy-start(f32[1024]{0:T(1024)} %param.30) | copy-start | bytes 12292
  48.5 21.5 %copy-start.4 = (s32[64]{0:T(128)S(1)}, s32[64]{0:T(128)}, u32[]{:S(2)}) copy-start(s32[64]{0:T(128)} %prompts.9) | copy-start | bytes 772
  48.5 21.5 %copy-start.5 = (s32[32]{0:T(128)S(1)}, s32[32]{0:T(128)}, u32[]{:S(2)}) copy-start(s32[32]{0:T(128)} %slots.9) | copy-start | bytes 388
  48.5 21.5 %copy-start.6 = (s32[2]{0:T(128)S(1)}, s32[2]{0:T(128)}, u32[]{:S(2)}) copy-start(s32[2]{0:T(128)} %pad_add_fusion.meta) | copy-start | bytes 28
  48.5 102.5 %all-gather.3.cloned.1.call-start = ((), (), s32[]{:S(2)}) async-start(), calls=%async_computation.3 | async-start | bytes 11796480 | tf_op jit(solution)/shard_map/all_gather | solution.py:762
  56.2 28.7 %collective-permute-start.22 = (bf16[512,1280]{1,0:T(8,128)(2,1)}, bf16[512,1280]{1,0:T(8,128)(2,1)}, u32[]{:S(2)}, u32[]{:S(2)}) collective-permute-start(bf16[512,1280]{1,0:T(8,128)(2,1)} %pad_maximum_fusion), channel_id=1, source_target_pairs={{0,68},{1,69},{2,70},{3,71},{4,64},{5,65},{6,66},{7,67},{8,76},{9,... | collective-permute-start | bytes 3932168 | tf_op jit(solution)/shard_map/ppermute | solution.py:722
  57.8 12.1 %collective-permute-start.4 = (bf16[16,16,1024]{2,1,0:T(8,128)(2,1)S(1)}, bf16[16,16,1024]{2,1,0:T(8,128)(2,1)S(1)}, u32[]{:S(2)}, u32[]{:S(2)}) collective-permute-start(bf16[16,16,1024]{2,1,0:T(8,128)(2,1)S(1)} %constant_dynamic-update-slice_fusion.2.here_ref), channel_id=1, source_target_pairs={{0,8},{8,0},{16,24},{24,16},{32,40},{40,32},{48,56},{56,48},{64,72... | collective-permute-start | bytes 1572872 | tf_op jit(solution)/shard_map/ppermute | solution.py:700
  85.0 21.6 %collective-permute-start.5 = (bf16[4,64,2048]{2,1,0:T(8,128)(2,1)}, bf16[4,64,2048]{2,1,0:T(8,128)(2,1)S(1)}, u32[]{:S(2)}, u32[]{:S(2)}) collective-permute-start(bf16[4,64,2048]{2,1,0:T(8,128)(2,1)} %get-tuple-element.41), channel_id=1, source_target_pairs={{0,4},{1,5},{2,6},{3,7},{4,0},{5,1},{6,2},{7,3},{8,12},{9,13},{10,... | collective-permute-start | bytes 3145736 | tf_op jit(solution)/shard_map/ppermute | solution.py:629
  85.2 16.5 %collective-permute-start.14 = (bf16[64,2048]{1,0:T(8,128)(2,1)S(1)}, bf16[64,2048]{1,0:T(8,128)(2,1)S(1)}, u32[]{:S(2)}, u32[]{:S(2)}) collective-permute-start(bf16[64,2048]{1,0:T(8,128)(2,1)S(1)} %get-tuple-element.44), channel_id=1, source_target_pairs={{0,2},{1,3},{2,0},{3,1},{4,6},{5,7},{6,4},{7,5},{8,10},{9,11},{10,... | collective-permute-start | bytes 786440 | tf_op jit(solution)/shard_map/ppermute | solution.py:628
  86.7 17.7 %collective-permute-start.13 = (bf16[64,2048]{1,0:T(8,128)(2,1)S(1)}, bf16[64,2048]{1,0:T(8,128)(2,1)S(1)}, u32[]{:S(2)}, u32[]{:S(2)}) collective-permute-start(bf16[64,2048]{1,0:T(8,128)(2,1)S(1)} %get-tuple-element.45), channel_id=1, source_target_pairs={{0,3},{1,0},{2,1},{3,2},{4,7},{5,4},{6,5},{7,6},{8,11},{9,8},{10,9... | collective-permute-start | bytes 786440 | tf_op jit(solution)/shard_map/ppermute | solution.py:628
  88.8 17.1 %collective-permute-start.12 = (bf16[64,2048]{1,0:T(8,128)(2,1)S(1)}, bf16[64,2048]{1,0:T(8,128)(2,1)S(1)}, u32[]{:S(2)}, u32[]{:S(2)}) collective-permute-start(bf16[64,2048]{1,0:T(8,128)(2,1)S(1)} %get-tuple-element.43), channel_id=1, source_target_pairs={{0,1},{1,2},{2,3},{3,0},{4,5},{5,6},{6,7},{7,4},{8,9},{9,10},{10,1... | collective-permute-start | bytes 786440 | tf_op jit(solution)/shard_map/ppermute | solution.py:628
  101.0 10.5 %collective-permute-start.6 = (bf16[64,2048]{1,0:T(8,128)(2,1)S(1)}, bf16[64,2048]{1,0:T(8,128)(2,1)S(1)}, u32[]{:S(2)}, u32[]{:S(2)}) collective-permute-start(bf16[64,2048]{1,0:T(8,128)(2,1)S(1)} %get-tuple-element.48), channel_id=1, source_target_pairs={{0,1},{1,2},{2,3},{3,0},{4,5},{5,6},{6,7},{7,4},{8,9},{9,10},{10,1... | collective-permute-start | bytes 786440 | tf_op jit(solution)/shard_map/ppermute | solution.py:634
  101.7 14.3 %collective-permute-start.7 = (bf16[64,2048]{1,0:T(8,128)(2,1)S(1)}, bf16[64,2048]{1,0:T(8,128)(2,1)S(1)}, u32[]{:S(2)}, u32[]{:S(2)}) collective-permute-start(bf16[64,2048]{1,0:T(8,128)(2,1)S(1)} %get-tuple-element.49), channel_id=1, source_target_pairs={{0,3},{1,0},{2,1},{3,2},{4,7},{5,4},{6,5},{7,6},{8,11},{9,8},{10,9... | collective-permute-start | bytes 786440 | tf_op jit(solution)/shard_map/ppermute | solution.py:634
  104.4 11.5 %collective-permute-start.8 = (bf16[64,2048]{1,0:T(8,128)(2,1)S(1)}, bf16[64,2048]{1,0:T(8,128)(2,1)S(1)}, u32[]{:S(2)}, u32[]{:S(2)}) collective-permute-start(bf16[64,2048]{1,0:T(8,128)(2,1)S(1)} %get-tuple-element.50), channel_id=1, source_target_pairs={{0,2},{1,3},{2,0},{3,1},{4,6},{5,7},{6,4},{7,5},{8,10},{9,11},{10,... | collective-permute-start | bytes 786440 | tf_op jit(solution)/shard_map/ppermute | solution.py:634
  106.6 25.9 %copy-start.10 = (bf16[64,4096]{1,0:T(8,128)(2,1)S(1)}, bf16[64,4096]{1,0:T(8,128)(2,1)}, u32[]{:S(2)}) copy-start(bf16[64,4096]{1,0:T(8,128)(2,1)} %param.21) | copy-start | bytes 1572868
  116.1 8.0 %collective-permute-start.11 = (bf16[64,2048]{1,0:T(8,128)(2,1)S(1)}, bf16[64,2048]{1,0:T(8,128)(2,1)S(1)}, u32[]{:S(2)}, u32[]{:S(2)}) collective-permute-start(bf16[64,2048]{1,0:T(8,128)(2,1)S(1)} %get-tuple-element.71), channel_id=1, source_target_pairs={{0,2},{1,3},{2,0},{3,1},{4,6},{5,7},{6,4},{7,5},{8,10},{9,11},{10,... | collective-permute-start | bytes 786440 | tf_op jit(solution)/shard_map/ppermute | solution.py:639
  116.2 16.3 %collective-permute-start.10 = (bf16[64,2048]{1,0:T(8,128)(2,1)S(1)}, bf16[64,2048]{1,0:T(8,128)(2,1)S(1)}, u32[]{:S(2)}, u32[]{:S(2)}) collective-permute-start(bf16[64,2048]{1,0:T(8,128)(2,1)S(1)} %get-tuple-element.72), channel_id=1, source_target_pairs={{0,3},{1,0},{2,1},{3,2},{4,7},{5,4},{6,5},{7,6},{8,11},{9,8},{10,9... | collective-permute-start | bytes 786440 | tf_op jit(solution)/shard_map/ppermute | solution.py:639
  119.9 12.6 %collective-permute-start.9 = (bf16[64,2048]{1,0:T(8,128)(2,1)S(1)}, bf16[64,2048]{1,0:T(8,128)(2,1)S(1)}, u32[]{:S(2)}, u32[]{:S(2)}) collective-permute-start(bf16[64,2048]{1,0:T(8,128)(2,1)S(1)} %get-tuple-element.70), channel_id=1, source_target_pairs={{0,1},{1,2},{2,3},{3,0},{4,5},{5,6},{6,7},{7,4},{8,9},{9,10},{10,1... | collective-permute-start | bytes 786440 | tf_op jit(solution)/shard_map/ppermute | solution.py:639
  120.7 11.8 %collective-permute-start.15 = (bf16[64,2048]{1,0:T(8,128)(2,1)S(1)}, bf16[64,2048]{1,0:T(8,128)(2,1)S(1)}, u32[]{:S(2)}, u32[]{:S(2)}) collective-permute-start(bf16[64,2048]{1,0:T(8,128)(2,1)S(1)} %add_convert_fusion), channel_id=1, source_target_pairs={{0,4},{1,5},{2,6},{3,7},{4,0},{5,1},{6,2},{7,3},{8,12},{9,13},{10,... | collective-permute-start | bytes 786440 | tf_op jit(solution)/shard_map/ppermute | solution.py:636
  133.0 18.1 %copy-start.7 = (bf16[64,2048]{1,0:T(8,128)(2,1)}, bf16[64,2048]{1,0:T(8,128)(2,1)S(1)}, u32[]{:S(2)}) copy-start(bf16[64,2048]{1,0:T(8,128)(2,1)S(1)} %get-tuple-element.66.refs_0_) | copy-start | bytes 786436
  133.0 18.1 %copy-start.8 = (bf16[64,2048]{1,0:T(8,128)(2,1)}, bf16[64,2048]{1,0:T(8,128)(2,1)S(1)}, u32[]{:S(2)}) copy-start(bf16[64,2048]{1,0:T(8,128)(2,1)S(1)} %get-tuple-element.73.refs_4_) | copy-start | bytes 786436
  133.0 9.1 %collective-permute-start.16 = (bf16[64,2048]{1,0:T(8,128)(2,1)S(1)}, bf16[64,2048]{1,0:T(8,128)(2,1)S(1)}, u32[]{:S(2)}, u32[]{:S(2)}) collective-permute-start(bf16[64,2048]{1,0:T(8,128)(2,1)S(1)} %get-tuple-element.66.refs_0_), channel_id=1, source_target_pairs={{0,3},{1,0},{2,1},{3,2},{4,7},{5,4},{6,5},{7,6},{8,11},{9,8},{10,9... | collective-permute-start | bytes 786440 | tf_op jit(solution)/shard_map/ppermute | solution.py:648
  134.1 8.9 %collective-permute-start.17 = (bf16[64,2048]{1,0:T(8,128)(2,1)S(1)}, bf16[64,2048]{1,0:T(8,128)(2,1)S(1)}, u32[]{:S(2)}, u32[]{:S(2)}) collective-permute-start(bf16[64,2048]{1,0:T(8,128)(2,1)S(1)} %get-tuple-element.66.refs_0_), channel_id=1, source_target_pairs={{0,2},{1,3},{2,0},{3,1},{4,6},{5,7},{6,4},{7,5},{8,10},{9,11},{10,... | collective-permute-start | bytes 786440 | tf_op jit(solution)/shard_map/ppermute | solution.py:648
  134.7 10.3 %collective-permute-start.18 = (bf16[64,2048]{1,0:T(8,128)(2,1)S(1)}, bf16[64,2048]{1,0:T(8,128)(2,1)S(1)}, u32[]{:S(2)}, u32[]{:S(2)}) collective-permute-start(bf16[64,2048]{1,0:T(8,128)(2,1)S(1)} %get-tuple-element.66.refs_0_), channel_id=1, source_target_pairs={{0,1},{1,2},{2,3},{3,0},{4,5},{5,6},{6,7},{7,4},{8,9},{9,10},{10,1... | collective-permute-start | bytes 786440 | tf_op jit(solution)/shard_map/ppermute | solution.py:648
  135.1 12.5 %collective-permute-start.19 = (bf16[64,2048]{1,0:T(8,128)(2,1)S(1)}, bf16[64,2048]{1,0:T(8,128)(2,1)S(1)}, u32[]{:S(2)}, u32[]{:S(2)}) collective-permute-start(bf16[64,2048]{1,0:T(8,128)(2,1)S(1)} %get-tuple-element.73.refs_4_), channel_id=1, source_target_pairs={{0,3},{1,0},{2,1},{3,2},{4,7},{5,4},{6,5},{7,6},{8,11},{9,8},{10,9... | collective-permute-start | bytes 786440 | tf_op jit(solution)/shard_map/ppermute | solution.py:648
  137.9 10.4 %collective-permute-start.20 = (bf16[64,2048]{1,0:T(8,128)(2,1)S(1)}, bf16[64,2048]{1,0:T(8,128)(2,1)S(1)}, u32[]{:S(2)}, u32[]{:S(2)}) collective-permute-start(bf16[64,2048]{1,0:T(8,128)(2,1)S(1)} %get-tuple-element.73.refs_4_), channel_id=1, source_target_pairs={{0,2},{1,3},{2,0},{3,1},{4,6},{5,7},{6,4},{7,5},{8,10},{9,11},{10,... | collective-permute-start | bytes 786440 | tf_op jit(solution)/shard_map/ppermute | solution.py:648
  142.1 9.0 %copy-start.11 = (bf16[64,2048]{1,0:T(8,128)(2,1)}, bf16[64,2048]{1,0:T(8,128)(2,1)S(1)}, u32[]{:S(2)}) copy-start(bf16[64,2048]{1,0:T(8,128)(2,1)S(1)} %collective-permute-done.16.refs_1_) | copy-start | bytes 786436
  142.1 8.9 %collective-permute-start.21 = (bf16[64,2048]{1,0:T(8,128)(2,1)S(1)}, bf16[64,2048]{1,0:T(8,128)(2,1)S(1)}, u32[]{:S(2)}, u32[]{:S(2)}) collective-permute-start(bf16[64,2048]{1,0:T(8,128)(2,1)S(1)} %get-tuple-element.73.refs_4_), channel_id=1, source_target_pairs={{0,1},{1,2},{2,3},{3,0},{4,5},{5,6},{6,7},{7,4},{8,9},{9,10},{10,1... | collective-permute-start | bytes 786440 | tf_op jit(solution)/shard_map/ppermute | solution.py:648
  143.0 8.0 %copy-start.12 = (bf16[64,2048]{1,0:T(8,128)(2,1)}, bf16[64,2048]{1,0:T(8,128)(2,1)S(1)}, u32[]{:S(2)}) copy-start(bf16[64,2048]{1,0:T(8,128)(2,1)S(1)} %collective-permute-done.17.refs_2_) | copy-start | bytes 786436
  143.0 8.0 %collective-permute-start.24 = (bf16[2,512,128]{2,1,0:T(8,128)(2,1)}, bf16[2,512,128]{2,1,0:T(8,128)(2,1)S(1)}, u32[]{:S(2)}, u32[]{:S(2)}) collective-permute-start(bf16[2,512,128]{2,1,0:T(8,128)(2,1)} %pick_far.1), channel_id=1, source_target_pairs={{0,4},{1,5},{2,6},{3,7},{4,0},{5,1},{6,2},{7,3},{8,12},{9,13},{10,... | collective-permute-start | bytes 786440 | tf_op jit(solution)/shard_map/ppermute | solution.py:771
  145.0 6.1 %copy-start.13 = (bf16[64,2048]{1,0:T(8,128)(2,1)}, bf16[64,2048]{1,0:T(8,128)(2,1)S(1)}, u32[]{:S(2)}) copy-start(bf16[64,2048]{1,0:T(8,128)(2,1)S(1)} %collective-permute-done.18.refs_3_) | copy-start | bytes 786436
  147.6 3.5 %copy-start.14 = (bf16[64,2048]{1,0:T(8,128)(2,1)}, bf16[64,2048]{1,0:T(8,128)(2,1)S(1)}, u32[]{:S(2)}) copy-start(bf16[64,2048]{1,0:T(8,128)(2,1)S(1)} %collective-permute-done.19.refs_5_) | copy-start | bytes 786436
  148.3 2.8 %copy-start.15 = (bf16[64,2048]{1,0:T(8,128)(2,1)}, bf16[64,2048]{1,0:T(8,128)(2,1)S(1)}, u32[]{:S(2)}) copy-start(bf16[64,2048]{1,0:T(8,128)(2,1)S(1)} %collective-permute-done.20.refs_6_) | copy-start | bytes 786436
  151.0 0.7 copy-start.16
  151.0 0.8 copy-start.17
  165.1 12.1 %collective-permute-start.27 = (bf16[64,4096]{1,0:T(8,128)(2,1)}, bf16[64,4096]{1,0:T(8,128)(2,1)S(1)}, u32[]{:S(2)}, u32[]{:S(2)}) collective-permute-start(bf16[64,4096]{1,0:T(8,128)(2,1)} %get-tuple-element.62), channel_id=1, source_target_pairs={{0,2},{1,3},{2,0},{3,1},{4,6},{5,7},{6,4},{7,5},{8,10},{9,11},{10,... | collective-permute-start | bytes 1572872 | tf_op jit(solution)/shard_map/ppermute | solution.py:786
  166.7 16.4 %collective-permute-start.26 = (bf16[64,4096]{1,0:T(8,128)(2,1)}, bf16[64,4096]{1,0:T(8,128)(2,1)S(1)}, u32[]{:S(2)}, u32[]{:S(2)}) collective-permute-start(bf16[64,4096]{1,0:T(8,128)(2,1)} %get-tuple-element.61), channel_id=1, source_target_pairs={{0,3},{1,0},{2,1},{3,2},{4,7},{5,4},{6,5},{7,6},{8,11},{9,8},{10,9... | collective-permute-start | bytes 1572872 | tf_op jit(solution)/shard_map/ppermute | solution.py:786
  168.3 14.8 %collective-permute-start.25 = (bf16[64,4096]{1,0:T(8,128)(2,1)}, bf16[64,4096]{1,0:T(8,128)(2,1)S(1)}, u32[]{:S(2)}, u32[]{:S(2)}) collective-permute-start(bf16[64,4096]{1,0:T(8,128)(2,1)} %get-tuple-element.60), channel_id=1, source_target_pairs={{0,1},{1,2},{2,3},{3,0},{4,5},{5,6},{6,7},{7,4},{8,9},{9,10},{10,1... | collective-permute-start | bytes 1572872 | tf_op jit(solution)/shard_map/ppermute | solution.py:786
Sparse Core Ops, SparseCore 0:
  40.8 32.1 all-gather.4
  85.1 57.0 all-gather.2
